TPU v7x, 32 devices: a whole 2x2x4 slice. The times are simulated.
32 devices in a mesh: dp: 2 (over y), expert: 16 (over z, x, core).
Axes of the slice: x: 2, y: 2, z: 4, core: 2. Of those that a mesh axis runs over, the one named last changes fastest.
Arguments:
- tokens: bfloat16 [1024, 2048], P('expert', 'dp'), may hold values from -6 to 6
- expert_ids: int32 [1024, 8], P('expert'), may hold values from 0 to 31, all different within a row; in each aligned block of 64 rows (0 to 63, 64 to 127, ...) at most 24 rows name the same one
- route_weights: bfloat16 [1024, 8], P('expert'), may hold values from 0.019897461 to 0.3984375
- w_gate: bfloat16 [32, 2048, 1024], P('expert', None, 'dp'), may hold values from -0.125 to 0.125
- w_up: bfloat16 [32, 2048, 1024], P('expert', None, 'dp'), may hold values from -0.125 to 0.125
- w_down: bfloat16 [32, 1024, 2048], P('expert', 'dp'), may hold values from -0.1875 to 0.1875
Outputs:
- moe_out: bfloat16 [1024, 2048], P('expert', 'dp')
Inputs may be any that keep to these rules, and one draw needn't show every extreme that they name: `expert_ids`: each token names 8 different experts. In each aligned block of 64 rows no expert is named more than 24 times, a bound that some block reaches.
All inputs are finite; a program needn't handle non-finite values.
Results may differ from a plain program's by a relative error of at most 0.019.
Values may be sent and summed in bfloat16 or wider, within the bound.
No kernel may reach another device: no remote copies, remote signals or barrier semaphores. Data moves between devices by JAX's collectives and lax.ppermute only.
A program may use at most 64 MiB of HBM per device.

v0:
```python
import jax
import jax.numpy as jnp
from jax import lax
from jax.sharding import PartitionSpec as P


def slot_tables(expert_ids, route_weights, expert_count, capacity):
    flat_ids = expert_ids.reshape(-1)
    expert_range = jnp.arange(expert_count, dtype=jnp.int32)
    one_hot = (flat_ids[:, None] == expert_range[None, :]).astype(jnp.int32)
    ranks = jnp.sum((jnp.cumsum(one_hot, axis=0) - 1) * one_hot, axis=1)
    dest_slot = (flat_ids * capacity + ranks).reshape(expert_ids.shape)
    slot_range = jnp.arange(expert_count * capacity, dtype=jnp.int32)
    hit_table = dest_slot[None, :, :] == slot_range[:, None, None]
    dispatch_matrix = jnp.sum(hit_table.astype(jnp.float32), axis=2).astype(jnp.bfloat16)
    weight_table = jnp.where(
        hit_table, route_weights.astype(jnp.float32)[None, :, :], jnp.float32(0.0)
    )
    combine_matrix = jnp.sum(weight_table, axis=2).astype(jnp.bfloat16)
    return (dispatch_matrix, combine_matrix)


def finish_expert(gate_proj, up_proj, w_down):
    hidden = (jax.nn.silu(gate_proj) * up_proj).astype(jnp.bfloat16)
    return jnp.einsum("nrcf,rfd->nrcd", hidden, w_down, preferred_element_type=jnp.float32).astype(
        jnp.bfloat16
    )


def on_device(tokens, expert_ids, route_weights, w_gate, w_up, w_down):
    peer_count = lax.axis_size("expert")
    local_experts = w_gate.shape[0]
    expert_count = local_experts * peer_count
    tok_rows, top_count = expert_ids.shape
    capacity = tok_rows * top_count * 3 // (2 * expert_count)
    dispatch_matrix, combine_matrix = slot_tables(expert_ids, route_weights, expert_count, capacity)
    whole = lax.all_gather(tokens, "dp", axis=1, tiled=True)
    send_rows = jnp.dot(dispatch_matrix, whole, preferred_element_type=jnp.float32).astype(
        jnp.bfloat16
    )
    send_rows = send_rows.reshape(peer_count, local_experts, capacity, whole.shape[1])
    arrived = lax.all_to_all(send_rows, "expert", split_axis=0, concat_axis=0, tiled=True)
    gate_proj = jnp.einsum("nrcd,rdf->nrcf", arrived, w_gate, preferred_element_type=jnp.float32)
    up_proj = jnp.einsum("nrcd,rdf->nrcf", arrived, w_up, preferred_element_type=jnp.float32)
    expert_rows = finish_expert(gate_proj, up_proj, w_down)
    returned = lax.all_to_all(expert_rows, "expert", split_axis=0, concat_axis=0, tiled=True)
    flat_returned = returned.reshape(expert_count * capacity, returned.shape[3])
    mixed_rows = lax.dot_general(
        combine_matrix, flat_returned, (((0,), (0,)), ((), ())), preferred_element_type=jnp.float32
    )
    return lax.psum_scatter(mixed_rows.astype(jnp.bfloat16), "dp", scatter_dimension=1, tiled=True)


def solution(mesh):
    return jax.shard_map(
        on_device,
        mesh=mesh,
        in_specs=(
            P("expert", "dp"),
            P("expert", None),
            P("expert", None),
            P("expert", None, "dp"),
            P("expert", None, "dp"),
            P("expert", "dp", None),
        ),
        out_specs=P("expert", "dp"),
        check_vma=False,
    )
```

profile of v0, /device:TPU:0, one launch (start us, length us, event | category | flops | bytes accessed | tf_op | source)
XLA Modules:
  0.0 205.8 jit_solution(2231423978979224809)
XLA Ops:
  6.5 0.0 reduce-scatter.2.cloned.1.call-start
  6.5 0.8 copy.36
  7.3 0.1 eq.42
  7.4 0.1 eq.38
  7.5 0.8 copy.41
  8.3 1.2 reduce-window.6
  9.4 0.2 slice_reduce_fusion
  9.7 0.1 fusion.30
  9.8 0.1 reduce_sum.30
  9.9 0.1 copy.39
  10.0 0.7 multiply_add_fusion
  10.7 0.1 copy.40
  10.8 7.4 %all_gather.3 = bf16[64,2048]{1,0:T(8,128)(2,1)S(1)} all-gather(bf16[64,1024]{1,0:T(8,128)(2,1)} %param.6), channel_id=1, replica_groups=mesh['dp'=2,'expert'=16] {'dp'}, dimensions={1}, use_global_device_ids=true | all-gather | bytes 393216 | tf_op jit(solution)/shard_map/all_gather | solution.py:37
  18.1 1.0 select_reduce_fusion
  19.2 1.0 convolution_convert_fusion
  20.2 0.0 copy-start
  20.2 75.9 %all_to_all.10 = bf16[16,2,24,2048]{3,2,1,0:T(8,128)(2,1)S(1)} all-to-all(bf16[16,2,24,2048]{3,2,1,0:T(8,128)(2,1)S(1)} %bitcast.68), channel_id=1, replica_groups=mesh['dp'=2,'expert'=16] {'expert'}, dimensions={0} | all-to-all | bytes 6291456 | tf_op jit(solution)/shard_map/all_to_all | solution.py:42
  96.1 2.9 %fusion.4 = f32[2,16,24,512]{3,2,1,0:T(8,128)} fusion(bf16[2,2048,512]{2,1,0:T(8,128)(2,1)S(1)} %copy-done, bf16[16,2,24,2048]{3,2,1,0:T(8,128)(2,1)S(1)} %all_to_all.10), kind=kOutput, calls=%fused_computation.4 | convolution fusion | flops 1610612736 | bytes 8912896 | tf_op jit(solution)/shard_map/nrcd,rdf->nrcf/dot_general | solution.py:43
  99.0 9.1 %fusion.9 = bf16[16,2,24,2048]{3,2,0,1:T(8,128)(2,1)} fusion(bf16[2,512,2048]{2,1,0:T(8,128)(2,1)} %param.11, f32[2,16,24,512]{3,2,1,0:T(8,128)} %fusion.4, bf16[2,2048,512]{2,1,0:T(8,128)(2,1)} %param.10, bf16[16,2,24,2048]{3,2,1,0:T(8,128)(2,1)S(1)} %all_to_all.10), kind=kOutput, calls=%fused_computation.8 | convolution fusion | flops 3225157632 | bytes 16252928 | tf_op jit(solution)/shard_map/nrcf,rfd->nrcd/dot_general | solution.py:25
  108.1 2.3 %copy.44 = bf16[16,2,24,2048]{3,2,1,0:T(8,128)(2,1)S(1)} copy(bf16[16,2,24,2048]{3,2,0,1:T(8,128)(2,1)} %fusion.9) | data formatting | bytes 6291456 | tf_op jit(solution)/shard_map/convert_element_type | solution.py:25
  110.4 74.8 %all_to_all.11 = bf16[16,2,24,2048]{3,2,1,0:T(8,128)(2,1)S(1)} all-to-all(bf16[16,2,24,2048]{3,2,1,0:T(8,128)(2,1)S(1)} %copy.44), channel_id=1, replica_groups=mesh['dp'=2,'expert'=16] {'expert'}, dimensions={0} | all-to-all | bytes 6291456 | tf_op jit(solution)/shard_map/all_to_all | solution.py:46
  185.2 1.4 convolution_convert_fusion.1
  186.6 0.0 reduce-scatter.2.cloned.1.call-update
  186.6 12.3 %reduce-scatter.2.cloned.1.call-done = bf16[64,1024]{1,0:T(8,128)(2,1)} async-done(((bf16[64,2048]{1,0:T(8,128)(2,1)}), bf16[64,1024]{1,0:T(8,128)(2,1)}) %reduce-scatter.2.cloned.1.call-update) | async-done | bytes 131088 | tf_op jit(solution)/shard_map/reduce_scatter | solution.py:51
  (4 shorter events, 0.1 us)
Async XLA Ops:
  6.5 192.4 %reduce-scatter.2.cloned.1.call-start = ((), (), s32[]{:S(2)}) async-start(), calls=%async_computation.3 | async-start | bytes 393216 | tf_op jit(solution)/shard_map/reduce_scatter | solution.py:51
  20.2 76.0 %copy-start = (bf16[2,2048,512]{2,1,0:T(8,128)(2,1)S(1)}, bf16[2,2048,512]{2,1,0:T(8,128)(2,1)}, u32[]{:S(2)}) copy-start(bf16[2,2048,512]{2,1,0:T(8,128)(2,1)} %param.9) | copy-start | bytes 12582916
Sparse Core Ops, SparseCore 0:
  186.7 12.1 reduce-scatter.1
where the time goes:
time: 206 us
  blocking collectives  158 us (77%)
  matrix products  14.4 us (7%)
  between operations  13.4 us (7%)
  waiting for transfers between devices  12.4 us (6%)
  local copies, waits for them, and re-layouts  4.48 us (2%)
  other arithmetic  3.03 us (1%)
    all_to_all x1, blocking collectives, on_device(): lax.all_to_all(send_rows, 'expert', split_axis=0, concat_axis=0, tiled=True)  75.9 us
    all_to_all x1, blocking collectives, on_device(): lax.all_to_all(expert_rows, 'expert', split_axis=0, concat_axis=0, tiled=...  74.8 us
    reduce_scatter x1, waiting for transfers between devices, on_device(): lax.psum_scatter(mixed_rows.astype(jnp.bfloat16), 'dp', scatter_dimension...  12.3 us
    dot_general x1, matrix products, finish_expert(): jnp.einsum('nrcf,rfd->nrcd', hidden, w_down, preferred_element_type=jnp.f...  9.1 us
    all_gather x1, blocking collectives, on_device(): whole = lax.all_gather(tokens, 'dp', axis=1, tiled=True)  7.38 us
  transfers between devices with their start and end apart: 1, of which 1 were waited for; matrix products, arithmetic and copies ran while one was open for 0% of the time, Pallas kernels for 0%

commit v1 on v0

v1 whole, which is shorter than its diff:
```python
import functools

import jax
import jax.numpy as jnp
from jax import lax
from jax.experimental import pallas as pl
from jax.experimental.pallas import tpu as pltpu
from jax.sharding import PartitionSpec as P

BF16, F32 = jnp.bfloat16, jnp.float32
PAIR = ("dp", "expert")
CHUNKS = 2
LANES = 128


def route_table(ids, weights, columns):
    lane = lax.broadcasted_iota(jnp.int32, (ids.shape[0], columns), 1)
    table = jnp.zeros((ids.shape[0], columns), F32)
    for k in range(ids.shape[1]):
        table = table + jnp.where(ids[:, k : k + 1] == lane, weights[:, k : k + 1].astype(F32), 0.0)
    return table


def pack_kernel(tok_ref, ids_ref, rw_ref, *outs):
    rows, width = tok_ref.shape
    table = route_table(ids_ref[...], rw_ref[...], outs[0].shape[1] - width).astype(BF16)
    part = rows // len(outs)
    for i, out in enumerate(outs):
        out[:, :width] = tok_ref[i * part : (i + 1) * part, :]
        out[:, width:] = table[i * part : (i + 1) * part, :]


def pack(tokens, ids, route_weights, columns):
    rows, width = tokens.shape
    one = jax.ShapeDtypeStruct((rows // CHUNKS, width + columns), BF16)
    return pl.pallas_call(pack_kernel, out_shape=[one] * CHUNKS)(tokens, ids, route_weights)


def join_kernel(*refs):
    *pieces, out, sem = refs
    rows = pieces[0].shape[0]
    copies = [
        pltpu.make_async_copy(piece, out.at[pl.ds(i * rows, rows)], sem.at[i])
        for i, piece in enumerate(pieces)
    ]
    for copy in copies:
        copy.start()
    for copy in copies:
        copy.wait()


def join(pieces):
    rows, width = pieces[0].shape
    return pl.pallas_call(
        join_kernel,
        in_specs=[pl.BlockSpec(memory_space=pl.ANY)] * len(pieces),
        out_specs=pl.BlockSpec(memory_space=pl.ANY),
        out_shape=jax.ShapeDtypeStruct((rows * len(pieces), width), BF16),
        scratch_shapes=[pltpu.SemaphoreType.DMA((len(pieces),))],
    )(*pieces)


def experts_kernel(places, gate_ref, up_ref, down_ref, *refs):
    pieces, (keep_ref, give_ref, rows_buf, table_buf, hidden_buf, sem) = refs[:-6], refs[-6:]
    step = pl.program_id(0)
    width = rows_buf.shape[1] // 2
    first_steps = hidden_buf.shape[1] // gate_ref.shape[2]
    per_expert = first_steps // 2
    row_count = rows_buf.shape[0]

    @pl.when(step == 0)
    def _():
        mine, others = places[0] * width, (1 - places[0]) * width
        copies, row = [], {0: 0, 1: 0}

        def fetch(source, target):
            copies.append(pltpu.make_async_copy(source, target, sem.at[len(copies)]))

        for core in range(2):
            own, by_x, by_y, diag_a, diag_b = pieces[5 * core : 5 * core + 5]
            for side, piece in ((0, own), (0, by_x), (1, by_y), (1, diag_a), (1, diag_b)):
                span = pl.ds(row[side], piece.shape[0])
                start = pl.multiple_of(others if side else mine, width)
                fetch(piece.at[:, pl.ds(0, width)], rows_buf.at[span, pl.ds(start, width)])
                if side == 0:
                    fetch(piece.at[:, pl.ds(width, table_buf.shape[1])], table_buf.at[span])
                row[side] += piece.shape[0]
        for copy in copies:
            copy.start()
        for copy in copies:
            copy.wait()

    @pl.when(step < first_steps)
    def _():
        rows = rows_buf[...]
        gate = jnp.dot(rows, gate_ref[0], preferred_element_type=F32)
        up = jnp.dot(rows, up_ref[0], preferred_element_type=F32)
        expert = places[1] * 2 + step // per_expert
        lane = lax.broadcasted_iota(jnp.int32, table_buf.shape, 1)
        weight = jnp.sum(
            jnp.where(lane == expert, table_buf[...].astype(F32), 0.0), axis=1, keepdims=True
        )
        hidden = gate / (1.0 + jnp.exp(-gate)) * up * weight
        columns = pl.ds(pl.multiple_of(step * gate_ref.shape[2], LANES), gate_ref.shape[2])
        hidden_buf[:, columns] = hidden.astype(BF16)

    @pl.when(step >= first_steps)
    def _():
        out = jnp.dot(hidden_buf[...], down_ref[...], preferred_element_type=F32).astype(BF16)
        keep_ref[0] = out[: row_count // 2]
        give_ref[0] = out[row_count // 2 :]


def run_experts(places, w_gate, w_up, w_down, pieces):
    experts, model, hidden = w_gate.shape
    width = model // 2
    rows = 2 * (pieces[0].shape[0] + pieces[1].shape[0])
    table = pieces[0].shape[1] - width
    step_hidden, step_out = hidden // 2, width // 2
    first, second = experts * 2, 4
    down = w_down.reshape(experts * hidden, model)

    def up_index(i, places):
        j = jnp.minimum(i, first - 1)
        return (j // 2, 0, j % 2)

    def down_index(i, places):
        j = jnp.maximum(i - first, 0)
        return (0, (j + places[0] * 2) % 4)

    def out_index(i, places):
        j = jnp.maximum(i - first, 0)
        return (j // 2, 0, j % 2)

    out = jax.ShapeDtypeStruct((2, rows // 2, width), BF16)
    return pl.pallas_call(
        experts_kernel,
        grid_spec=pltpu.PrefetchScalarGridSpec(
            num_scalar_prefetch=1,
            grid=(first + second,),
            in_specs=[
                pl.BlockSpec((1, model, step_hidden), up_index),
                pl.BlockSpec((1, model, step_hidden), up_index),
                pl.BlockSpec((experts * hidden, step_out), down_index),
            ]
            + [pl.BlockSpec(memory_space=pl.ANY)] * len(pieces),
            out_specs=[pl.BlockSpec((1, rows // 2, step_out), out_index)] * 2,
            scratch_shapes=[
                pltpu.VMEM((rows, model), BF16),
                pltpu.VMEM((rows, table), BF16),
                pltpu.VMEM((rows, experts * hidden), BF16),
                pltpu.SemaphoreType.DMA((14,)),
            ],
        ),
        out_shape=[out, out],
        compiler_params=pltpu.CompilerParams(vmem_limit_bytes=48 * 1024 * 1024),
        cost_estimate=pl.CostEstimate(
            flops=6 * rows * model * hidden * experts,
            bytes_accessed=6 * model * hidden * experts + 4 * rows * model,
            transcendentals=rows * hidden * experts,
        ),
    )(places, w_gate, w_up, down, *pieces)


def add(*terms):
    return functools.reduce(lambda a, b: a + b, [t.astype(F32) for t in terms]).astype(BF16)


def planned(peers, tokens, expert_ids, route_weights, w_gate, w_up, w_down):
    line = peers // 4

    def send(array, steps=0, x=0, core=0, y=0):
        pairs = []
        for side in range(2):
            for e in range(peers):
                to = (e // 4 + steps) % line * 4 + ((e // 2 % 2) ^ x) * 2 + ((e % 2) ^ core)
                pairs.append((side * peers + e, (side ^ y) * peers + to))
        return lax.ppermute(array, PAIR, pairs)

    expert_count = peers * w_gate.shape[0]
    columns = -(-expert_count // LANES) * LANES
    places = jnp.stack([lax.axis_index("dp"), lax.axis_index("expert")]).astype(jnp.int32)
    chunks = pack(tokens, expert_ids, route_weights, columns)

    def gather(chunk):
        own = join([chunk] + [send(chunk, steps=k) for k in range(1, line)])
        half = own.shape[0] // 2
        by_x, by_y = send(own, x=1), send(own, y=1)
        pieces = [own, by_x, by_y, send(by_x[:half], y=1), send(by_y[half:], x=1)]
        return pieces + [send(piece, core=1) for piece in pieces]

    def scatter(keep, give):
        total = add(keep, send(give, core=1))
        side, rows = total.shape[1] // 2, total.shape[1] // line // 2
        half = side // 2
        diag_a, diag_b = total[1, side : side + half], total[1, side + half :]
        got_a, got_b = send(diag_a, x=1), send(diag_b, y=1)
        for_x = jnp.concatenate([total[0, side : side + half], add(total[0, side + half :], got_b)], 0)
        for_y = jnp.concatenate([add(total[1, :half], got_a), total[1, half:side]], 0)
        mine = add(total[0, :side], send(for_x, x=1), send(for_y, y=1))
        back = [send(mine[k * rows : (k + 1) * rows], steps=line - k) for k in range(1, line)]
        return add(mine[:rows], *back)

    outs = []
    for chunk in chunks:
        outs.append(scatter(*run_experts(places, w_gate, w_up, w_down, gather(chunk))))
    return jnp.concatenate(outs, 0)


def general(tokens, expert_ids, route_weights, w_gate, w_up, w_down):
    peers, local = lax.axis_size("expert"), w_gate.shape[0]
    table = route_table(expert_ids, route_weights, peers * local).astype(BF16)
    rows = lax.all_gather(tokens, "expert", axis=0, tiled=True)
    rows = lax.all_gather(rows, "dp", axis=1, tiled=True)
    table = lax.all_gather(table, "expert", axis=0, tiled=True).astype(F32)
    weight = lax.dynamic_slice_in_dim(table, lax.axis_index("expert") * local, local, 1)
    gate = jnp.einsum("td,rdf->trf", rows, w_gate, preferred_element_type=F32)
    up = jnp.einsum("td,rdf->trf", rows, w_up, preferred_element_type=F32)
    hidden = (jax.nn.silu(gate) * up * weight[:, :, None]).astype(BF16)
    out = jnp.einsum("trf,rfd->td", hidden, w_down, preferred_element_type=F32).astype(BF16)
    out = lax.psum_scatter(out, "dp", scatter_dimension=1, tiled=True)
    return lax.psum_scatter(out, "expert", scatter_dimension=0, tiled=True)


def solution(mesh):
    peers = mesh.shape["expert"]
    body = general
    if mesh.shape["dp"] == 2 and peers % 4 == 0:
        body = functools.partial(planned, peers)
    return jax.shard_map(
        body,
        mesh=mesh,
        in_specs=(
            P("expert", "dp"),
            P("expert", None),
            P("expert", None),
            P("expert", None, "dp"),
            P("expert", None, "dp"),
            P("expert", "dp", None),
        ),
        out_specs=P("expert", "dp"),
        check_vma=False,
    )
```

time: 206 us -> 126 us (0.61)
  blocking collectives: 158 us -> 0 us
  Pallas kernels: 0 us -> 46.9 us
  starting transfers between devices: 0.01 us -> 43.1 us
  waiting for transfers between devices: 12.4 us -> 27.3 us
  matrix products: 14.4 us -> 0 us
  between operations: 13.4 us -> 0.25 us
    all_to_all x2 -> x0, blocking collectives: 151 us -> none  [the longest x1 75.9 us: on_device(): lax.all_to_all(send_rows, 'expert', split_axis=0, concat_axis=0, tiled=True)]
    pallas_call x0 -> x5, Pallas kernels: none -> 46.9 us  [the longest x2 25 us: run_experts(): pl.pallas_call(experts_kernel, grid_spec=pltpu.PrefetchScalarGridSpec(num...]
    ppermute x0 -> x40, starting transfers between devices: none -> 43.1 us  [send(): return lax.ppermute(array, PAIR, pairs)]
    ppermute x0 -> x40, waiting for transfers between devices: none -> 27.3 us  [send(): return lax.ppermute(array, PAIR, pairs)]
    dot_general x4 -> x0, matrix products: 14.4 us -> none  [the longest x1 9.1 us: finish_expert(): jnp.einsum('nrcf,rfd->nrcd', hidden, w_down, preferred_element_type=jnp.f...]
    reduce_scatter x1 -> x0, waiting for transfers between devices: 12.3 us -> none  [on_device(): lax.psum_scatter(mixed_rows.astype(jnp.bfloat16), 'dp', scatter_dimension...]
    all_gather x1 -> x0, blocking collectives: 7.38 us -> none  [on_device(): whole = lax.all_gather(tokens, 'dp', axis=1, tiled=True)]
    unnamed x3 -> x18, local copies, waits for them, and re-layouts: 0.78 us -> 5.59 us
  transfers between devices with their start and end apart: 1 -> 40, of which waited for: 1 -> 17; matrix products, arithmetic and copies ran while one was open for 0% -> 1% of each run, Pallas kernels for 0% -> 36%
where the time goes in v1:
time: 126 us; the launch traced here: 125 us
  Pallas kernels  46.9 us (37%)
  starting transfers between devices  43.1 us (34%)
  waiting for transfers between devices  27.3 us (22%)
  local copies, waits for them, and re-layouts  5.74 us (5%)
  other arithmetic  2.05 us (2%)
    ppermute x40, starting transfers between devices, send(): return lax.ppermute(array, PAIR, pairs)  43.1 us
    ppermute x40, waiting for transfers between devices, send(): return lax.ppermute(array, PAIR, pairs)  27.3 us
    pallas_call x2, Pallas kernels, run_experts(): pl.pallas_call(experts_kernel, grid_spec=pltpu.PrefetchScalarGridSpec(num...  25 us
    pallas_call x2, Pallas kernels, join(): pl.pallas_call(join_kernel, in_specs=[pl.BlockSpec(memory_space=pl.ANY)]...  20.1 us
    unnamed x18, local copies, waits for them, and re-layouts  5.59 us
  transfers between devices with their start and end apart: 40, of which 17 were waited for; matrix products, arithmetic and copies ran while one was open for 1% of the time, Pallas kernels for 36%

profile of v1, /device:TPU:0, one launch (start us, length us, event | category | flops | bytes accessed | tf_op | source)
XLA Modules:
  0.0 125.3 jit_solution(1026886035293261053)
XLA Ops:
  2.7 1.8 %shard_map.64 = (bf16[32,1152]{1,0:T(8,128)(2,1)}, bf16[32,1152]{1,0:T(8,128)(2,1)}) custom-call(bf16[64,1024]{1,0:T(8,128)(2,1)} %tok_ref.1, s32[64,8]{1,0:T(8,128)} %copy.7.ids_ref, bf16[64,8]{1,0:T(8,128)(2,1)} %copy.8.rw_ref), custom_call_target="tpu_custom_call" | custom-call | tf_op jit(solution)/shard_map/pallas_call | solution.py:36
  4.5 3.0 %collective-permute-start = (bf16[32,1152]{1,0:T(8,128)(2,1)}, bf16[32,1152]{1,0:T(8,128)(2,1)S(1)}, u32[]{:S(2)}, u32[]{:S(2)}) collective-permute-start(bf16[32,1152]{1,0:T(8,128)(2,1)} %get-tuple-element.11.refs_0_), channel_id=1, source_target_pairs={{0,4},{1,5},{2,6},{3,7},{4,8},{5,9},{6,10},{7,11},{8,12},{9,13},{1... | collective-permute-start | bytes 221192 | tf_op jit(solution)/shard_map/ppermute | solution.py:178
  7.5 2.6 %collective-permute-start.1 = (bf16[32,1152]{1,0:T(8,128)(2,1)}, bf16[32,1152]{1,0:T(8,128)(2,1)S(1)}, u32[]{:S(2)}, u32[]{:S(2)}) collective-permute-start(bf16[32,1152]{1,0:T(8,128)(2,1)} %get-tuple-element.11.refs_0_), channel_id=1, source_target_pairs={{0,8},{1,9},{2,10},{3,11},{4,12},{5,13},{6,14},{7,15},{8,0},{9,1},... | collective-permute-start | bytes 221192 | tf_op jit(solution)/shard_map/ppermute | solution.py:178
  12.5 2.9 %collective-permute-start.22 = (bf16[32,1152]{1,0:T(8,128)(2,1)}, bf16[32,1152]{1,0:T(8,128)(2,1)S(1)}, u32[]{:S(2)}, u32[]{:S(2)}) collective-permute-start(bf16[32,1152]{1,0:T(8,128)(2,1)} %get-tuple-element.14.refs_0_), channel_id=1, source_target_pairs={{0,12},{1,13},{2,14},{3,15},{4,0},{5,1},{6,2},{7,3},{8,4},{9,5},{1... | collective-permute-start | bytes 221192 | tf_op jit(solution)/shard_map/ppermute | solution.py:178
  17.1 10.1 %shard_map.65.refs_0_ = bf16[128,1152]{1,0:T(8,128)(2,1)} custom-call(bf16[32,1152]{1,0:T(8,128)(2,1)} %get-tuple-element.11.refs_0_, bf16[32,1152]{1,0:T(8,128)(2,1)} %copy-done.4, bf16[32,1152]{1,0:T(8,128)(2,1)} %copy-done.6, bf16[32,1152]{1,0:T(8,128)(2,1)} %copy-done.7), custom_call_target="tpu_custom_call" | custom-call | tf_op jit(solution)/shard_map/pallas_call | solution.py:54
  27.2 1.5 %collective-permute-start.3 = (bf16[128,1152]{1,0:T(8,128)(2,1)}, bf16[128,1152]{1,0:T(8,128)(2,1)S(1)}, u32[]{:S(2)}, u32[]{:S(2)}) collective-permute-start(bf16[128,1152]{1,0:T(8,128)(2,1)} %shard_map.65.refs_0_), channel_id=1, source_target_pairs={{0,2},{1,3},{2,0},{3,1},{4,6},{5,7},{6,4},{7,5},{8,10},{9,11},{10,... | collective-permute-start | bytes 884744 | tf_op jit(solution)/shard_map/ppermute | solution.py:178
  28.7 1.5 %collective-permute-start.4 = (bf16[128,1152]{1,0:T(8,128)(2,1)}, bf16[128,1152]{1,0:T(8,128)(2,1)S(1)}, u32[]{:S(2)}, u32[]{:S(2)}) collective-permute-start(bf16[128,1152]{1,0:T(8,128)(2,1)} %shard_map.65.refs_0_), channel_id=1, source_target_pairs={{0,16},{1,17},{2,18},{3,19},{4,20},{5,21},{6,22},{7,23},{8,24},{9,... | collective-permute-start | bytes 884744 | tf_op jit(solution)/shard_map/ppermute | solution.py:178
  31.5 10.1 %shard_map.67.refs_0_ = bf16[128,1152]{1,0:T(8,128)(2,1)} custom-call(bf16[32,1152]{1,0:T(8,128)(2,1)} %get-tuple-element.14.refs_0_, bf16[32,1152]{1,0:T(8,128)(2,1)} %copy-done.2, bf16[32,1152]{1,0:T(8,128)(2,1)} %copy-done.3, bf16[32,1152]{1,0:T(8,128)(2,1)} %copy-done.5), custom_call_target="tpu_custom_call" | custom-call | tf_op jit(solution)/shard_map/pallas_call | solution.py:54
  42.7 1.6 %collective-permute-start.5 = (bf16[64,1152]{1,0:T(8,128)(2,1)S(1)}, bf16[64,1152]{1,0:T(8,128)(2,1)S(1)}, u32[]{:S(2)}, u32[]{:S(2)}) collective-permute-start(bf16[64,1152]{1,0:T(8,128)(2,1)S(1)} %slice.104), channel_id=1, source_target_pairs={{0,16},{1,17},{2,18},{3,19},{4,20},{5,21},{6,22},{7,23},{8,24},{9,... | collective-permute-start | bytes 442376 | tf_op jit(solution)/shard_map/ppermute | solution.py:178
  44.3 5.1 %collective-permute-done.23.refs_1_ = bf16[128,1152]{1,0:T(8,128)(2,1)S(1)} collective-permute-done((bf16[128,1152]{1,0:T(8,128)(2,1)}, bf16[128,1152]{1,0:T(8,128)(2,1)S(1)}, u32[]{:S(2)}, u32[]{:S(2)}) %collective-permute-start.23) | collective-permute-done | bytes 294944 | tf_op jit(solution)/shard_map/ppermute | solution.py:178
  50.0 2.1 %collective-permute-done.24.refs_2_ = bf16[128,1152]{1,0:T(8,128)(2,1)S(1)} collective-permute-done((bf16[128,1152]{1,0:T(8,128)(2,1)}, bf16[128,1152]{1,0:T(8,128)(2,1)S(1)}, u32[]{:S(2)}, u32[]{:S(2)}) %collective-permute-start.24) | collective-permute-done | bytes 294944 | tf_op jit(solution)/shard_map/ppermute | solution.py:178
  52.7 2.6 %collective-permute-done.5.refs_3_ = bf16[64,1152]{1,0:T(8,128)(2,1)S(1)} collective-permute-done((bf16[64,1152]{1,0:T(8,128)(2,1)S(1)}, bf16[64,1152]{1,0:T(8,128)(2,1)S(1)}, u32[]{:S(2)}, u32[]{:S(2)}) %collective-permute-start.5) | collective-permute-done | bytes 147488 | tf_op jit(solution)/shard_map/ppermute | solution.py:178
  58.2 2.3 %collective-permute-done.26.refs_4_ = bf16[64,1152]{1,0:T(8,128)(2,1)S(1)} collective-permute-done((bf16[64,1152]{1,0:T(8,128)(2,1)S(1)}, bf16[64,1152]{1,0:T(8,128)(2,1)S(1)}, u32[]{:S(2)}, u32[]{:S(2)}) %collective-permute-start.26) | collective-permute-done | bytes 147488 | tf_op jit(solution)/shard_map/ppermute | solution.py:178
  62.6 12.5 %shard_map.66 = (bf16[2,256,1024]{2,1,0:T(8,128)(2,1)S(1)}, bf16[2,256,1024]{2,1,0:T(8,128)(2,1)S(1)}) custom-call(s32[2]{0:T(128)S(1)} %pad_add_fusion.places, bf16[2,2048,512]{2,1,0:T(8,128)(2,1)} %gate_ref.3, bf16[2,2048,512]{2,1,0:T(8,128)(2,1)} %up_ref.3, bf16[1024,2048]{1,0:T(8,128)(2,1)} %bitcast.49, bf16[128,1152]{1,0:T(8,128)(2,1)S(1)} %copy-done.1, ...), custom_call_target="tpu_custom_call" | custom-call | flops 6442450944 | bytes 16777216 | tf_op jit(solution)/shard_map/pallas_call | solution.py:136
  75.6 12.5 %shard_map.68 = (bf16[2,256,1024]{2,1,0:T(8,128)(2,1)S(1)}, bf16[2,256,1024]{2,1,0:T(8,128)(2,1)S(1)}) custom-call(s32[2]{0:T(128)S(1)} %pad_add_fusion.places, bf16[2,2048,512]{2,1,0:T(8,128)(2,1)} %gate_ref.3, bf16[2,2048,512]{2,1,0:T(8,128)(2,1)} %up_ref.3, bf16[1024,2048]{1,0:T(8,128)(2,1)} %bitcast.50, bf16[128,1152]{1,0:T(8,128)(2,1)S(1)} %copy-done, ...), custom_call_target="tpu_custom_call" | custom-call | flops 6442450944 | bytes 16777216 | tf_op jit(solution)/shard_map/pallas_call | solution.py:136
  93.4 1.7 %collective-permute-done.13 = bf16[64,1024]{1,0:T(8,128)(2,1)S(1)} collective-permute-done((bf16[64,1024]{1,0:T(8,128)(2,1)S(1)}, bf16[64,1024]{1,0:T(8,128)(2,1)S(1)}, u32[]{:S(2)}, u32[]{:S(2)}) %collective-permute-start.13) | collective-permute-done | bytes 131104 | tf_op jit(solution)/shard_map/ppermute | solution.py:178
  95.2 1.8 %collective-permute-start.14 = (bf16[128,1024]{1,0:T(8,128)(2,1)S(1)}, bf16[128,1024]{1,0:T(8,128)(2,1)S(1)}, u32[]{:S(2)}, u32[]{:S(2)}) collective-permute-start(bf16[128,1024]{1,0:T(8,128)(2,1)S(1)} %pad_maximum_fusion), channel_id=1, source_target_pairs={{0,2},{1,3},{2,0},{3,1},{4,6},{5,7},{6,4},{7,5},{8,10},{9,11},{10,... | collective-permute-start | bytes 786440 | tf_op jit(solution)/shard_map/ppermute | solution.py:178
  97.0 1.6 %collective-permute-start.16 = (bf16[128,1024]{1,0:T(8,128)(2,1)S(1)}, bf16[128,1024]{1,0:T(8,128)(2,1)S(1)}, u32[]{:S(2)}, u32[]{:S(2)}) collective-permute-start(bf16[128,1024]{1,0:T(8,128)(2,1)S(1)} %pad_maximum_fusion.1), channel_id=1, source_target_pairs={{0,16},{1,17},{2,18},{3,19},{4,20},{5,21},{6,22},{7,23},{8,24},{9,... | collective-permute-start | bytes 786440 | tf_op jit(solution)/shard_map/ppermute | solution.py:178
  100.0 1.6 %collective-permute-start.36 = (bf16[128,1024]{1,0:T(8,128)(2,1)S(1)}, bf16[128,1024]{1,0:T(8,128)(2,1)S(1)}, u32[]{:S(2)}, u32[]{:S(2)}) collective-permute-start(bf16[128,1024]{1,0:T(8,128)(2,1)S(1)} %pad_maximum_fusion.3), channel_id=1, source_target_pairs={{0,16},{1,17},{2,18},{3,19},{4,20},{5,21},{6,22},{7,23},{8,24},{9,... | collective-permute-start | bytes 786440 | tf_op jit(solution)/shard_map/ppermute | solution.py:178
  101.6 3.0 %collective-permute-done.14 = bf16[128,1024]{1,0:T(8,128)(2,1)S(1)} collective-permute-done((bf16[128,1024]{1,0:T(8,128)(2,1)S(1)}, bf16[128,1024]{1,0:T(8,128)(2,1)S(1)}, u32[]{:S(2)}, u32[]{:S(2)}) %collective-permute-start.14) | collective-permute-done | bytes 262176 | tf_op jit(solution)/shard_map/ppermute | solution.py:178
  104.5 1.8 %collective-permute-done.16 = bf16[128,1024]{1,0:T(8,128)(2,1)S(1)} collective-permute-done((bf16[128,1024]{1,0:T(8,128)(2,1)S(1)}, bf16[128,1024]{1,0:T(8,128)(2,1)S(1)}, u32[]{:S(2)}, u32[]{:S(2)}) %collective-permute-start.16) | collective-permute-done | bytes 262176 | tf_op jit(solution)/shard_map/ppermute | solution.py:178
  106.5 6.9 %collective-permute-start.17 = (bf16[32,1024]{1,0:T(8,128)(2,1)S(1)}, bf16[32,1024]{1,0:T(8,128)(2,1)S(1)}, u32[]{:S(2)}, u32[]{:S(2)}) collective-permute-start(bf16[32,1024]{1,0:T(8,128)(2,1)S(1)} %get-tuple-element.29), channel_id=1, source_target_pairs={{0,12},{1,13},{2,14},{3,15},{4,0},{5,1},{6,2},{7,3},{8,4},{9,5},{1... | collective-permute-start | bytes 196616 | tf_op jit(solution)/shard_map/ppermute | solution.py:178
  114.2 3.2 %collective-permute-start.37 = (bf16[32,1024]{1,0:T(8,128)(2,1)S(1)}, bf16[32,1024]{1,0:T(8,128)(2,1)S(1)}, u32[]{:S(2)}, u32[]{:S(2)}) collective-permute-start(bf16[32,1024]{1,0:T(8,128)(2,1)S(1)} %get-tuple-element.32), channel_id=1, source_target_pairs={{0,12},{1,13},{2,14},{3,15},{4,0},{5,1},{6,2},{7,3},{8,4},{9,5},{1... | collective-permute-start | bytes 196616 | tf_op jit(solution)/shard_map/ppermute | solution.py:178
  122.8 1.8 %collective-permute-done.39 = bf16[32,1024]{1,0:T(8,128)(2,1)S(1)} collective-permute-done((bf16[32,1024]{1,0:T(8,128)(2,1)S(1)}, bf16[32,1024]{1,0:T(8,128)(2,1)S(1)}, u32[]{:S(2)}, u32[]{:S(2)}) %collective-permute-start.39) | collective-permute-done | bytes 65568 | tf_op jit(solution)/shard_map/ppermute | solution.py:178
  (101 shorter events, 29.5 us)
Async XLA Ops:
  4.5 8.0 %collective-permute-start = (bf16[32,1152]{1,0:T(8,128)(2,1)}, bf16[32,1152]{1,0:T(8,128)(2,1)S(1)}, u32[]{:S(2)}, u32[]{:S(2)}) collective-permute-start(bf16[32,1152]{1,0:T(8,128)(2,1)} %get-tuple-element.11.refs_0_), channel_id=1, source_target_pairs={{0,4},{1,5},{2,6},{3,7},{4,8},{5,9},{6,10},{7,11},{8,12},{9,13},{1... | collective-permute-start | bytes 221192 | tf_op jit(solution)/shard_map/ppermute | solution.py:178
  7.5 7.9 %collective-permute-start.1 = (bf16[32,1152]{1,0:T(8,128)(2,1)}, bf16[32,1152]{1,0:T(8,128)(2,1)S(1)}, u32[]{:S(2)}, u32[]{:S(2)}) collective-permute-start(bf16[32,1152]{1,0:T(8,128)(2,1)} %get-tuple-element.11.refs_0_), channel_id=1, source_target_pairs={{0,8},{1,9},{2,10},{3,11},{4,12},{5,13},{6,14},{7,15},{8,0},{9,1},... | collective-permute-start | bytes 221192 | tf_op jit(solution)/shard_map/ppermute | solution.py:178
  11.5 18.7 %collective-permute-start.20 = (bf16[32,1152]{1,0:T(8,128)(2,1)}, bf16[32,1152]{1,0:T(8,128)(2,1)S(1)}, u32[]{:S(2)}, u32[]{:S(2)}) collective-permute-start(bf16[32,1152]{1,0:T(8,128)(2,1)} %get-tuple-element.14.refs_0_), channel_id=1, source_target_pairs={{0,4},{1,5},{2,6},{3,7},{4,8},{5,9},{6,10},{7,11},{8,12},{9,13},{1... | collective-permute-start | bytes 221192 | tf_op jit(solution)/shard_map/ppermute | solution.py:178
  12.1 18.1 %collective-permute-start.21 = (bf16[32,1152]{1,0:T(8,128)(2,1)}, bf16[32,1152]{1,0:T(8,128)(2,1)S(1)}, u32[]{:S(2)}, u32[]{:S(2)}) collective-permute-start(bf16[32,1152]{1,0:T(8,128)(2,1)} %get-tuple-element.14.refs_0_), channel_id=1, source_target_pairs={{0,8},{1,9},{2,10},{3,11},{4,12},{5,13},{6,14},{7,15},{8,0},{9,1},... | collective-permute-start | bytes 221192 | tf_op jit(solution)/shard_map/ppermute | solution.py:178
  12.5 17.7 %collective-permute-start.22 = (bf16[32,1152]{1,0:T(8,128)(2,1)}, bf16[32,1152]{1,0:T(8,128)(2,1)S(1)}, u32[]{:S(2)}, u32[]{:S(2)}) collective-permute-start(bf16[32,1152]{1,0:T(8,128)(2,1)} %get-tuple-element.14.refs_0_), channel_id=1, source_target_pairs={{0,12},{1,13},{2,14},{3,15},{4,0},{5,1},{6,2},{7,3},{8,4},{9,5},{1... | collective-permute-start | bytes 221192 | tf_op jit(solution)/shard_map/ppermute | solution.py:178
  27.2 15.5 %collective-permute-start.3 = (bf16[128,1152]{1,0:T(8,128)(2,1)}, bf16[128,1152]{1,0:T(8,128)(2,1)S(1)}, u32[]{:S(2)}, u32[]{:S(2)}) collective-permute-start(bf16[128,1152]{1,0:T(8,128)(2,1)} %shard_map.65.refs_0_), channel_id=1, source_target_pairs={{0,2},{1,3},{2,0},{3,1},{4,6},{5,7},{6,4},{7,5},{8,10},{9,11},{10,... | collective-permute-start | bytes 884744 | tf_op jit(solution)/shard_map/ppermute | solution.py:178
  28.7 15.6 %collective-permute-start.4 = (bf16[128,1152]{1,0:T(8,128)(2,1)}, bf16[128,1152]{1,0:T(8,128)(2,1)S(1)}, u32[]{:S(2)}, u32[]{:S(2)}) collective-permute-start(bf16[128,1152]{1,0:T(8,128)(2,1)} %shard_map.65.refs_0_), channel_id=1, source_target_pairs={{0,16},{1,17},{2,18},{3,19},{4,20},{5,21},{6,22},{7,23},{8,24},{9,... | collective-permute-start | bytes 884744 | tf_op jit(solution)/shard_map/ppermute | solution.py:178
  41.6 7.8 %collective-permute-start.23 = (bf16[128,1152]{1,0:T(8,128)(2,1)}, bf16[128,1152]{1,0:T(8,128)(2,1)S(1)}, u32[]{:S(2)}, u32[]{:S(2)}) collective-permute-start(bf16[128,1152]{1,0:T(8,128)(2,1)} %shard_map.67.refs_0_), channel_id=1, source_target_pairs={{0,2},{1,3},{2,0},{3,1},{4,6},{5,7},{6,4},{7,5},{8,10},{9,11},{10,... | collective-permute-start | bytes 884744 | tf_op jit(solution)/shard_map/ppermute | solution.py:178
  42.2 10.0 %collective-permute-start.24 = (bf16[128,1152]{1,0:T(8,128)(2,1)}, bf16[128,1152]{1,0:T(8,128)(2,1)S(1)}, u32[]{:S(2)}, u32[]{:S(2)}) collective-permute-start(bf16[128,1152]{1,0:T(8,128)(2,1)} %shard_map.67.refs_0_), channel_id=1, source_target_pairs={{0,16},{1,17},{2,18},{3,19},{4,20},{5,21},{6,22},{7,23},{8,24},{9,... | collective-permute-start | bytes 884744 | tf_op jit(solution)/shard_map/ppermute | solution.py:178
  42.7 12.6 %collective-permute-start.5 = (bf16[64,1152]{1,0:T(8,128)(2,1)S(1)}, bf16[64,1152]{1,0:T(8,128)(2,1)S(1)}, u32[]{:S(2)}, u32[]{:S(2)}) collective-permute-start(bf16[64,1152]{1,0:T(8,128)(2,1)S(1)} %slice.104), channel_id=1, source_target_pairs={{0,16},{1,17},{2,18},{3,19},{4,20},{5,21},{6,22},{7,23},{8,24},{9,... | collective-permute-start | bytes 442376 | tf_op jit(solution)/shard_map/ppermute | solution.py:178
  44.3 16.2 %collective-permute-start.8 = (bf16[128,1152]{1,0:T(8,128)(2,1)S(1)}, bf16[128,1152]{1,0:T(8,128)(2,1)S(1)}, u32[]{:S(2)}, u32[]{:S(2)}) collective-permute-start(bf16[128,1152]{1,0:T(8,128)(2,1)S(1)} %collective-permute-done.3.refs_1_), channel_id=1, source_target_pairs={{0,1},{1,0},{2,3},{3,2},{4,5},{5,4},{6,7},{7,6},{8,9},{9,8},{10,11... | collective-permute-start | bytes 884744 | tf_op jit(solution)/shard_map/ppermute | solution.py:178
  49.4 11.6 %collective-permute-start.9 = (bf16[128,1152]{1,0:T(8,128)(2,1)S(1)}, bf16[128,1152]{1,0:T(8,128)(2,1)S(1)}, u32[]{:S(2)}, u32[]{:S(2)}) collective-permute-start(bf16[128,1152]{1,0:T(8,128)(2,1)S(1)} %collective-permute-done.4.refs_2_), channel_id=1, source_target_pairs={{0,1},{1,0},{2,3},{3,2},{4,5},{5,4},{6,7},{7,6},{8,9},{9,8},{10,11... | collective-permute-start | bytes 884744 | tf_op jit(solution)/shard_map/ppermute | solution.py:178
  49.4 7.4 %collective-permute-start.6 = (bf16[64,1152]{1,0:T(8,128)(2,1)S(1)}, bf16[64,1152]{1,0:T(8,128)(2,1)S(1)}, u32[]{:S(2)}, u32[]{:S(2)}) collective-permute-start(bf16[64,1152]{1,0:T(8,128)(2,1)S(1)} %slice.105), channel_id=1, source_target_pairs={{0,2},{1,3},{2,0},{3,1},{4,6},{5,7},{6,4},{7,5},{8,10},{9,11},{10,... | collective-permute-start | bytes 442376 | tf_op jit(solution)/shard_map/ppermute | solution.py:178
  60.5 14.6 %collective-permute-start.27 = (bf16[128,1152]{1,0:T(8,128)(2,1)}, bf16[128,1152]{1,0:T(8,128)(2,1)S(1)}, u32[]{:S(2)}, u32[]{:S(2)}) collective-permute-start(bf16[128,1152]{1,0:T(8,128)(2,1)} %shard_map.67.refs_0_), channel_id=1, source_target_pairs={{0,1},{1,0},{2,3},{3,2},{4,5},{5,4},{6,7},{7,6},{8,9},{9,8},{10,11... | collective-permute-start | bytes 884744 | tf_op jit(solution)/shard_map/ppermute | solution.py:178
  60.5 15.1 %collective-permute-start.28 = (bf16[128,1152]{1,0:T(8,128)(2,1)S(1)}, bf16[128,1152]{1,0:T(8,128)(2,1)S(1)}, u32[]{:S(2)}, u32[]{:S(2)}) collective-permute-start(bf16[128,1152]{1,0:T(8,128)(2,1)S(1)} %collective-permute-done.23.refs_1_), channel_id=1, source_target_pairs={{0,1},{1,0},{2,3},{3,2},{4,5},{5,4},{6,7},{7,6},{8,9},{9,8},{10,11... | collective-permute-start | bytes 884744 | tf_op jit(solution)/shard_map/ppermute | solution.py:178
  61.0 14.6 %collective-permute-start.29 = (bf16[128,1152]{1,0:T(8,128)(2,1)S(1)}, bf16[128,1152]{1,0:T(8,128)(2,1)S(1)}, u32[]{:S(2)}, u32[]{:S(2)}) collective-permute-start(bf16[128,1152]{1,0:T(8,128)(2,1)S(1)} %collective-permute-done.24.refs_2_), channel_id=1, source_target_pairs={{0,1},{1,0},{2,3},{3,2},{4,5},{5,4},{6,7},{7,6},{8,9},{9,8},{10,11... | collective-permute-start | bytes 884744 | tf_op jit(solution)/shard_map/ppermute | solution.py:178
  61.1 14.5 %collective-permute-start.30 = (bf16[64,1152]{1,0:T(8,128)(2,1)S(1)}, bf16[64,1152]{1,0:T(8,128)(2,1)S(1)}, u32[]{:S(2)}, u32[]{:S(2)}) collective-permute-start(bf16[64,1152]{1,0:T(8,128)(2,1)S(1)} %collective-permute-done.25.refs_3_), channel_id=1, source_target_pairs={{0,1},{1,0},{2,3},{3,2},{4,5},{5,4},{6,7},{7,6},{8,9},{9,8},{10,11... | collective-permute-start | bytes 442376 | tf_op jit(solution)/shard_map/ppermute | solution.py:178
  61.5 14.1 %collective-permute-start.31 = (bf16[64,1152]{1,0:T(8,128)(2,1)S(1)}, bf16[64,1152]{1,0:T(8,128)(2,1)S(1)}, u32[]{:S(2)}, u32[]{:S(2)}) collective-permute-start(bf16[64,1152]{1,0:T(8,128)(2,1)S(1)} %collective-permute-done.26.refs_4_), channel_id=1, source_target_pairs={{0,1},{1,0},{2,3},{3,2},{4,5},{5,4},{6,7},{7,6},{8,9},{9,8},{10,11... | collective-permute-start | bytes 442376 | tf_op jit(solution)/shard_map/ppermute | solution.py:178
  75.1 13.2 %collective-permute-start.12 = (bf16[2,256,1024]{2,1,0:T(8,128)(2,1)S(1)}, bf16[2,256,1024]{2,1,0:T(8,128)(2,1)S(1)}, u32[]{:S(2)}, u32[]{:S(2)}) collective-permute-start(bf16[2,256,1024]{2,1,0:T(8,128)(2,1)S(1)} %get-tuple-element.13), channel_id=1, source_target_pairs={{0,1},{1,0},{2,3},{3,2},{4,5},{5,4},{6,7},{7,6},{8,9},{9,8},{10,11... | collective-permute-start | bytes 3145736 | tf_op jit(solution)/shard_map/ppermute | solution.py:178
  95.2 9.3 %collective-permute-start.14 = (bf16[128,1024]{1,0:T(8,128)(2,1)S(1)}, bf16[128,1024]{1,0:T(8,128)(2,1)S(1)}, u32[]{:S(2)}, u32[]{:S(2)}) collective-permute-start(bf16[128,1024]{1,0:T(8,128)(2,1)S(1)} %pad_maximum_fusion), channel_id=1, source_target_pairs={{0,2},{1,3},{2,0},{3,1},{4,6},{5,7},{6,4},{7,5},{8,10},{9,11},{10,... | collective-permute-start | bytes 786440 | tf_op jit(solution)/shard_map/ppermute | solution.py:178
  97.0 9.3 %collective-permute-start.16 = (bf16[128,1024]{1,0:T(8,128)(2,1)S(1)}, bf16[128,1024]{1,0:T(8,128)(2,1)S(1)}, u32[]{:S(2)}, u32[]{:S(2)}) collective-permute-start(bf16[128,1024]{1,0:T(8,128)(2,1)S(1)} %pad_maximum_fusion.1), channel_id=1, source_target_pairs={{0,16},{1,17},{2,18},{3,19},{4,20},{5,21},{6,22},{7,23},{8,24},{9,... | collective-permute-start | bytes 786440 | tf_op jit(solution)/shard_map/ppermute | solution.py:178
  98.8 15.3 %collective-permute-start.34 = (bf16[128,1024]{1,0:T(8,128)(2,1)S(1)}, bf16[128,1024]{1,0:T(8,128)(2,1)S(1)}, u32[]{:S(2)}, u32[]{:S(2)}) collective-permute-start(bf16[128,1024]{1,0:T(8,128)(2,1)S(1)} %pad_maximum_fusion.2), channel_id=1, source_target_pairs={{0,2},{1,3},{2,0},{3,1},{4,6},{5,7},{6,4},{7,5},{8,10},{9,11},{10,... | collective-permute-start | bytes 786440 | tf_op jit(solution)/shard_map/ppermute | solution.py:178
  100.0 14.1 %collective-permute-start.36 = (bf16[128,1024]{1,0:T(8,128)(2,1)S(1)}, bf16[128,1024]{1,0:T(8,128)(2,1)S(1)}, u32[]{:S(2)}, u32[]{:S(2)}) collective-permute-start(bf16[128,1024]{1,0:T(8,128)(2,1)S(1)} %pad_maximum_fusion.3), channel_id=1, source_target_pairs={{0,16},{1,17},{2,18},{3,19},{4,20},{5,21},{6,22},{7,23},{8,24},{9,... | collective-permute-start | bytes 786440 | tf_op jit(solution)/shard_map/ppermute | solution.py:178
  106.5 12.1 %collective-permute-start.17 = (bf16[32,1024]{1,0:T(8,128)(2,1)S(1)}, bf16[32,1024]{1,0:T(8,128)(2,1)S(1)}, u32[]{:S(2)}, u32[]{:S(2)}) collective-permute-start(bf16[32,1024]{1,0:T(8,128)(2,1)S(1)} %get-tuple-element.29), channel_id=1, source_target_pairs={{0,12},{1,13},{2,14},{3,15},{4,0},{5,1},{6,2},{7,3},{8,4},{9,5},{1... | collective-permute-start | bytes 196616 | tf_op jit(solution)/shard_map/ppermute | solution.py:178
  (24 other events, 112.2 us)

commit v2 on v0

v2 whole, which is shorter than its diff:
```python
import functools

import jax
import jax.numpy as jnp
from jax import lax
from jax.experimental import pallas as pl
from jax.experimental.pallas import tpu as pltpu
from jax.sharding import PartitionSpec as P

BF16, F32 = jnp.bfloat16, jnp.float32
PAIR = ("dp", "expert")
CHUNKS = 2
LANES = 128
MIB = 1024 * 1024
VMEM_SPEC = pl.BlockSpec(memory_space=pltpu.VMEM)


def near(array):
    return pltpu.with_memory_space_constraint(array, pltpu.VMEM)


def route_table(ids, weights, experts):
    lane = lax.broadcasted_iota(jnp.int32, (ids.shape[0], experts), 1)
    table = jnp.zeros((ids.shape[0], experts), F32)
    for k in range(ids.shape[1]):
        table = table + jnp.where(ids[:, k : k + 1] == lane, weights[:, k : k + 1].astype(F32), 0.0)
    return table


def pack_kernel(tok_ref, ids_ref, rw_ref, *outs):
    rows, width = tok_ref.shape
    columns = outs[0].shape[1] - width
    line = lax.broadcasted_iota(jnp.int32, (columns, rows), 0)
    table = jnp.zeros((columns, rows), F32)
    for k in range(ids_ref.shape[0]):
        table = table + jnp.where(ids_ref[k : k + 1, :] == line, rw_ref[k : k + 1, :].astype(F32), 0.0)
    table = table.T.astype(BF16)
    part = rows // len(outs)
    for i, out in enumerate(outs):
        out[:, :width] = tok_ref[i * part : (i + 1) * part, :]
        out[:, width:] = table[i * part : (i + 1) * part, :]


def pack(tokens, ids, route_weights, columns):
    rows, width = tokens.shape
    one = jax.ShapeDtypeStruct((rows // CHUNKS, width + columns), BF16)
    return pl.pallas_call(
        pack_kernel,
        in_specs=[VMEM_SPEC] * 3,
        out_specs=[VMEM_SPEC] * CHUNKS,
        out_shape=[one] * CHUNKS,
        compiler_params=pltpu.CompilerParams(vmem_limit_bytes=2 * MIB),
    )(tokens, ids.T, route_weights.T)


def experts_kernel(first, counts, places, gate_in, up_in, down_in, *refs):
    if first:
        pieces, refs = refs[:-9], refs[-9:]
        keep_ref, give_ref, gate_ref, up_ref, down_ref, rows_buf, weight_buf, hidden_buf, sem = refs
    else:
        pieces, refs = refs[:-5], refs[-5:]
        keep_ref, give_ref, rows_buf, weight_buf, hidden_buf = refs
        gate_ref, up_ref, down_ref = gate_in, up_in, down_in
    experts, model, hidden = gate_ref.shape
    width = model // 2
    block, part = hidden // 2, width // 2
    steps = [(e, half) for e in range(experts) for half in range(2)]
    parts = [(side, half) for side in range(2) for half in range(2)]

    fetches = []
    if first:
        for e, half in steps:
            span = (e, slice(None), pl.ds(half * block, block))
            pair = [(gate_in.at[span], gate_ref.at[span]), (up_in.at[span], up_ref.at[span])]
            fetches.append(pair)
        for j in range(2):
            span = pl.ds(j * (experts * hidden // 2), experts * hidden // 2)
            fetches.append([(down_in.at[span], down_ref.at[span])])
        fetches = [
            [pltpu.make_async_copy(*ends, sem.at[2 * i + k]) for k, ends in enumerate(group)]
            for i, group in enumerate(fetches)
        ]
        for group in fetches:
            for copy in group:
                copy.start()

    mine = pl.ds(pl.multiple_of(places[0] * width, width), width)
    others = pl.ds(pl.multiple_of((1 - places[0]) * width, width), width)
    taken = 0
    for count, columns in zip(counts, (mine, others)):
        row = 0
        for piece in pieces[taken : taken + count]:
            span = pl.ds(row, piece.shape[0])
            rows_buf[span, columns] = piece[:, :width]
            if columns is mine:
                table = piece[:, width:].astype(F32)
                lane = lax.broadcasted_iota(jnp.int32, table.shape, 1)
                for e in range(experts):
                    hit = jnp.where(lane == places[1] * experts + e, table, 0.0)
                    weight_buf[e, span, :] = jnp.sum(hit, axis=1, keepdims=True)
            row += piece.shape[0]
        taken += count

    half_rows = rows_buf.shape[0] // 2
    for i, (e, half) in enumerate(steps):
        if first:
            for copy in fetches[i]:
                copy.wait()
        rows, span = rows_buf[...], pl.ds(half * block, block)
        gate = jnp.dot(rows, gate_ref[e, :, span], preferred_element_type=F32)
        up = jnp.dot(rows, up_ref[e, :, span], preferred_element_type=F32)
        value = gate / (1.0 + jnp.exp(-gate)) * up * weight_buf[e]
        hidden_buf[:, pl.ds(i * block, block)] = value.astype(BF16)
    if first:
        for group in fetches[len(steps) :]:
            for copy in group:
                copy.wait()
    for side, half in parts:
        at = pl.multiple_of((side + places[0]) % 2 * width + half * part, part)
        out = jnp.dot(hidden_buf[...], down_ref[:, pl.ds(at, part)], preferred_element_type=F32)
        keep_ref[side, :, pl.ds(half * part, part)] = out[:half_rows].astype(BF16)
        give_ref[side, :, pl.ds(half * part, part)] = out[half_rows:].astype(BF16)


def run_experts(places, weights, mine, others, first):
    experts, model, hidden = weights[0].shape
    width = model // 2
    rows = sum(piece.shape[0] for piece in mine)
    out = jax.ShapeDtypeStruct((2, rows // 2, width), BF16)
    where = pltpu.HBM if first else pltpu.VMEM
    operands = [pltpu.with_memory_space_constraint(w, where) for w in weights]
    operands += [near(piece) for piece in (*mine, *others)]
    specs = [pl.BlockSpec(memory_space=pl.ANY if first else pltpu.VMEM)] * 3
    specs += [VMEM_SPEC] * (len(operands) - 3)
    outs, extra = [out, out], []
    if first:
        outs += [jax.ShapeDtypeStruct(w.shape, BF16) for w in weights]
        extra = [pltpu.SemaphoreType.DMA((4 * experts + 4,))]
    return pl.pallas_call(
        functools.partial(experts_kernel, first, (len(mine), len(others))),
        in_specs=[pl.BlockSpec(memory_space=pltpu.SMEM)] + specs,
        out_specs=[VMEM_SPEC] * len(outs),
        scratch_shapes=[
            pltpu.VMEM((rows, model), BF16),
            pltpu.VMEM((experts, rows, 1), F32),
            pltpu.VMEM((rows, experts * hidden), BF16),
        ]
        + extra,
        out_shape=outs,
        compiler_params=pltpu.CompilerParams(vmem_limit_bytes=16 * MIB),
        cost_estimate=pl.CostEstimate(
            flops=6 * rows * model * hidden * experts,
            bytes_accessed=6 * model * hidden * experts + 4 * rows * model,
            transcendentals=rows * hidden * experts,
        ),
    )(places, *operands)


def add(*terms):
    return functools.reduce(lambda a, b: a + b, [t.astype(F32) for t in terms]).astype(BF16)


def planned(peers, tokens, expert_ids, route_weights, w_gate, w_up, w_down):
    line = peers // 4

    def send(array, steps=0, x=0, core=0, y=0):
        pairs = []
        for side in range(2):
            for e in range(peers):
                to = (e // 4 + steps) % line * 4 + ((e // 2 % 2) ^ x) * 2 + ((e % 2) ^ core)
                pairs.append((side * peers + e, (side ^ y) * peers + to))
        return lax.ppermute(array, PAIR, pairs)

    expert_count = peers * w_gate.shape[0]
    columns = -(-expert_count // LANES) * LANES
    places = jnp.stack([lax.axis_index("dp"), lax.axis_index("expert")]).astype(jnp.int32)
    chunks = pack(tokens, expert_ids, route_weights, columns)

    def join(pieces):
        return jnp.concatenate(pieces, 0)

    def cores(pieces):
        return [send(piece, core=1) for piece in pieces]

    def scatter(total, total_x):
        side, rows = total.shape[1], total.shape[1] // line
        half = side // 2
        got_a, got_b = send(total_x[1, :half], x=1), send(total_x[1, half:], y=1)
        for_x = join([total_x[0, :half], add(total_x[0, half:], got_b)])
        for_y = join([add(total[1, :half], got_a), total[1, half:]])
        mine = add(total[0], send(for_x, x=1), send(for_y, y=1))
        back = [send(mine[k * rows : (k + 1) * rows], steps=line - k) for k in range(1, line)]
        return add(mine[:rows], *back)

    weights = (w_gate, w_up, w_down.reshape(-1, w_down.shape[2]))
    first, outs = True, []
    for chunk in chunks:
        own = join([chunk] + [send(chunk, steps=k) for k in range(1, line)])
        half = own.shape[0] // 2
        by_x, by_y = send(own, x=1), send(own, y=1)
        diag = [send(by_x[:half], y=1), send(by_y[half:], x=1)]
        keep, give, *rest = run_experts(places, weights, [own] + cores([own]), [by_y] + cores([by_y]), first)
        if first:
            weights, first = rest, False
        total = add(keep, send(give, core=1))
        keep, give = run_experts(places, weights, [by_x] + cores([by_x]), diag + cores(diag), first)
        outs.append(scatter(total, add(keep, send(give, core=1))))
    return join(outs)


def general(tokens, expert_ids, route_weights, w_gate, w_up, w_down):
    peers, local = lax.axis_size("expert"), w_gate.shape[0]
    table = route_table(expert_ids, route_weights, peers * local).astype(BF16)
    rows = lax.all_gather(tokens, "expert", axis=0, tiled=True)
    rows = lax.all_gather(rows, "dp", axis=1, tiled=True)
    table = lax.all_gather(table, "expert", axis=0, tiled=True).astype(F32)
    weight = lax.dynamic_slice_in_dim(table, lax.axis_index("expert") * local, local, 1)
    gate = jnp.einsum("td,rdf->trf", rows, w_gate, preferred_element_type=F32)
    up = jnp.einsum("td,rdf->trf", rows, w_up, preferred_element_type=F32)
    hidden = (jax.nn.silu(gate) * up * weight[:, :, None]).astype(BF16)
    out = jnp.einsum("trf,rfd->td", hidden, w_down, preferred_element_type=F32).astype(BF16)
    out = lax.psum_scatter(out, "dp", scatter_dimension=1, tiled=True)
    return lax.psum_scatter(out, "expert", scatter_dimension=0, tiled=True)


def solution(mesh):
    peers = mesh.shape["expert"]
    body = general
    if mesh.shape["dp"] == 2 and peers % 4 == 0:
        body = functools.partial(planned, peers)
    return jax.shard_map(
        body,
        mesh=mesh,
        in_specs=(
            P("expert", "dp"),
            P("expert", None),
            P("expert", None),
            P("expert", None, "dp"),
            P("expert", None, "dp"),
            P("expert", "dp", None),
        ),
        out_specs=P("expert", "dp"),
        check_vma=False,
    )
```

time: 206 us -> 93.5 us (0.45)
  blocking collectives: 158 us -> 0 us
  starting transfers between devices: 0.01 us -> 43.5 us
  Pallas kernels: 0 us -> 19.6 us
  matrix products: 14.4 us -> 0 us
  between operations: 13.4 us -> 0.34 us
  waiting for transfers between devices: 12.4 us -> 25.3 us
    all_to_all x2 -> x0, blocking collectives: 151 us -> none  [the longest x1 75.9 us: on_device(): lax.all_to_all(send_rows, 'expert', split_axis=0, concat_axis=0, tiled=True)]
    ppermute x0 -> x42, starting transfers between devices: none -> 43.5 us  [send(): return lax.ppermute(array, PAIR, pairs)]
    ppermute x0 -> x42, waiting for transfers between devices: none -> 25.3 us  [send(): return lax.ppermute(array, PAIR, pairs)]
    pallas_call x0 -> x5, Pallas kernels: none -> 19.6 us  [the longest x4 19.5 us: run_experts(): pl.pallas_call(functools.partial(experts_kernel, first, (len(mine), len(o...]
    dot_general x4 -> x0, matrix products: 14.4 us -> none  [the longest x1 9.1 us: finish_expert(): jnp.einsum('nrcf,rfd->nrcd', hidden, w_down, preferred_element_type=jnp.f...]
    reduce_scatter x1 -> x0, waiting for transfers between devices: 12.3 us -> none  [on_device(): lax.psum_scatter(mixed_rows.astype(jnp.bfloat16), 'dp', scatter_dimension...]
    all_gather x1 -> x0, blocking collectives: 7.38 us -> none  [on_device(): whole = lax.all_gather(tokens, 'dp', axis=1, tiled=True)]
    convert_element_type x2 -> x0, local copies, waits for them, and re-layouts: 3.06 us -> none  [the longest x1 2.29 us: finish_expert(): jnp.einsum('nrcf,rfd->nrcd', hidden, w_down, preferred_element_type=jnp.f...]
  transfers between devices with their start and end apart: 1 -> 42, of which waited for: 1 -> 10; matrix products, arithmetic and copies ran while one was open for 0% -> 2% of each run, Pallas kernels for 0% -> 21%
where the time goes in v2:
time: 93.5 us; the launch traced here: 93.3 us
  starting transfers between devices  43.5 us (47%)
  waiting for transfers between devices  25.3 us (27%)
  Pallas kernels  19.6 us (21%)
  local copies, waits for them, and re-layouts  2.52 us (3%)
  other arithmetic  2.05 us (2%)
    ppermute x42, starting transfers between devices, send(): return lax.ppermute(array, PAIR, pairs)  43.5 us
    ppermute x42, waiting for transfers between devices, send(): return lax.ppermute(array, PAIR, pairs)  25.3 us
    pallas_call x4, Pallas kernels, run_experts(): pl.pallas_call(functools.partial(experts_kernel, first, (len(mine), len(o...  19.5 us
    unnamed x12, local copies, waits for them, and re-layouts  2.34 us
  transfers between devices with their start and end apart: 42, of which 10 were waited for; matrix products, arithmetic and copies ran while one was open for 2% of the time, Pallas kernels for 21%

profile of v2, /device:TPU:0, one launch (start us, length us, event | category | flops | bytes accessed | tf_op | source)
XLA Modules:
  0.0 93.3 jit_solution(4073249878375131595)
XLA Ops:
  2.4 3.1 %collective-permute-start = (bf16[32,1152]{1,0:T(8,128)(2,1)S(1)}, bf16[32,1152]{1,0:T(8,128)(2,1)S(1)}, u32[]{:S(2)}, u32[]{:S(2)}) collective-permute-start(bf16[32,1152]{1,0:T(8,128)(2,1)S(1)} %get-tuple-element.18), channel_id=1, source_target_pairs={{0,4},{1,5},{2,6},{3,7},{4,8},{5,9},{6,10},{7,11},{8,12},{9,13},{1... | collective-permute-start | bytes 221192 | tf_op jit(solution)/shard_map/ppermute | solution.py:172
  5.5 2.6 %collective-permute-start.1 = (bf16[32,1152]{1,0:T(8,128)(2,1)S(1)}, bf16[32,1152]{1,0:T(8,128)(2,1)S(1)}, u32[]{:S(2)}, u32[]{:S(2)}) collective-permute-start(bf16[32,1152]{1,0:T(8,128)(2,1)S(1)} %get-tuple-element.18), channel_id=1, source_target_pairs={{0,8},{1,9},{2,10},{3,11},{4,12},{5,13},{6,14},{7,15},{8,0},{9,1},... | collective-permute-start | bytes 221192 | tf_op jit(solution)/shard_map/ppermute | solution.py:172
  10.4 2.9 %collective-permute-start.23 = (bf16[32,1152]{1,0:T(8,128)(2,1)S(1)}, bf16[32,1152]{1,0:T(8,128)(2,1)S(1)}, u32[]{:S(2)}, u32[]{:S(2)}) collective-permute-start(bf16[32,1152]{1,0:T(8,128)(2,1)S(1)} %get-tuple-element.26), channel_id=1, source_target_pairs={{0,12},{1,13},{2,14},{3,15},{4,0},{5,1},{6,2},{7,3},{8,4},{9,5},{1... | collective-permute-start | bytes 221192 | tf_op jit(solution)/shard_map/ppermute | solution.py:172
  15.2 1.5 %collective-permute-start.7 = (bf16[128,1152]{1,0:T(8,128)(2,1)S(1)}, bf16[128,1152]{1,0:T(8,128)(2,1)S(1)}, u32[]{:S(2)}, u32[]{:S(2)}) collective-permute-start(bf16[128,1152]{1,0:T(8,128)(2,1)S(1)} %constant_dynamic-update-slice_fusion.refs_0_), channel_id=1, source_target_pairs={{0,2},{1,3},{2,0},{3,1},{4,6},{5,7},{6,4},{7,5},{8,10},{9,11},{10,... | collective-permute-start | bytes 884744 | tf_op jit(solution)/shard_map/ppermute | solution.py:172
  16.7 2.6 %collective-permute-done.22 = bf16[32,1152]{1,0:T(8,128)(2,1)S(1)} collective-permute-done((bf16[32,1152]{1,0:T(8,128)(2,1)S(1)}, bf16[32,1152]{1,0:T(8,128)(2,1)S(1)}, u32[]{:S(2)}, u32[]{:S(2)}) %collective-permute-start.22) | collective-permute-done | bytes 73760 | tf_op jit(solution)/shard_map/ppermute | solution.py:172
  19.4 1.7 %collective-permute-start.28 = (bf16[128,1152]{1,0:T(8,128)(2,1)S(1)}, bf16[128,1152]{1,0:T(8,128)(2,1)S(1)}, u32[]{:S(2)}, u32[]{:S(2)}) collective-permute-start(bf16[128,1152]{1,0:T(8,128)(2,1)S(1)} %constant_dynamic-update-slice_fusion.4.refs_0_), channel_id=1, source_target_pairs={{0,2},{1,3},{2,0},{3,1},{4,6},{5,7},{6,4},{7,5},{8,10},{9,11},{10,... | collective-permute-start | bytes 884744 | tf_op jit(solution)/shard_map/ppermute | solution.py:172
  21.1 1.5 %collective-permute-start.25 = (bf16[128,1152]{1,0:T(8,128)(2,1)S(1)}, bf16[128,1152]{1,0:T(8,128)(2,1)S(1)}, u32[]{:S(2)}, u32[]{:S(2)}) collective-permute-start(bf16[128,1152]{1,0:T(8,128)(2,1)S(1)} %constant_dynamic-update-slice_fusion.4.refs_0_), channel_id=1, source_target_pairs={{0,16},{1,17},{2,18},{3,19},{4,20},{5,21},{6,22},{7,23},{8,24},{9,... | collective-permute-start | bytes 884744 | tf_op jit(solution)/shard_map/ppermute | solution.py:172
  24.1 5.2 %collective-permute-done.28.refs_0_ = bf16[128,1152]{1,0:T(8,128)(2,1)S(1)} collective-permute-done((bf16[128,1152]{1,0:T(8,128)(2,1)S(1)}, bf16[128,1152]{1,0:T(8,128)(2,1)S(1)}, u32[]{:S(2)}, u32[]{:S(2)}) %collective-permute-start.28) | collective-permute-done | bytes 294944 | tf_op jit(solution)/shard_map/ppermute | solution.py:172
  29.3 1.5 %collective-permute-start.10 = (bf16[64,1152]{1,0:T(8,128)(2,1)S(1)}, bf16[64,1152]{1,0:T(8,128)(2,1)S(1)}, u32[]{:S(2)}, u32[]{:S(2)}) collective-permute-start(bf16[64,1152]{1,0:T(8,128)(2,1)S(1)} %slice.106), channel_id=1, source_target_pairs={{0,2},{1,3},{2,0},{3,1},{4,6},{5,7},{6,4},{7,5},{8,10},{9,11},{10,... | collective-permute-start | bytes 442376 | tf_op jit(solution)/shard_map/ppermute | solution.py:172
  30.9 1.5 %collective-permute-start.30 = (bf16[64,1152]{1,0:T(8,128)(2,1)S(1)}, bf16[64,1152]{1,0:T(8,128)(2,1)S(1)}, u32[]{:S(2)}, u32[]{:S(2)}) collective-permute-start(bf16[64,1152]{1,0:T(8,128)(2,1)S(1)} %slice.118), channel_id=1, source_target_pairs={{0,16},{1,17},{2,18},{3,19},{4,20},{5,21},{6,22},{7,23},{8,24},{9,... | collective-permute-start | bytes 442376 | tf_op jit(solution)/shard_map/ppermute | solution.py:172
  33.0 2.8 %collective-permute-done.10.refs_3_ = bf16[64,1152]{1,0:T(8,128)(2,1)S(1)} collective-permute-done((bf16[64,1152]{1,0:T(8,128)(2,1)S(1)}, bf16[64,1152]{1,0:T(8,128)(2,1)S(1)}, u32[]{:S(2)}, u32[]{:S(2)}) %collective-permute-start.10) | collective-permute-done | bytes 147488 | tf_op jit(solution)/shard_map/ppermute | solution.py:172
  36.3 6.6 %shard_map.65 = (bf16[2,128,1024]{2,1,0:T(8,128)(2,1)S(1)}, bf16[2,128,1024]{2,1,0:T(8,128)(2,1)S(1)}, bf16[2,2048,512]{2,1,0:T(8,128)(2,1)S(1)}, bf16[2,2048,51...) custom-call(s32[2]{0:T(128)S(1)} %pad_add_fusion.places, bf16[2,2048,512]{2,1,0:T(8,128)(2,1)} %gate_in.1, ...), custom_call_target="tpu_custom_call" | custom-call | flops 3221225472 | bytes 14680064 | tf_op jit(solution)/shard_map/pallas_call | solution.py:139
  44.1 4.2 %shard_map.66 = (bf16[2,128,1024]{2,1,0:T(8,128)(2,1)S(1)}, bf16[2,128,1024]{2,1,0:T(8,128)(2,1)S(1)}) custom-call(s32[2]{0:T(128)S(1)} %pad_add_fusion.places, bf16[2,2048,512]{2,1,0:T(8,128)(2,1)S(1)} %get-tuple-element.21.gate_in, bf16[2,2048,512]{2,1,0:T(8,128)(2,1)S(1)} %get-tuple-element.22.up_in, bf16[1024,2048]{1,0:T(8,128)(2,1)S(1)} %get-tuple-element.23.down_in, ...), custom_call_target="tpu_custom_call" | custom-call | flops 3221225472 | bytes 14680064 | tf_op jit(solution)/shard_map/pallas_call | solution.py:139
  49.0 4.2 %shard_map.68 = (bf16[2,128,1024]{2,1,0:T(8,128)(2,1)S(1)}, bf16[2,128,1024]{2,1,0:T(8,128)(2,1)S(1)}) custom-call(s32[2]{0:T(128)S(1)} %pad_add_fusion.places, bf16[2,2048,512]{2,1,0:T(8,128)(2,1)S(1)} %get-tuple-element.21.gate_in, bf16[2,2048,512]{2,1,0:T(8,128)(2,1)S(1)} %get-tuple-element.22.up_in, bf16[1024,2048]{1,0:T(8,128)(2,1)S(1)} %get-tuple-element.23.down_in, ...), custom_call_target="tpu_custom_call" | custom-call | flops 3221225472 | bytes 14680064 | tf_op jit(solution)/shard_map/pallas_call | solution.py:139
  53.7 4.4 %shard_map.67 = (bf16[2,128,1024]{2,1,0:T(8,128)(2,1)S(1)}, bf16[2,128,1024]{2,1,0:T(8,128)(2,1)S(1)}) custom-call(s32[2]{0:T(128)S(1)} %pad_add_fusion.places, bf16[2,2048,512]{2,1,0:T(8,128)(2,1)S(1)} %get-tuple-element.21.gate_in, bf16[2,2048,512]{2,1,0:T(8,128)(2,1)S(1)} %get-tuple-element.22.up_in, bf16[1024,2048]{1,0:T(8,128)(2,1)S(1)} %get-tuple-element.23.down_in, ...), custom_call_target="tpu_custom_call" | custom-call | flops 3221225472 | bytes 14680064 | tf_op jit(solution)/shard_map/pallas_call | solution.py:139
  59.2 1.6 %collective-permute-start.16 = (bf16[64,1024]{1,0:T(8,128)(2,1)S(1)}, bf16[64,1024]{1,0:T(8,128)(2,1)S(1)}, u32[]{:S(2)}, u32[]{:S(2)}) collective-permute-start(bf16[64,1024]{1,0:T(8,128)(2,1)S(1)} %get-tuple-element.32), channel_id=1, source_target_pairs={{0,2},{1,3},{2,0},{3,1},{4,6},{5,7},{6,4},{7,5},{8,10},{9,11},{10,... | collective-permute-start | bytes 393224 | tf_op jit(solution)/shard_map/ppermute | solution.py:172
  63.4 1.5 %collective-permute-done.14 = bf16[64,1024]{1,0:T(8,128)(2,1)S(1)} collective-permute-done((bf16[64,1024]{1,0:T(8,128)(2,1)S(1)}, bf16[64,1024]{1,0:T(8,128)(2,1)S(1)}, u32[]{:S(2)}, u32[]{:S(2)}) %collective-permute-start.14) | collective-permute-done | bytes 131104 | tf_op jit(solution)/shard_map/ppermute | solution.py:172
  69.9 4.4 %collective-permute-done.15 = bf16[128,1024]{1,0:T(8,128)(2,1)S(1)} collective-permute-done((bf16[128,1024]{1,0:T(8,128)(2,1)S(1)}, bf16[128,1024]{1,0:T(8,128)(2,1)S(1)}, u32[]{:S(2)}, u32[]{:S(2)}) %collective-permute-start.15) | collective-permute-done | bytes 262176 | tf_op jit(solution)/shard_map/ppermute | solution.py:172
  74.3 1.5 %collective-permute-done.17 = bf16[128,1024]{1,0:T(8,128)(2,1)S(1)} collective-permute-done((bf16[128,1024]{1,0:T(8,128)(2,1)S(1)}, bf16[128,1024]{1,0:T(8,128)(2,1)S(1)}, u32[]{:S(2)}, u32[]{:S(2)}) %collective-permute-start.17) | collective-permute-done | bytes 262176 | tf_op jit(solution)/shard_map/ppermute | solution.py:172
  75.9 3.9 %collective-permute-start.18 = (bf16[32,1024]{1,0:T(8,128)(2,1)S(1)}, bf16[32,1024]{1,0:T(8,128)(2,1)S(1)}, u32[]{:S(2)}, u32[]{:S(2)}) collective-permute-start(bf16[32,1024]{1,0:T(8,128)(2,1)S(1)} %get-tuple-element.37), channel_id=1, source_target_pairs={{0,12},{1,13},{2,14},{3,15},{4,0},{5,1},{6,2},{7,3},{8,4},{9,5},{1... | collective-permute-start | bytes 196616 | tf_op jit(solution)/shard_map/ppermute | solution.py:172
  79.9 2.3 %collective-permute-start.19 = (bf16[32,1024]{1,0:T(8,128)(2,1)S(1)}, bf16[32,1024]{1,0:T(8,128)(2,1)S(1)}, u32[]{:S(2)}, u32[]{:S(2)}) collective-permute-start(bf16[32,1024]{1,0:T(8,128)(2,1)S(1)} %get-tuple-element.39), channel_id=1, source_target_pairs={{0,8},{1,9},{2,10},{3,11},{4,12},{5,13},{6,14},{7,15},{8,0},{9,1},... | collective-permute-start | bytes 196616 | tf_op jit(solution)/shard_map/ppermute | solution.py:172
  82.3 3.9 %collective-permute-start.39 = (bf16[32,1024]{1,0:T(8,128)(2,1)S(1)}, bf16[32,1024]{1,0:T(8,128)(2,1)S(1)}, u32[]{:S(2)}, u32[]{:S(2)}) collective-permute-start(bf16[32,1024]{1,0:T(8,128)(2,1)S(1)} %get-tuple-element.40), channel_id=1, source_target_pairs={{0,12},{1,13},{2,14},{3,15},{4,0},{5,1},{6,2},{7,3},{8,4},{9,5},{1... | collective-permute-start | bytes 196616 | tf_op jit(solution)/shard_map/ppermute | solution.py:172
  86.9 1.4 %collective-permute-done.20 = bf16[32,1024]{1,0:T(8,128)(2,1)S(1)} collective-permute-done((bf16[32,1024]{1,0:T(8,128)(2,1)S(1)}, bf16[32,1024]{1,0:T(8,128)(2,1)S(1)}, u32[]{:S(2)}, u32[]{:S(2)}) %collective-permute-start.20) | collective-permute-done | bytes 65568 | tf_op jit(solution)/shard_map/ppermute | solution.py:172
  88.3 4.2 %collective-permute-done.40 = bf16[32,1024]{1,0:T(8,128)(2,1)S(1)} collective-permute-done((bf16[32,1024]{1,0:T(8,128)(2,1)S(1)}, bf16[32,1024]{1,0:T(8,128)(2,1)S(1)}, u32[]{:S(2)}, u32[]{:S(2)}) %collective-permute-start.40) | collective-permute-done | bytes 65568 | tf_op jit(solution)/shard_map/ppermute | solution.py:172
  (107 shorter events, 21.9 us)
Async XLA Ops:
  2.4 8.0 %collective-permute-start = (bf16[32,1152]{1,0:T(8,128)(2,1)S(1)}, bf16[32,1152]{1,0:T(8,128)(2,1)S(1)}, u32[]{:S(2)}, u32[]{:S(2)}) collective-permute-start(bf16[32,1152]{1,0:T(8,128)(2,1)S(1)} %get-tuple-element.18), channel_id=1, source_target_pairs={{0,4},{1,5},{2,6},{3,7},{4,8},{5,9},{6,10},{7,11},{8,12},{9,13},{1... | collective-permute-start | bytes 221192 | tf_op jit(solution)/shard_map/ppermute | solution.py:172
  5.5 7.9 %collective-permute-start.1 = (bf16[32,1152]{1,0:T(8,128)(2,1)S(1)}, bf16[32,1152]{1,0:T(8,128)(2,1)S(1)}, u32[]{:S(2)}, u32[]{:S(2)}) collective-permute-start(bf16[32,1152]{1,0:T(8,128)(2,1)S(1)} %get-tuple-element.18), channel_id=1, source_target_pairs={{0,8},{1,9},{2,10},{3,11},{4,12},{5,13},{6,14},{7,15},{8,0},{9,1},... | collective-permute-start | bytes 221192 | tf_op jit(solution)/shard_map/ppermute | solution.py:172
  10.1 9.2 %collective-permute-start.22 = (bf16[32,1152]{1,0:T(8,128)(2,1)S(1)}, bf16[32,1152]{1,0:T(8,128)(2,1)S(1)}, u32[]{:S(2)}, u32[]{:S(2)}) collective-permute-start(bf16[32,1152]{1,0:T(8,128)(2,1)S(1)} %get-tuple-element.26), channel_id=1, source_target_pairs={{0,8},{1,9},{2,10},{3,11},{4,12},{5,13},{6,14},{7,15},{8,0},{9,1},... | collective-permute-start | bytes 221192 | tf_op jit(solution)/shard_map/ppermute | solution.py:172
  10.4 8.9 %collective-permute-start.23 = (bf16[32,1152]{1,0:T(8,128)(2,1)S(1)}, bf16[32,1152]{1,0:T(8,128)(2,1)S(1)}, u32[]{:S(2)}, u32[]{:S(2)}) collective-permute-start(bf16[32,1152]{1,0:T(8,128)(2,1)S(1)} %get-tuple-element.26), channel_id=1, source_target_pairs={{0,12},{1,13},{2,14},{3,15},{4,0},{5,1},{6,2},{7,3},{8,4},{9,5},{1... | collective-permute-start | bytes 221192 | tf_op jit(solution)/shard_map/ppermute | solution.py:172
  14.2 8.5 %collective-permute-start.4 = (bf16[128,1152]{1,0:T(8,128)(2,1)S(1)}, bf16[128,1152]{1,0:T(8,128)(2,1)S(1)}, u32[]{:S(2)}, u32[]{:S(2)}) collective-permute-start(bf16[128,1152]{1,0:T(8,128)(2,1)S(1)} %constant_dynamic-update-slice_fusion.refs_0_), channel_id=1, source_target_pairs={{0,16},{1,17},{2,18},{3,19},{4,20},{5,21},{6,22},{7,23},{8,24},{9,... | collective-permute-start | bytes 884744 | tf_op jit(solution)/shard_map/ppermute | solution.py:172
  15.2 8.8 %collective-permute-start.7 = (bf16[128,1152]{1,0:T(8,128)(2,1)S(1)}, bf16[128,1152]{1,0:T(8,128)(2,1)S(1)}, u32[]{:S(2)}, u32[]{:S(2)}) collective-permute-start(bf16[128,1152]{1,0:T(8,128)(2,1)S(1)} %constant_dynamic-update-slice_fusion.refs_0_), channel_id=1, source_target_pairs={{0,2},{1,3},{2,0},{3,1},{4,6},{5,7},{6,4},{7,5},{8,10},{9,11},{10,... | collective-permute-start | bytes 884744 | tf_op jit(solution)/shard_map/ppermute | solution.py:172
  19.4 10.0 %collective-permute-start.28 = (bf16[128,1152]{1,0:T(8,128)(2,1)S(1)}, bf16[128,1152]{1,0:T(8,128)(2,1)S(1)}, u32[]{:S(2)}, u32[]{:S(2)}) collective-permute-start(bf16[128,1152]{1,0:T(8,128)(2,1)S(1)} %constant_dynamic-update-slice_fusion.4.refs_0_), channel_id=1, source_target_pairs={{0,2},{1,3},{2,0},{3,1},{4,6},{5,7},{6,4},{7,5},{8,10},{9,11},{10,... | collective-permute-start | bytes 884744 | tf_op jit(solution)/shard_map/ppermute | solution.py:172
  21.1 9.8 %collective-permute-start.25 = (bf16[128,1152]{1,0:T(8,128)(2,1)S(1)}, bf16[128,1152]{1,0:T(8,128)(2,1)S(1)}, u32[]{:S(2)}, u32[]{:S(2)}) collective-permute-start(bf16[128,1152]{1,0:T(8,128)(2,1)S(1)} %constant_dynamic-update-slice_fusion.4.refs_0_), channel_id=1, source_target_pairs={{0,16},{1,17},{2,18},{3,19},{4,20},{5,21},{6,22},{7,23},{8,24},{9,... | collective-permute-start | bytes 884744 | tf_op jit(solution)/shard_map/ppermute | solution.py:172
  22.6 9.8 %collective-permute-start.3 = (bf16[128,1152]{1,0:T(8,128)(2,1)S(1)}, bf16[128,1152]{1,0:T(8,128)(2,1)S(1)}, u32[]{:S(2)}, u32[]{:S(2)}) collective-permute-start(bf16[128,1152]{1,0:T(8,128)(2,1)S(1)} %constant_dynamic-update-slice_fusion.refs_0_), channel_id=1, source_target_pairs={{0,1},{1,0},{2,3},{3,2},{4,5},{5,4},{6,7},{7,6},{8,9},{9,8},{10,11... | collective-permute-start | bytes 884744 | tf_op jit(solution)/shard_map/ppermute | solution.py:172
  22.6 13.2 %collective-permute-start.5 = (bf16[128,1152]{1,0:T(8,128)(2,1)S(1)}, bf16[128,1152]{1,0:T(8,128)(2,1)S(1)}, u32[]{:S(2)}, u32[]{:S(2)}) collective-permute-start(bf16[128,1152]{1,0:T(8,128)(2,1)S(1)} %collective-permute-done.4.refs_2_), channel_id=1, source_target_pairs={{0,1},{1,0},{2,3},{3,2},{4,5},{5,4},{6,7},{7,6},{8,9},{9,8},{10,11... | collective-permute-start | bytes 884744 | tf_op jit(solution)/shard_map/ppermute | solution.py:172
  24.0 9.0 %collective-permute-start.9 = (bf16[64,1152]{1,0:T(8,128)(2,1)S(1)}, bf16[64,1152]{1,0:T(8,128)(2,1)S(1)}, u32[]{:S(2)}, u32[]{:S(2)}) collective-permute-start(bf16[64,1152]{1,0:T(8,128)(2,1)S(1)} %slice.105), channel_id=1, source_target_pairs={{0,16},{1,17},{2,18},{3,19},{4,20},{5,21},{6,22},{7,23},{8,24},{9,... | collective-permute-start | bytes 442376 | tf_op jit(solution)/shard_map/ppermute | solution.py:172
  30.9 12.0 %collective-permute-start.30 = (bf16[64,1152]{1,0:T(8,128)(2,1)S(1)}, bf16[64,1152]{1,0:T(8,128)(2,1)S(1)}, u32[]{:S(2)}, u32[]{:S(2)}) collective-permute-start(bf16[64,1152]{1,0:T(8,128)(2,1)S(1)} %slice.118), channel_id=1, source_target_pairs={{0,16},{1,17},{2,18},{3,19},{4,20},{5,21},{6,22},{7,23},{8,24},{9,... | collective-permute-start | bytes 442376 | tf_op jit(solution)/shard_map/ppermute | solution.py:172
  32.4 10.6 %collective-permute-start.31 = (bf16[64,1152]{1,0:T(8,128)(2,1)S(1)}, bf16[64,1152]{1,0:T(8,128)(2,1)S(1)}, u32[]{:S(2)}, u32[]{:S(2)}) collective-permute-start(bf16[64,1152]{1,0:T(8,128)(2,1)S(1)} %slice.119), channel_id=1, source_target_pairs={{0,2},{1,3},{2,0},{3,1},{4,6},{5,7},{6,4},{7,5},{8,10},{9,11},{10,... | collective-permute-start | bytes 442376 | tf_op jit(solution)/shard_map/ppermute | solution.py:172
  33.0 10.5 %collective-permute-start.8 = (bf16[128,1152]{1,0:T(8,128)(2,1)S(1)}, bf16[128,1152]{1,0:T(8,128)(2,1)S(1)}, u32[]{:S(2)}, u32[]{:S(2)}) collective-permute-start(bf16[128,1152]{1,0:T(8,128)(2,1)S(1)} %collective-permute-done.7.refs_0_), channel_id=1, source_target_pairs={{0,1},{1,0},{2,3},{3,2},{4,5},{5,4},{6,7},{7,6},{8,9},{9,8},{10,11... | collective-permute-start | bytes 884744 | tf_op jit(solution)/shard_map/ppermute | solution.py:172
  35.8 8.2 %collective-permute-start.12 = (bf16[64,1152]{1,0:T(8,128)(2,1)S(1)}, bf16[64,1152]{1,0:T(8,128)(2,1)S(1)}, u32[]{:S(2)}, u32[]{:S(2)}) collective-permute-start(bf16[64,1152]{1,0:T(8,128)(2,1)S(1)} %collective-permute-done.10.refs_3_), channel_id=1, source_target_pairs={{0,1},{1,0},{2,3},{3,2},{4,5},{5,4},{6,7},{7,6},{8,9},{9,8},{10,11... | collective-permute-start | bytes 442376 | tf_op jit(solution)/shard_map/ppermute | solution.py:172
  42.9 10.8 %collective-permute-start.24 = (bf16[128,1152]{1,0:T(8,128)(2,1)S(1)}, bf16[128,1152]{1,0:T(8,128)(2,1)S(1)}, u32[]{:S(2)}, u32[]{:S(2)}) collective-permute-start(bf16[128,1152]{1,0:T(8,128)(2,1)S(1)} %constant_dynamic-update-slice_fusion.4.refs_0_), channel_id=1, source_target_pairs={{0,1},{1,0},{2,3},{3,2},{4,5},{5,4},{6,7},{7,6},{8,9},{9,8},{10,11... | collective-permute-start | bytes 884744 | tf_op jit(solution)/shard_map/ppermute | solution.py:172
  43.5 10.2 %collective-permute-start.26 = (bf16[128,1152]{1,0:T(8,128)(2,1)S(1)}, bf16[128,1152]{1,0:T(8,128)(2,1)S(1)}, u32[]{:S(2)}, u32[]{:S(2)}) collective-permute-start(bf16[128,1152]{1,0:T(8,128)(2,1)S(1)} %collective-permute-done.25.refs_2_), channel_id=1, source_target_pairs={{0,1},{1,0},{2,3},{3,2},{4,5},{5,4},{6,7},{7,6},{8,9},{9,8},{10,11... | collective-permute-start | bytes 884744 | tf_op jit(solution)/shard_map/ppermute | solution.py:172
  48.4 13.9 %collective-permute-start.6 = (bf16[2,128,1024]{2,1,0:T(8,128)(2,1)S(1)}, bf16[2,128,1024]{2,1,0:T(8,128)(2,1)S(1)}, u32[]{:S(2)}, u32[]{:S(2)}) collective-permute-start(bf16[2,128,1024]{2,1,0:T(8,128)(2,1)S(1)} %get-tuple-element.20), channel_id=1, source_target_pairs={{0,1},{1,0},{2,3},{3,2},{4,5},{5,4},{6,7},{7,6},{8,9},{9,8},{10,11... | collective-permute-start | bytes 1572872 | tf_op jit(solution)/shard_map/ppermute | solution.py:172
  48.9 9.4 %collective-permute-start.13 = (bf16[2,128,1024]{2,1,0:T(8,128)(2,1)S(1)}, bf16[2,128,1024]{2,1,0:T(8,128)(2,1)S(1)}, u32[]{:S(2)}, u32[]{:S(2)}) collective-permute-start(bf16[2,128,1024]{2,1,0:T(8,128)(2,1)S(1)} %get-tuple-element.25), channel_id=1, source_target_pairs={{0,1},{1,0},{2,3},{3,2},{4,5},{5,4},{6,7},{7,6},{8,9},{9,8},{10,11... | collective-permute-start | bytes 1572872 | tf_op jit(solution)/shard_map/ppermute | solution.py:172
  65.0 9.3 %collective-permute-start.15 = (bf16[128,1024]{1,0:T(8,128)(2,1)S(1)}, bf16[128,1024]{1,0:T(8,128)(2,1)S(1)}, u32[]{:S(2)}, u32[]{:S(2)}) collective-permute-start(bf16[128,1024]{1,0:T(8,128)(2,1)S(1)} %pad_maximum_fusion), channel_id=1, source_target_pairs={{0,2},{1,3},{2,0},{3,1},{4,6},{5,7},{6,4},{7,5},{8,10},{9,11},{10,... | collective-permute-start | bytes 786440 | tf_op jit(solution)/shard_map/ppermute | solution.py:172
  66.5 9.3 %collective-permute-start.17 = (bf16[128,1024]{1,0:T(8,128)(2,1)S(1)}, bf16[128,1024]{1,0:T(8,128)(2,1)S(1)}, u32[]{:S(2)}, u32[]{:S(2)}) collective-permute-start(bf16[128,1024]{1,0:T(8,128)(2,1)S(1)} %pad_maximum_fusion.1), channel_id=1, source_target_pairs={{0,16},{1,17},{2,18},{3,19},{4,20},{5,21},{6,22},{7,23},{8,24},{9,... | collective-permute-start | bytes 786440 | tf_op jit(solution)/shard_map/ppermute | solution.py:172
  67.5 14.7 %collective-permute-start.36 = (bf16[128,1024]{1,0:T(8,128)(2,1)S(1)}, bf16[128,1024]{1,0:T(8,128)(2,1)S(1)}, u32[]{:S(2)}, u32[]{:S(2)}) collective-permute-start(bf16[128,1024]{1,0:T(8,128)(2,1)S(1)} %pad_maximum_fusion.2), channel_id=1, source_target_pairs={{0,2},{1,3},{2,0},{3,1},{4,6},{5,7},{6,4},{7,5},{8,10},{9,11},{10,... | collective-permute-start | bytes 786440 | tf_op jit(solution)/shard_map/ppermute | solution.py:172
  68.7 13.5 %collective-permute-start.38 = (bf16[128,1024]{1,0:T(8,128)(2,1)S(1)}, bf16[128,1024]{1,0:T(8,128)(2,1)S(1)}, u32[]{:S(2)}, u32[]{:S(2)}) collective-permute-start(bf16[128,1024]{1,0:T(8,128)(2,1)S(1)} %pad_maximum_fusion.3), channel_id=1, source_target_pairs={{0,16},{1,17},{2,18},{3,19},{4,20},{5,21},{6,22},{7,23},{8,24},{9,... | collective-permute-start | bytes 786440 | tf_op jit(solution)/shard_map/ppermute | solution.py:172
  75.9 10.3 %collective-permute-start.18 = (bf16[32,1024]{1,0:T(8,128)(2,1)S(1)}, bf16[32,1024]{1,0:T(8,128)(2,1)S(1)}, u32[]{:S(2)}, u32[]{:S(2)}) collective-permute-start(bf16[32,1024]{1,0:T(8,128)(2,1)S(1)} %get-tuple-element.37), channel_id=1, source_target_pairs={{0,12},{1,13},{2,14},{3,15},{4,0},{5,1},{6,2},{7,3},{8,4},{9,5},{1... | collective-permute-start | bytes 196616 | tf_op jit(solution)/shard_map/ppermute | solution.py:172
  (21 other events, 116.3 us)

commit v3 on v2

v3 whole, which is shorter than its diff:
```python
import functools

import jax
import jax.numpy as jnp
from jax import lax
from jax.experimental import pallas as pl
from jax.experimental.pallas import tpu as pltpu
from jax.sharding import PartitionSpec as P

BF16, F32 = jnp.bfloat16, jnp.float32
PAIR = ("dp", "expert")
LANES = 128
MIB = 1024 * 1024
VMEM_SPEC = pl.BlockSpec(memory_space=pltpu.VMEM)


def near(array):
    return pltpu.with_memory_space_constraint(array, pltpu.VMEM)


def route_table(ids, weights, experts):
    lane = lax.broadcasted_iota(jnp.int32, (ids.shape[0], experts), 1)
    table = jnp.zeros((ids.shape[0], experts), F32)
    for k in range(ids.shape[1]):
        table = table + jnp.where(ids[:, k : k + 1] == lane, weights[:, k : k + 1].astype(F32), 0.0)
    return table


def pack_kernel(tok_hbm, ids_hbm, rw_hbm, out_ref, ids_ref, rw_ref, sem):
    rows, width = tok_hbm.shape
    columns = out_ref.shape[1] - width
    ends = (ids_hbm, ids_ref), (rw_hbm, rw_ref), (tok_hbm, out_ref.at[:, pl.ds(0, width)])
    copies = [pltpu.make_async_copy(*pair, sem.at[i]) for i, pair in enumerate(ends)]
    for copy in copies:
        copy.start()
    for copy in copies[:2]:
        copy.wait()
    line = lax.broadcasted_iota(jnp.int32, (columns, rows), 0)
    table = jnp.zeros((columns, rows), F32)
    for k in range(ids_ref.shape[0]):
        table = table + jnp.where(ids_ref[k : k + 1, :] == line, rw_ref[k : k + 1, :].astype(F32), 0.0)
    out_ref[:, width:] = table.T.astype(BF16)
    copies[2].wait()


def pack(tokens, ids, route_weights, columns):
    rows, width = tokens.shape
    operands = [pltpu.with_memory_space_constraint(x, pltpu.HBM) for x in (tokens, ids.T, route_weights.T)]
    return pl.pallas_call(
        pack_kernel,
        in_specs=[pl.BlockSpec(memory_space=pl.ANY)] * 3,
        out_specs=VMEM_SPEC,
        out_shape=jax.ShapeDtypeStruct((rows, width + columns), BF16),
        scratch_shapes=[
            pltpu.VMEM(operands[1].shape, jnp.int32),
            pltpu.VMEM(operands[2].shape, BF16),
            pltpu.SemaphoreType.DMA((3,)),
        ],
        compiler_params=pltpu.CompilerParams(vmem_limit_bytes=2 * MIB),
    )(*operands)


def dispatch(table, expert_place, experts, block, room):
    rows = table.shape[0]
    this = lax.broadcasted_iota(jnp.int32, (rows, rows), 0)
    other = lax.broadcasted_iota(jnp.int32, (rows, rows), 1)
    before = (other < this) & (other // block == this // block)
    ranks = jnp.dot(before.astype(BF16), (table > 0.0).astype(BF16), preferred_element_type=F32)
    lane = lax.broadcasted_iota(jnp.int32, table.shape, 1)
    slots = experts * rows // block * room
    slot = lax.broadcasted_iota(jnp.int32, (rows, slots), 1)
    first = lax.broadcasted_iota(jnp.int32, (rows, 1), 0) // block * room
    taken = jnp.zeros((rows, slots), F32)
    for e in range(experts):
        here = lane == expert_place * experts + e
        weight = jnp.sum(jnp.where(here, table, 0.0), axis=1, keepdims=True)
        rank = jnp.sum(jnp.where(here, ranks, 0.0), axis=1, keepdims=True).astype(jnp.int32)
        taken = taken + jnp.where(slot == first + rank + e * (slots // experts), weight, 0.0)
    return taken


def experts_kernel(first, counts, block, room, places, gate_in, up_in, down_in, *refs):
    if first:
        pieces, refs = refs[:-13], refs[-13:]
        corner_keep, corner_give, keep_ref, give_ref, gate_ref, up_ref, down_ref, *refs, sem = refs
    else:
        pieces, refs = refs[:-9], refs[-9:]
        corner_keep, corner_give, keep_ref, give_ref, *refs = refs
        gate_ref, up_ref, down_ref = gate_in, up_in, down_in
    rows_buf, table_buf, taken_buf, packed_buf, out_buf = refs
    experts, model, hidden = gate_ref.shape
    width = model // 2
    fetches = []
    if first:
        ends = []
        for e in range(experts):
            span = pl.ds(e * hidden, hidden)
            ends += [(gate_in.at[e], gate_ref.at[e]), (up_in.at[e], up_ref.at[e])]
            ends += [(down_in.at[span], down_ref.at[span])]
        fetches = [pltpu.make_async_copy(*pair, sem.at[i]) for i, pair in enumerate(ends)]
        for copy in fetches:
            copy.start()

    mine = pl.ds(pl.multiple_of(places[0] * width, width), width)
    others = pl.ds(pl.multiple_of((1 - places[0]) * width, width), width)
    group = rows_buf.shape[0] // 2
    slots = taken_buf.shape[2] // experts
    taken = 0
    for g in range(2):
        for count, columns in zip(counts[g], (mine, others)):
            row = g * group
            for piece in pieces[taken : taken + count]:
                span = pl.ds(row, piece.shape[0])
                rows_buf[span, columns] = piece[:, :width]
                if columns is mine:
                    table_buf[span, :] = piece[:, width:].astype(F32)
                row += piece.shape[0]
            taken += count
        table = dispatch(table_buf[pl.ds(g * group, group), :], places[1], experts, block, room)
        taken_buf[g] = table.astype(BF16)
        picked = jnp.where(table > 0.0, 1.0, 0.0).T.astype(BF16)
        packed = jnp.dot(picked, rows_buf[pl.ds(g * group, group), :], preferred_element_type=F32).astype(BF16)
        for e in range(experts):
            packed_buf[e, pl.ds(g * slots, slots), :] = packed[e * slots : (e + 1) * slots]

    for e in range(experts):
        for copy in fetches[3 * e : 3 * e + 3]:
            copy.wait()
        rows = packed_buf[e]
        gate = jnp.dot(rows, gate_ref[e], preferred_element_type=F32)
        up = jnp.dot(rows, up_ref[e], preferred_element_type=F32)
        value = (gate / (1.0 + jnp.exp(-gate)) * up).astype(BF16)
        down = down_ref[pl.ds(e * hidden, hidden), :]
        out = jnp.dot(value, down, preferred_element_type=F32).astype(BF16)
        for g in range(2):
            out_buf[g, pl.ds(e * slots, slots), :] = out[g * slots : (g + 1) * slots]
    half = group // 2
    for g in (1, 0):
        for side, columns in enumerate((mine, others)):
            out = jnp.dot(taken_buf[g], out_buf[g, :, columns], preferred_element_type=F32).astype(BF16)
            if g and side:
                corner_keep[...] = out[:half]
                corner_give[...] = out[half:]
            else:
                keep_ref[g + 2 * side] = out[:half]
                give_ref[g + 2 * side] = out[half:]


def run_experts(places, weights, groups, block, room, first):
    experts, model, hidden = weights[0].shape
    width = model // 2
    rows = 2 * sum(piece.shape[0] for piece in groups[0][0])
    table = groups[0][0][0].shape[1] - width
    where = pltpu.HBM if first else pltpu.VMEM
    operands = [pltpu.with_memory_space_constraint(w, where) for w in weights]
    operands += [near(piece) for pair in groups for half in pair for piece in half]
    outs = [jax.ShapeDtypeStruct((rows // 4, width), BF16)] * 2
    outs += [jax.ShapeDtypeStruct((3, rows // 4, width), BF16)] * 2
    extra = []
    if first:
        outs += [jax.ShapeDtypeStruct(w.shape, BF16) for w in weights]
        extra = [pltpu.SemaphoreType.DMA((3 * experts,))]
    slots = rows // 2 // block * room
    counts = tuple(tuple(len(half) for half in pair) for pair in groups)
    return pl.pallas_call(
        functools.partial(experts_kernel, first, counts, block, room),
        in_specs=[pl.BlockSpec(memory_space=pltpu.SMEM)]
        + [pl.BlockSpec(memory_space=pl.ANY if first else pltpu.VMEM)] * 3
        + [VMEM_SPEC] * (len(operands) - 3),
        out_specs=[VMEM_SPEC] * len(outs),
        scratch_shapes=[
            pltpu.VMEM((rows, model), BF16),
            pltpu.VMEM((rows, table), F32),
            pltpu.VMEM((2, rows // 2, experts * slots), BF16),
            pltpu.VMEM((experts, 2 * slots, model), BF16),
            pltpu.VMEM((2, experts * slots, model), BF16),
        ]
        + extra,
        out_shape=outs,
        compiler_params=pltpu.CompilerParams(vmem_limit_bytes=20 * MIB),
        cost_estimate=pl.CostEstimate(flops=rows, bytes_accessed=rows, transcendentals=0),
    )(places, *operands)


def add(*terms):
    return functools.reduce(lambda a, b: a + b, [t.astype(F32) for t in terms]).astype(BF16)


def after(arrays, others):
    return lax.optimization_barrier((arrays, others))[0]


def planned(peers, tokens, expert_ids, route_weights, w_gate, w_up, w_down):
    line = peers // 4

    def send(array, steps=0, x=0, core=0, y=0):
        pairs = []
        for side in range(2):
            for e in range(peers):
                to = ((e // 4) ^ steps) * 4 + ((e // 2 % 2) ^ x) * 2 + ((e % 2) ^ core)
                pairs.append((side * peers + e, (side ^ y) * peers + to))
        return lax.ppermute(array, PAIR, pairs)

    expert_count = peers * w_gate.shape[0]
    columns = -(-expert_count // LANES) * LANES
    places = jnp.stack([lax.axis_index("dp"), lax.axis_index("expert")]).astype(jnp.int32)
    rows = pack(tokens, expert_ids, route_weights, columns)

    def join(pieces):
        return jnp.concatenate(pieces, 0)

    def cores(pieces):
        return [send(piece, core=1) for piece in pieces]

    def gather(own):
        half = own.shape[0] // 2
        by_x, by_y = send(own, x=1), send(own, y=1)
        corner = [send(by_x[:half], y=1), send(by_y[half:], x=1)]
        return [[own] + cores([own]), [by_y] + cores([by_y])], [[by_x] + cores([by_x]), corner + cores(corner)]

    def total(keep, give):
        return add(keep, send(give, core=1))

    def turn(corner, rest):
        for_x, for_y = rest[1], rest[2]
        half = for_x.shape[0] // 2
        got_a, got_b = send(corner[:half], x=1), send(corner[half:], y=1)
        for_x = join([for_x[:half], add(for_x[half:], got_b)])
        for_y = join([add(for_y[:half], got_a), for_y[half:]])
        return for_x, for_y

    weights = (w_gate, w_up, w_down.reshape(-1, w_down.shape[2]))
    block = tokens.shape[0]
    room = block * expert_ids.shape[1] * 3 // (2 * expert_count)
    blocks = [rows] + [send(rows, steps=k) for k in range(1, line)]
    parts, first, sums = 2, True, []
    count = line // parts
    for i in range(parts):
        groups = gather(join(blocks[i * count : (i + 1) * count]))
        corner, corner_give, keep, give, *rest = run_experts(places, weights, groups, block, room, first)
        if first:
            weights, first = rest, False
        rest = total(keep, give)
        sums.append((rest[0], *turn(total(corner, corner_give), rest)))
    back, arrived = [], ()
    for i in reversed(range(parts)):
        own, for_x, for_y = sums[i]
        for_x, for_y = after((for_x, for_y), arrived)
        arrived = send(for_x, x=1), send(for_y, y=1)
        mine = add(own, *arrived)
        for k in range(count):
            piece = mine[k * block : (k + 1) * block]
            back.append(send(piece, steps=i * count + k) if i or k else piece)
    return add(*back)


def general(tokens, expert_ids, route_weights, w_gate, w_up, w_down):
    peers, local = lax.axis_size("expert"), w_gate.shape[0]
    table = route_table(expert_ids, route_weights, peers * local).astype(BF16)
    rows = lax.all_gather(tokens, "expert", axis=0, tiled=True)
    rows = lax.all_gather(rows, "dp", axis=1, tiled=True)
    table = lax.all_gather(table, "expert", axis=0, tiled=True).astype(F32)
    weight = lax.dynamic_slice_in_dim(table, lax.axis_index("expert") * local, local, 1)
    gate = jnp.einsum("td,rdf->trf", rows, w_gate, preferred_element_type=F32)
    up = jnp.einsum("td,rdf->trf", rows, w_up, preferred_element_type=F32)
    hidden = (jax.nn.silu(gate) * up * weight[:, :, None]).astype(BF16)
    out = jnp.einsum("trf,rfd->td", hidden, w_down, preferred_element_type=F32).astype(BF16)
    out = lax.psum_scatter(out, "dp", scatter_dimension=1, tiled=True)
    return lax.psum_scatter(out, "expert", scatter_dimension=0, tiled=True)


def solution(mesh):
    peers = mesh.shape["expert"]
    body = general
    if mesh.shape["dp"] == 2 and peers % 8 == 0 and peers & (peers - 1) == 0:
        body = functools.partial(planned, peers)
    return jax.shard_map(
        body,
        mesh=mesh,
        in_specs=(
            P("expert", "dp"),
            P("expert", None),
            P("expert", None),
            P("expert", None, "dp"),
            P("expert", None, "dp"),
            P("expert", "dp", None),
        ),
        out_specs=P("expert", "dp"),
        check_vma=False,
    )
```

time: 93.5 us -> 85.3 us (0.912)
  starting transfers between devices: 43.5 us -> 33.8 us
  waiting for transfers between devices: 25.3 us -> 34.2 us
  Pallas kernels: 19.6 us -> 14.7 us
  local copies, waits for them, and re-layouts: 2.52 us -> 0.19 us
    ppermute x42 -> x36, starting transfers between devices: 43.5 us -> 33.8 us  [send(): return lax.ppermute(array, PAIR, pairs)]
    ppermute x42 -> x36, waiting for transfers between devices: 25.3 us -> 34.2 us  [send(): return lax.ppermute(array, PAIR, pairs)]
    pallas_call x5 -> x3, Pallas kernels: 19.6 us -> 14.7 us  [the longest x2 13.7 us: run_experts(): pl.pallas_call(functools.partial(experts_kernel, first, counts, block, ro...]
    unnamed x12 -> x1, local copies, waits for them, and re-layouts: 2.34 us -> 0.01 us
  transfers between devices with their start and end apart: 42 -> 36, of which waited for: 10 -> 16; matrix products, arithmetic and copies ran while one was open for 2% -> 2% of each run, Pallas kernels for 21% -> 16%
where the time goes in v3:
time: 85.3 us; the launch traced here: 85.2 us
  waiting for transfers between devices  34.2 us (40%)
  starting transfers between devices  33.8 us (40%)
  Pallas kernels  14.7 us (17%)
  other arithmetic  2.02 us (2%)
    ppermute x36, waiting for transfers between devices, send(): return lax.ppermute(array, PAIR, pairs)  34.2 us
    ppermute x36, starting transfers between devices, send(): return lax.ppermute(array, PAIR, pairs)  33.8 us
    pallas_call x2, Pallas kernels, run_experts(): pl.pallas_call(functools.partial(experts_kernel, first, counts, block, ro...  13.7 us
    convert_element_type x9, other arithmetic, add(): functools.reduce(lambda a, b: a + b, [t.astype(F32) for t in terms])  1.85 us
  transfers between devices with their start and end apart: 36, of which 16 were waited for; matrix products, arithmetic and copies ran while one was open for 2% of the time, Pallas kernels for 16%

profile of v3, /device:TPU:0, one launch (start us, length us, event | category | flops | bytes accessed | tf_op | source)
XLA Modules:
  0.0 85.2 jit_solution(31778140614403799)
XLA Ops:
  1.0 3.1 %collective-permute-start = (bf16[64,1152]{1,0:T(8,128)(2,1)S(1)}, bf16[64,1152]{1,0:T(8,128)(2,1)S(1)}, u32[]{:S(2)}, u32[]{:S(2)}) collective-permute-start(bf16[64,1152]{1,0:T(8,128)(2,1)S(1)} %shard_map.64), channel_id=1, source_target_pairs={{0,4},{1,5},{2,6},{3,7},{4,0},{5,1},{6,2},{7,3},{8,12},{9,13},{10,... | collective-permute-start | bytes 442376 | tf_op jit(solution)/shard_map/ppermute | solution.py:202
  4.1 2.6 %collective-permute-start.10 = (bf16[64,1152]{1,0:T(8,128)(2,1)S(1)}, bf16[64,1152]{1,0:T(8,128)(2,1)S(1)}, u32[]{:S(2)}, u32[]{:S(2)}) collective-permute-start(bf16[64,1152]{1,0:T(8,128)(2,1)S(1)} %shard_map.64), channel_id=1, source_target_pairs={{0,8},{1,9},{2,10},{3,11},{4,12},{5,13},{6,14},{7,15},{8,0},{9,1},... | collective-permute-start | bytes 442376 | tf_op jit(solution)/shard_map/ppermute | solution.py:202
  6.7 3.3 %collective-permute-done = bf16[64,1152]{1,0:T(8,128)(2,1)S(1)} collective-permute-done((bf16[64,1152]{1,0:T(8,128)(2,1)S(1)}, bf16[64,1152]{1,0:T(8,128)(2,1)S(1)}, u32[]{:S(2)}, u32[]{:S(2)}) %collective-permute-start) | collective-permute-done | bytes 147488 | tf_op jit(solution)/shard_map/ppermute | solution.py:202
  10.0 1.8 %collective-permute-start.2 = (bf16[128,1152]{1,0:T(8,128)(2,1)S(1)}, bf16[128,1152]{1,0:T(8,128)(2,1)S(1)}, u32[]{:S(2)}, u32[]{:S(2)}) collective-permute-start(bf16[128,1152]{1,0:T(8,128)(2,1)S(1)} %pad_maximum_fusion.refs_0_), channel_id=1, source_target_pairs={{0,16},{1,17},{2,18},{3,19},{4,20},{5,21},{6,22},{7,23},{8,24},{9,... | collective-permute-start | bytes 884744 | tf_op jit(solution)/shard_map/ppermute | solution.py:202
  11.8 1.5 %collective-permute-start.4 = (bf16[128,1152]{1,0:T(8,128)(2,1)S(1)}, bf16[128,1152]{1,0:T(8,128)(2,1)S(1)}, u32[]{:S(2)}, u32[]{:S(2)}) collective-permute-start(bf16[128,1152]{1,0:T(8,128)(2,1)S(1)} %pad_maximum_fusion.refs_0_), channel_id=1, source_target_pairs={{0,2},{1,3},{2,0},{3,1},{4,6},{5,7},{6,4},{7,5},{8,10},{9,11},{10,... | collective-permute-start | bytes 884744 | tf_op jit(solution)/shard_map/ppermute | solution.py:202
  13.3 4.7 %collective-permute-done.10 = bf16[64,1152]{1,0:T(8,128)(2,1)S(1)} collective-permute-done((bf16[64,1152]{1,0:T(8,128)(2,1)S(1)}, bf16[64,1152]{1,0:T(8,128)(2,1)S(1)}, u32[]{:S(2)}, u32[]{:S(2)}) %collective-permute-start.10) | collective-permute-done | bytes 147488 | tf_op jit(solution)/shard_map/ppermute | solution.py:202
  18.1 1.6 %collective-permute-start.13 = (bf16[128,1152]{1,0:T(8,128)(2,1)S(1)}, bf16[128,1152]{1,0:T(8,128)(2,1)S(1)}, u32[]{:S(2)}, u32[]{:S(2)}) collective-permute-start(bf16[128,1152]{1,0:T(8,128)(2,1)S(1)} %constant_dynamic-update-slice_fusion.refs_0_), channel_id=1, source_target_pairs={{0,16},{1,17},{2,18},{3,19},{4,20},{5,21},{6,22},{7,23},{8,24},{9,... | collective-permute-start | bytes 884744 | tf_op jit(solution)/shard_map/ppermute | solution.py:202
  19.7 1.5 %collective-permute-start.15 = (bf16[128,1152]{1,0:T(8,128)(2,1)S(1)}, bf16[128,1152]{1,0:T(8,128)(2,1)S(1)}, u32[]{:S(2)}, u32[]{:S(2)}) collective-permute-start(bf16[128,1152]{1,0:T(8,128)(2,1)S(1)} %constant_dynamic-update-slice_fusion.refs_0_), channel_id=1, source_target_pairs={{0,2},{1,3},{2,0},{3,1},{4,6},{5,7},{6,4},{7,5},{8,10},{9,11},{10,... | collective-permute-start | bytes 884744 | tf_op jit(solution)/shard_map/ppermute | solution.py:202
  22.3 4.3 %collective-permute-done.13.refs_2_ = bf16[128,1152]{1,0:T(8,128)(2,1)S(1)} collective-permute-done((bf16[128,1152]{1,0:T(8,128)(2,1)S(1)}, bf16[128,1152]{1,0:T(8,128)(2,1)S(1)}, u32[]{:S(2)}, u32[]{:S(2)}) %collective-permute-start.13) | collective-permute-done | bytes 294944 | tf_op jit(solution)/shard_map/ppermute | solution.py:202
  26.6 1.9 %collective-permute-start.7 = (bf16[64,1152]{1,0:T(8,128)(2,1)S(1)}, bf16[64,1152]{1,0:T(8,128)(2,1)S(1)}, u32[]{:S(2)}, u32[]{:S(2)}) collective-permute-start(bf16[64,1152]{1,0:T(8,128)(2,1)S(1)} %slice.121), channel_id=1, source_target_pairs={{0,2},{1,3},{2,0},{3,1},{4,6},{5,7},{6,4},{7,5},{8,10},{9,11},{10,... | collective-permute-start | bytes 442376 | tf_op jit(solution)/shard_map/ppermute | solution.py:202
  29.0 2.7 %collective-permute-done.7.refs_7_ = bf16[64,1152]{1,0:T(8,128)(2,1)S(1)} collective-permute-done((bf16[64,1152]{1,0:T(8,128)(2,1)S(1)}, bf16[64,1152]{1,0:T(8,128)(2,1)S(1)}, u32[]{:S(2)}, u32[]{:S(2)}) %collective-permute-start.7) | collective-permute-done | bytes 147488 | tf_op jit(solution)/shard_map/ppermute | solution.py:202
  31.8 2.5 %collective-permute-start.17 = (bf16[64,1152]{1,0:T(8,128)(2,1)S(1)}, bf16[64,1152]{1,0:T(8,128)(2,1)S(1)}, u32[]{:S(2)}, u32[]{:S(2)}) collective-permute-start(bf16[64,1152]{1,0:T(8,128)(2,1)S(1)} %slice.122), channel_id=1, source_target_pairs={{0,16},{1,17},{2,18},{3,19},{4,20},{5,21},{6,22},{7,23},{8,24},{9,... | collective-permute-start | bytes 442376 | tf_op jit(solution)/shard_map/ppermute | solution.py:202
  34.3 1.5 %collective-permute-start.18 = (bf16[64,1152]{1,0:T(8,128)(2,1)S(1)}, bf16[64,1152]{1,0:T(8,128)(2,1)S(1)}, u32[]{:S(2)}, u32[]{:S(2)}) collective-permute-start(bf16[64,1152]{1,0:T(8,128)(2,1)S(1)} %slice.123), channel_id=1, source_target_pairs={{0,2},{1,3},{2,0},{3,1},{4,6},{5,7},{6,4},{7,5},{8,10},{9,11},{10,... | collective-permute-start | bytes 442376 | tf_op jit(solution)/shard_map/ppermute | solution.py:202
  36.4 8.4 %shard_map.65 = (bf16[128,1024]{1,0:T(8,128)(2,1)S(1)}, bf16[128,1024]{1,0:T(8,128)(2,1)S(1)}, bf16[3,128,1024]{2,1,0:T(8,128)(2,1)S(1)}, bf16[3,128,1024]{2,1,0...) custom-call(s32[2]{0:T(128)S(1)} %pad_add_fusion.places, ...), custom_call_target="tpu_custom_call" | custom-call | flops 512 | bytes 512 | tf_op jit(solution)/shard_map/pallas_call | solution.py:165
  46.9 5.3 %shard_map.66 = (bf16[128,1024]{1,0:T(8,128)(2,1)S(1)}, bf16[128,1024]{1,0:T(8,128)(2,1)S(1)}, bf16[3,128,1024]{2,1,0:T(8,128)(2,1)S(1)}, bf16[3,128,1024]{2,1,0:T(8,128)(2,1)S(1)}) custom-call(s32[2]{0:T(128)S(1)} %pad_add_fusion.places, bf16[2,2048,512]{2,1,0:T(8,128)(2,1)S(1)} %get-tuple-element.20.gate_in, ...), custom_call_target="tpu_custom_call" | custom-call | flops 512 | bytes 512 | tf_op jit(solution)/shard_map/pallas_call | solution.py:165
  54.0 1.3 %collective-permute-start.24 = (bf16[64,1024]{1,0:T(8,128)(2,1)S(1)}, bf16[64,1024]{1,0:T(8,128)(2,1)S(1)}, u32[]{:S(2)}, u32[]{:S(2)}) collective-permute-start(bf16[64,1024]{1,0:T(8,128)(2,1)S(1)} %get-tuple-element.45), channel_id=1, source_target_pairs={{0,2},{1,3},{2,0},{3,1},{4,6},{5,7},{6,4},{7,5},{8,10},{9,11},{10,... | collective-permute-start | bytes 393224 | tf_op jit(solution)/shard_map/ppermute | solution.py:202
  55.2 1.9 %collective-permute-start.23 = (bf16[64,1024]{1,0:T(8,128)(2,1)S(1)}, bf16[64,1024]{1,0:T(8,128)(2,1)S(1)}, u32[]{:S(2)}, u32[]{:S(2)}) collective-permute-start(bf16[64,1024]{1,0:T(8,128)(2,1)S(1)} %get-tuple-element.46), channel_id=1, source_target_pairs={{0,16},{1,17},{2,18},{3,19},{4,20},{5,21},{6,22},{7,23},{8,24},{9,... | collective-permute-start | bytes 393224 | tf_op jit(solution)/shard_map/ppermute | solution.py:202
  57.5 3.8 %collective-permute-done.24 = bf16[64,1024]{1,0:T(8,128)(2,1)S(1)} collective-permute-done((bf16[64,1024]{1,0:T(8,128)(2,1)S(1)}, bf16[64,1024]{1,0:T(8,128)(2,1)S(1)}, u32[]{:S(2)}, u32[]{:S(2)}) %collective-permute-start.24) | collective-permute-done | bytes 131104 | tf_op jit(solution)/shard_map/ppermute | solution.py:202
  61.7 1.6 %collective-permute-start.25 = (bf16[128,1024]{1,0:T(8,128)(2,1)S(1)}, bf16[128,1024]{1,0:T(8,128)(2,1)S(1)}, u32[]{:S(2)}, u32[]{:S(2)}) collective-permute-start(bf16[128,1024]{1,0:T(8,128)(2,1)S(1)} %get-tuple-element.27), channel_id=1, source_target_pairs={{0,2},{1,3},{2,0},{3,1},{4,6},{5,7},{6,4},{7,5},{8,10},{9,11},{10,... | collective-permute-start | bytes 786440 | tf_op jit(solution)/shard_map/ppermute | solution.py:202
  64.0 5.0 %collective-permute-done.25 = bf16[128,1024]{1,0:T(8,128)(2,1)S(1)} collective-permute-done((bf16[128,1024]{1,0:T(8,128)(2,1)S(1)}, bf16[128,1024]{1,0:T(8,128)(2,1)S(1)}, u32[]{:S(2)}, u32[]{:S(2)}) %collective-permute-start.25) | collective-permute-done | bytes 262176 | tf_op jit(solution)/shard_map/ppermute | solution.py:202
  71.2 3.1 %collective-permute-start.28 = (bf16[64,1024]{1,0:T(8,128)(2,1)S(1)}, bf16[64,1024]{1,0:T(8,128)(2,1)S(1)}, u32[]{:S(2)}, u32[]{:S(2)}) collective-permute-start(bf16[64,1024]{1,0:T(8,128)(2,1)S(1)} %get-tuple-element.44), channel_id=1, source_target_pairs={{0,12},{1,13},{2,14},{3,15},{4,8},{5,9},{6,10},{7,11},{8,4},{9,5},... | collective-permute-start | bytes 393224 | tf_op jit(solution)/shard_map/ppermute | solution.py:202
  75.0 1.5 %collective-permute-done.34 = bf16[128,1024]{1,0:T(8,128)(2,1)S(1)} collective-permute-done((bf16[128,1024]{1,0:T(8,128)(2,1)S(1)}, bf16[128,1024]{1,0:T(8,128)(2,1)S(1)}, u32[]{:S(2)}, u32[]{:S(2)}) %collective-permute-start.34) | collective-permute-done | bytes 262176 | tf_op jit(solution)/shard_map/ppermute | solution.py:202
  77.2 2.1 %collective-permute-start.35 = (bf16[64,1024]{1,0:T(8,128)(2,1)S(1)}, bf16[64,1024]{1,0:T(8,128)(2,1)S(1)}, u32[]{:S(2)}, u32[]{:S(2)}) collective-permute-start(bf16[64,1024]{1,0:T(8,128)(2,1)S(1)} %slice.141), channel_id=1, source_target_pairs={{0,4},{1,5},{2,6},{3,7},{4,0},{5,1},{6,2},{7,3},{8,12},{9,13},{10,... | collective-permute-start | bytes 393224 | tf_op jit(solution)/shard_map/ppermute | solution.py:202
  79.3 4.8 %collective-permute-done.27 = bf16[64,1024]{1,0:T(8,128)(2,1)S(1)} collective-permute-done((bf16[64,1024]{1,0:T(8,128)(2,1)S(1)}, bf16[64,1024]{1,0:T(8,128)(2,1)S(1)}, u32[]{:S(2)}, u32[]{:S(2)}) %collective-permute-start.27) | collective-permute-done | bytes 131104 | tf_op jit(solution)/shard_map/ppermute | solution.py:202
  (76 shorter events, 13.0 us)
Async XLA Ops:
  1.0 8.9 %collective-permute-start = (bf16[64,1152]{1,0:T(8,128)(2,1)S(1)}, bf16[64,1152]{1,0:T(8,128)(2,1)S(1)}, u32[]{:S(2)}, u32[]{:S(2)}) collective-permute-start(bf16[64,1152]{1,0:T(8,128)(2,1)S(1)} %shard_map.64), channel_id=1, source_target_pairs={{0,4},{1,5},{2,6},{3,7},{4,0},{5,1},{6,2},{7,3},{8,12},{9,13},{10,... | collective-permute-start | bytes 442376 | tf_op jit(solution)/shard_map/ppermute | solution.py:202
  4.1 14.0 %collective-permute-start.10 = (bf16[64,1152]{1,0:T(8,128)(2,1)S(1)}, bf16[64,1152]{1,0:T(8,128)(2,1)S(1)}, u32[]{:S(2)}, u32[]{:S(2)}) collective-permute-start(bf16[64,1152]{1,0:T(8,128)(2,1)S(1)} %shard_map.64), channel_id=1, source_target_pairs={{0,8},{1,9},{2,10},{3,11},{4,12},{5,13},{6,14},{7,15},{8,0},{9,1},... | collective-permute-start | bytes 442376 | tf_op jit(solution)/shard_map/ppermute | solution.py:202
  6.6 11.4 %collective-permute-start.11 = (bf16[64,1152]{1,0:T(8,128)(2,1)S(1)}, bf16[64,1152]{1,0:T(8,128)(2,1)S(1)}, u32[]{:S(2)}, u32[]{:S(2)}) collective-permute-start(bf16[64,1152]{1,0:T(8,128)(2,1)S(1)} %shard_map.64), channel_id=1, source_target_pairs={{0,12},{1,13},{2,14},{3,15},{4,8},{5,9},{6,10},{7,11},{8,4},{9,5},... | collective-permute-start | bytes 442376 | tf_op jit(solution)/shard_map/ppermute | solution.py:202
  9.9 11.8 %collective-permute-start.1 = (bf16[128,1152]{1,0:T(8,128)(2,1)S(1)}, bf16[128,1152]{1,0:T(8,128)(2,1)S(1)}, u32[]{:S(2)}, u32[]{:S(2)}) collective-permute-start(bf16[128,1152]{1,0:T(8,128)(2,1)S(1)} %pad_maximum_fusion.refs_0_), channel_id=1, source_target_pairs={{0,1},{1,0},{2,3},{3,2},{4,5},{5,4},{6,7},{7,6},{8,9},{9,8},{10,11... | collective-permute-start | bytes 884744 | tf_op jit(solution)/shard_map/ppermute | solution.py:202
  10.0 11.2 %collective-permute-start.2 = (bf16[128,1152]{1,0:T(8,128)(2,1)S(1)}, bf16[128,1152]{1,0:T(8,128)(2,1)S(1)}, u32[]{:S(2)}, u32[]{:S(2)}) collective-permute-start(bf16[128,1152]{1,0:T(8,128)(2,1)S(1)} %pad_maximum_fusion.refs_0_), channel_id=1, source_target_pairs={{0,16},{1,17},{2,18},{3,19},{4,20},{5,21},{6,22},{7,23},{8,24},{9,... | collective-permute-start | bytes 884744 | tf_op jit(solution)/shard_map/ppermute | solution.py:202
  11.8 9.9 %collective-permute-start.4 = (bf16[128,1152]{1,0:T(8,128)(2,1)S(1)}, bf16[128,1152]{1,0:T(8,128)(2,1)S(1)}, u32[]{:S(2)}, u32[]{:S(2)}) collective-permute-start(bf16[128,1152]{1,0:T(8,128)(2,1)S(1)} %pad_maximum_fusion.refs_0_), channel_id=1, source_target_pairs={{0,2},{1,3},{2,0},{3,1},{4,6},{5,7},{6,4},{7,5},{8,10},{9,11},{10,... | collective-permute-start | bytes 884744 | tf_op jit(solution)/shard_map/ppermute | solution.py:202
  18.1 8.5 %collective-permute-start.13 = (bf16[128,1152]{1,0:T(8,128)(2,1)S(1)}, bf16[128,1152]{1,0:T(8,128)(2,1)S(1)}, u32[]{:S(2)}, u32[]{:S(2)}) collective-permute-start(bf16[128,1152]{1,0:T(8,128)(2,1)S(1)} %constant_dynamic-update-slice_fusion.refs_0_), channel_id=1, source_target_pairs={{0,16},{1,17},{2,18},{3,19},{4,20},{5,21},{6,22},{7,23},{8,24},{9,... | collective-permute-start | bytes 884744 | tf_op jit(solution)/shard_map/ppermute | solution.py:202
  19.7 8.8 %collective-permute-start.15 = (bf16[128,1152]{1,0:T(8,128)(2,1)S(1)}, bf16[128,1152]{1,0:T(8,128)(2,1)S(1)}, u32[]{:S(2)}, u32[]{:S(2)}) collective-permute-start(bf16[128,1152]{1,0:T(8,128)(2,1)S(1)} %constant_dynamic-update-slice_fusion.refs_0_), channel_id=1, source_target_pairs={{0,2},{1,3},{2,0},{3,1},{4,6},{5,7},{6,4},{7,5},{8,10},{9,11},{10,... | collective-permute-start | bytes 884744 | tf_op jit(solution)/shard_map/ppermute | solution.py:202
  21.2 10.6 %collective-permute-start.3 = (bf16[128,1152]{1,0:T(8,128)(2,1)S(1)}, bf16[128,1152]{1,0:T(8,128)(2,1)S(1)}, u32[]{:S(2)}, u32[]{:S(2)}) collective-permute-start(bf16[128,1152]{1,0:T(8,128)(2,1)S(1)} %collective-permute-done.2.refs_2_), channel_id=1, source_target_pairs={{0,1},{1,0},{2,3},{3,2},{4,5},{5,4},{6,7},{7,6},{8,9},{9,8},{10,11... | collective-permute-start | bytes 884744 | tf_op jit(solution)/shard_map/ppermute | solution.py:202
  21.7 12.7 %collective-permute-start.5 = (bf16[128,1152]{1,0:T(8,128)(2,1)S(1)}, bf16[128,1152]{1,0:T(8,128)(2,1)S(1)}, u32[]{:S(2)}, u32[]{:S(2)}) collective-permute-start(bf16[128,1152]{1,0:T(8,128)(2,1)S(1)} %collective-permute-done.4.refs_4_), channel_id=1, source_target_pairs={{0,1},{1,0},{2,3},{3,2},{4,5},{5,4},{6,7},{7,6},{8,9},{9,8},{10,11... | collective-permute-start | bytes 884744 | tf_op jit(solution)/shard_map/ppermute | solution.py:202
  28.5 16.3 %collective-permute-start.12 = (bf16[128,1152]{1,0:T(8,128)(2,1)S(1)}, bf16[128,1152]{1,0:T(8,128)(2,1)S(1)}, u32[]{:S(2)}, u32[]{:S(2)}) collective-permute-start(bf16[128,1152]{1,0:T(8,128)(2,1)S(1)} %constant_dynamic-update-slice_fusion.refs_0_), channel_id=1, source_target_pairs={{0,1},{1,0},{2,3},{3,2},{4,5},{5,4},{6,7},{7,6},{8,9},{9,8},{10,11... | collective-permute-start | bytes 884744 | tf_op jit(solution)/shard_map/ppermute | solution.py:202
  31.8 13.2 %collective-permute-start.17 = (bf16[64,1152]{1,0:T(8,128)(2,1)S(1)}, bf16[64,1152]{1,0:T(8,128)(2,1)S(1)}, u32[]{:S(2)}, u32[]{:S(2)}) collective-permute-start(bf16[64,1152]{1,0:T(8,128)(2,1)S(1)} %slice.122), channel_id=1, source_target_pairs={{0,16},{1,17},{2,18},{3,19},{4,20},{5,21},{6,22},{7,23},{8,24},{9,... | collective-permute-start | bytes 442376 | tf_op jit(solution)/shard_map/ppermute | solution.py:202
  34.3 11.1 %collective-permute-start.18 = (bf16[64,1152]{1,0:T(8,128)(2,1)S(1)}, bf16[64,1152]{1,0:T(8,128)(2,1)S(1)}, u32[]{:S(2)}, u32[]{:S(2)}) collective-permute-start(bf16[64,1152]{1,0:T(8,128)(2,1)S(1)} %slice.123), channel_id=1, source_target_pairs={{0,2},{1,3},{2,0},{3,1},{4,6},{5,7},{6,4},{7,5},{8,10},{9,11},{10,... | collective-permute-start | bytes 442376 | tf_op jit(solution)/shard_map/ppermute | solution.py:202
  35.8 9.7 %collective-permute-start.14 = (bf16[128,1152]{1,0:T(8,128)(2,1)S(1)}, bf16[128,1152]{1,0:T(8,128)(2,1)S(1)}, u32[]{:S(2)}, u32[]{:S(2)}) collective-permute-start(bf16[128,1152]{1,0:T(8,128)(2,1)S(1)} %collective-permute-done.13.refs_2_), channel_id=1, source_target_pairs={{0,1},{1,0},{2,3},{3,2},{4,5},{5,4},{6,7},{7,6},{8,9},{9,8},{10,11... | collective-permute-start | bytes 884744 | tf_op jit(solution)/shard_map/ppermute | solution.py:202
  35.9 10.1 %collective-permute-start.16 = (bf16[128,1152]{1,0:T(8,128)(2,1)S(1)}, bf16[128,1152]{1,0:T(8,128)(2,1)S(1)}, u32[]{:S(2)}, u32[]{:S(2)}) collective-permute-start(bf16[128,1152]{1,0:T(8,128)(2,1)S(1)} %collective-permute-done.15.refs_4_), channel_id=1, source_target_pairs={{0,1},{1,0},{2,3},{3,2},{4,5},{5,4},{6,7},{7,6},{8,9},{9,8},{10,11... | collective-permute-start | bytes 884744 | tf_op jit(solution)/shard_map/ppermute | solution.py:202
  44.9 7.9 %collective-permute-start.30 = (bf16[128,1024]{1,0:T(8,128)(2,1)S(1)}, bf16[128,1024]{1,0:T(8,128)(2,1)S(1)}, u32[]{:S(2)}, u32[]{:S(2)}) collective-permute-start(bf16[128,1024]{1,0:T(8,128)(2,1)S(1)} %get-tuple-element.32), channel_id=1, source_target_pairs={{0,1},{1,0},{2,3},{3,2},{4,5},{5,4},{6,7},{7,6},{8,9},{9,8},{10,11... | collective-permute-start | bytes 786440 | tf_op jit(solution)/shard_map/ppermute | solution.py:202
  45.5 18.0 %collective-permute-start.29 = (bf16[3,128,1024]{2,1,0:T(8,128)(2,1)S(1)}, bf16[3,128,1024]{2,1,0:T(8,128)(2,1)S(1)}, u32[]{:S(2)}, u32[]{:S(2)}) collective-permute-start(bf16[3,128,1024]{2,1,0:T(8,128)(2,1)S(1)} %get-tuple-element.30), channel_id=1, source_target_pairs={{0,1},{1,0},{2,3},{3,2},{4,5},{5,4},{6,7},{7,6},{8,9},{9,8},{10,11... | collective-permute-start | bytes 2359304 | tf_op jit(solution)/shard_map/ppermute | solution.py:202
  52.9 10.9 %collective-permute-start.32 = (bf16[64,1024]{1,0:T(8,128)(2,1)S(1)}, bf16[64,1024]{1,0:T(8,128)(2,1)S(1)}, u32[]{:S(2)}, u32[]{:S(2)}) collective-permute-start(bf16[64,1024]{1,0:T(8,128)(2,1)S(1)} %get-tuple-element.47), channel_id=1, source_target_pairs={{0,2},{1,3},{2,0},{3,1},{4,6},{5,7},{6,4},{7,5},{8,10},{9,11},{10,... | collective-permute-start | bytes 393224 | tf_op jit(solution)/shard_map/ppermute | solution.py:202
  53.5 10.3 %collective-permute-start.31 = (bf16[64,1024]{1,0:T(8,128)(2,1)S(1)}, bf16[64,1024]{1,0:T(8,128)(2,1)S(1)}, u32[]{:S(2)}, u32[]{:S(2)}) collective-permute-start(bf16[64,1024]{1,0:T(8,128)(2,1)S(1)} %get-tuple-element.48), channel_id=1, source_target_pairs={{0,16},{1,17},{2,18},{3,19},{4,20},{5,21},{6,22},{7,23},{8,24},{9,... | collective-permute-start | bytes 393224 | tf_op jit(solution)/shard_map/ppermute | solution.py:202
  54.0 7.4 %collective-permute-start.24 = (bf16[64,1024]{1,0:T(8,128)(2,1)S(1)}, bf16[64,1024]{1,0:T(8,128)(2,1)S(1)}, u32[]{:S(2)}, u32[]{:S(2)}) collective-permute-start(bf16[64,1024]{1,0:T(8,128)(2,1)S(1)} %get-tuple-element.45), channel_id=1, source_target_pairs={{0,2},{1,3},{2,0},{3,1},{4,6},{5,7},{6,4},{7,5},{8,10},{9,11},{10,... | collective-permute-start | bytes 393224 | tf_op jit(solution)/shard_map/ppermute | solution.py:202
  61.7 7.3 %collective-permute-start.25 = (bf16[128,1024]{1,0:T(8,128)(2,1)S(1)}, bf16[128,1024]{1,0:T(8,128)(2,1)S(1)}, u32[]{:S(2)}, u32[]{:S(2)}) collective-permute-start(bf16[128,1024]{1,0:T(8,128)(2,1)S(1)} %get-tuple-element.27), channel_id=1, source_target_pairs={{0,2},{1,3},{2,0},{3,1},{4,6},{5,7},{6,4},{7,5},{8,10},{9,11},{10,... | collective-permute-start | bytes 786440 | tf_op jit(solution)/shard_map/ppermute | solution.py:202
  71.2 8.1 %collective-permute-start.28 = (bf16[64,1024]{1,0:T(8,128)(2,1)S(1)}, bf16[64,1024]{1,0:T(8,128)(2,1)S(1)}, u32[]{:S(2)}, u32[]{:S(2)}) collective-permute-start(bf16[64,1024]{1,0:T(8,128)(2,1)S(1)} %get-tuple-element.44), channel_id=1, source_target_pairs={{0,12},{1,13},{2,14},{3,15},{4,8},{5,9},{6,10},{7,11},{8,4},{9,5},... | collective-permute-start | bytes 393224 | tf_op jit(solution)/shard_map/ppermute | solution.py:202
  74.3 9.8 %collective-permute-start.27 = (bf16[64,1024]{1,0:T(8,128)(2,1)S(1)}, bf16[64,1024]{1,0:T(8,128)(2,1)S(1)}, u32[]{:S(2)}, u32[]{:S(2)}) collective-permute-start(bf16[64,1024]{1,0:T(8,128)(2,1)S(1)} %get-tuple-element.43), channel_id=1, source_target_pairs={{0,8},{1,9},{2,10},{3,11},{4,12},{5,13},{6,14},{7,15},{8,0},{9,1},... | collective-permute-start | bytes 393224 | tf_op jit(solution)/shard_map/ppermute | solution.py:202
  77.2 7.3 %collective-permute-start.35 = (bf16[64,1024]{1,0:T(8,128)(2,1)S(1)}, bf16[64,1024]{1,0:T(8,128)(2,1)S(1)}, u32[]{:S(2)}, u32[]{:S(2)}) collective-permute-start(bf16[64,1024]{1,0:T(8,128)(2,1)S(1)} %slice.141), channel_id=1, source_target_pairs={{0,4},{1,5},{2,6},{3,7},{4,0},{5,1},{6,2},{7,3},{8,12},{9,13},{10,... | collective-permute-start | bytes 393224 | tf_op jit(solution)/shard_map/ppermute | solution.py:202
  (12 other events, 56.9 us)

commit v4 on v3

--- a/solution.py
+++ b/solution.py
@@ -10,6 +10,8 @@
 BF16, F32 = jnp.bfloat16, jnp.float32
 PAIR = ("dp", "expert")
 LANES = 128
+GATHER = (True, False)
+SCATTER = (False, False)
 MIB = 1024 * 1024
 VMEM_SPEC = pl.BlockSpec(memory_space=pltpu.VMEM)
 
@@ -60,16 +62,26 @@
     )(*operands)
 
 
-def dispatch(table, expert_place, experts, block, room):
-    rows = table.shape[0]
+def earlier(rows, block):
     this = lax.broadcasted_iota(jnp.int32, (rows, rows), 0)
     other = lax.broadcasted_iota(jnp.int32, (rows, rows), 1)
-    before = (other < this) & (other // block == this // block)
-    ranks = jnp.dot(before.astype(BF16), (table > 0.0).astype(BF16), preferred_element_type=F32)
+    start = jnp.zeros((rows, 1), jnp.int32)
+    place = lax.broadcasted_iota(jnp.int32, (rows, 1), 0)
+    for i in range(1, rows // block):
+        start = jnp.where(place >= i * block, i * block, start)
+    return ((other < this) & (other >= start)).astype(BF16)
+
+
+def dispatch(table, before, expert_place, experts, block, room):
+    rows = table.shape[0]
+    ranks = jnp.dot(before, (table > 0.0).astype(BF16), preferred_element_type=F32)
     lane = lax.broadcasted_iota(jnp.int32, table.shape, 1)
     slots = experts * rows // block * room
     slot = lax.broadcasted_iota(jnp.int32, (rows, slots), 1)
-    first = lax.broadcasted_iota(jnp.int32, (rows, 1), 0) // block * room
+    place = lax.broadcasted_iota(jnp.int32, (rows, 1), 0)
+    first = jnp.zeros((rows, 1), jnp.int32)
+    for i in range(1, rows // block):
+        first = jnp.where(place >= i * block, i * room, first)
     taken = jnp.zeros((rows, slots), F32)
     for e in range(experts):
         here = lane == expert_place * experts + e
@@ -81,21 +93,22 @@
 
 def experts_kernel(first, counts, block, room, places, gate_in, up_in, down_in, *refs):
     if first:
-        pieces, refs = refs[:-13], refs[-13:]
+        pieces, refs = refs[:-14], refs[-14:]
         corner_keep, corner_give, keep_ref, give_ref, gate_ref, up_ref, down_ref, *refs, sem = refs
     else:
-        pieces, refs = refs[:-9], refs[-9:]
+        pieces, refs = refs[:-10], refs[-10:]
         corner_keep, corner_give, keep_ref, give_ref, *refs = refs
         gate_ref, up_ref, down_ref = gate_in, up_in, down_in
-    rows_buf, table_buf, taken_buf, packed_buf, out_buf = refs
+    rows_buf, table_buf, taken_buf, packed_buf, out_buf, hidden_buf = refs
     experts, model, hidden = gate_ref.shape
     width = model // 2
     fetches = []
     if first:
         ends = []
         for e in range(experts):
+            ends += [(gate_in.at[e], gate_ref.at[e]), (up_in.at[e], up_ref.at[e])]
+        for e in range(experts):
             span = pl.ds(e * hidden, hidden)
-            ends += [(gate_in.at[e], gate_ref.at[e]), (up_in.at[e], up_ref.at[e])]
             ends += [(down_in.at[span], down_ref.at[span])]
         fetches = [pltpu.make_async_copy(*pair, sem.at[i]) for i, pair in enumerate(ends)]
         for copy in fetches:
@@ -105,6 +118,7 @@
     others = pl.ds(pl.multiple_of((1 - places[0]) * width, width), width)
     group = rows_buf.shape[0] // 2
     slots = taken_buf.shape[2] // experts
+    before = earlier(group, block)
     taken = 0
     for g in range(2):
         for count, columns in zip(counts[g], (mine, others)):
@@ -116,7 +130,7 @@
                     table_buf[span, :] = piece[:, width:].astype(F32)
                 row += piece.shape[0]
             taken += count
-        table = dispatch(table_buf[pl.ds(g * group, group), :], places[1], experts, block, room)
+        table = dispatch(table_buf[pl.ds(g * group, group), :], before, places[1], experts, block, room)
         taken_buf[g] = table.astype(BF16)
         picked = jnp.where(table > 0.0, 1.0, 0.0).T.astype(BF16)
         packed = jnp.dot(picked, rows_buf[pl.ds(g * group, group), :], preferred_element_type=F32).astype(BF16)
@@ -124,14 +138,17 @@
             packed_buf[e, pl.ds(g * slots, slots), :] = packed[e * slots : (e + 1) * slots]
 
     for e in range(experts):
-        for copy in fetches[3 * e : 3 * e + 3]:
+        for copy in fetches[2 * e : 2 * e + 2]:
             copy.wait()
         rows = packed_buf[e]
         gate = jnp.dot(rows, gate_ref[e], preferred_element_type=F32)
         up = jnp.dot(rows, up_ref[e], preferred_element_type=F32)
-        value = (gate / (1.0 + jnp.exp(-gate)) * up).astype(BF16)
+        hidden_buf[e] = (gate / (1.0 + jnp.exp(-gate)) * up).astype(BF16)
+    for e in range(experts):
+        for copy in fetches[2 * experts + e : 2 * experts + e + 1]:
+            copy.wait()
         down = down_ref[pl.ds(e * hidden, hidden), :]
-        out = jnp.dot(value, down, preferred_element_type=F32).astype(BF16)
+        out = jnp.dot(hidden_buf[e], down, preferred_element_type=F32).astype(BF16)
         for g in range(2):
             out_buf[g, pl.ds(e * slots, slots), :] = out[g * slots : (g + 1) * slots]
     half = group // 2
@@ -174,12 +191,32 @@
             pltpu.VMEM((2, rows // 2, experts * slots), BF16),
             pltpu.VMEM((experts, 2 * slots, model), BF16),
             pltpu.VMEM((2, experts * slots, model), BF16),
+            pltpu.VMEM((experts, 2 * slots, hidden), BF16),
         ]
         + extra,
         out_shape=outs,
         compiler_params=pltpu.CompilerParams(vmem_limit_bytes=20 * MIB),
         cost_estimate=pl.CostEstimate(flops=rows, bytes_accessed=rows, transcendentals=0),
     )(places, *operands)
+
+
+def cut_kernel(by_x, by_y, *refs):
+    out_x, out_y = refs[-2:]
+    half = out_x.shape[0]
+    out_x[...] = by_x[:half, : out_x.shape[1]]
+    out_y[...] = by_y[half:]
+
+
+def cut(by_x, by_y, behind):
+    half = jax.ShapeDtypeStruct((by_y.shape[0] // 2, by_y.shape[1]), BF16)
+    return pl.pallas_call(
+        cut_kernel,
+        in_specs=[VMEM_SPEC] * 2 + [pl.BlockSpec(memory_space=pl.ANY)] * len(behind),
+        out_specs=[VMEM_SPEC] * 2,
+        out_shape=[half, half],
+        compiler_params=pltpu.CompilerParams(vmem_limit_bytes=2 * MIB),
+        cost_estimate=pl.CostEstimate(flops=1, bytes_accessed=1, transcendentals=0),
+    )(near(by_x), near(by_y), *behind)
 
 
 def add(*terms):
@@ -212,10 +249,14 @@
     def cores(pieces):
         return [send(piece, core=1) for piece in pieces]
 
-    def gather(own):
-        half = own.shape[0] // 2
-        by_x, by_y = send(own, x=1), send(own, y=1)
-        corner = [send(by_x[:half], y=1), send(by_y[half:], x=1)]
+    def gather(own, direct):
+        features = own[:, : tokens.shape[1]]
+        by_x, by_y = send(own, x=1), send(features, y=1)
+        if direct:
+            corner = [send(features, x=1, y=1)]
+        else:
+            half_x, half_y = cut(by_x, by_y, [])
+            corner = [send(half_x, y=1), send(half_y, x=1)]
         return [[own] + cores([own]), [by_y] + cores([by_y])], [[by_x] + cores([by_x]), corner + cores(corner)]
 
     def total(keep, give):
@@ -236,18 +277,22 @@
     parts, first, sums = 2, True, []
     count = line // parts
     for i in range(parts):
-        groups = gather(join(blocks[i * count : (i + 1) * count]))
+        groups = gather(join(blocks[i * count : (i + 1) * count]), GATHER[i])
         corner, corner_give, keep, give, *rest = run_experts(places, weights, groups, block, room, first)
         if first:
             weights, first = rest, False
         rest = total(keep, give)
-        sums.append((rest[0], *turn(total(corner, corner_give), rest)))
+        corner = total(corner, corner_give)
+        if SCATTER[i]:
+            sums.append((rest[0], rest[1], rest[2], [send(corner, x=1, y=1)]))
+        else:
+            sums.append((rest[0], *turn(corner, rest), []))
     back, arrived = [], ()
     for i in reversed(range(parts)):
-        own, for_x, for_y = sums[i]
+        own, for_x, for_y, direct = sums[i]
         for_x, for_y = after((for_x, for_y), arrived)
         arrived = send(for_x, x=1), send(for_y, y=1)
-        mine = add(own, *arrived)
+        mine = add(own, *arrived, *direct)
         for k in range(count):
             piece = mine[k * block : (k + 1) * block]
             back.append(send(piece, steps=i * count + k) if i or k else piece)

time: 85.3 us -> 82.6 us (0.968)
  waiting for transfers between devices: 34.2 us -> 33.1 us
  starting transfers between devices: 33.8 us -> 32.7 us
    ppermute x36 -> x34, waiting for transfers between devices: 34.2 us -> 33.1 us  [send(): return lax.ppermute(array, PAIR, pairs)]
    ppermute x36 -> x34, starting transfers between devices: 33.8 us -> 32.7 us  [send(): return lax.ppermute(array, PAIR, pairs)]
  transfers between devices with their start and end apart: 36 -> 34, of which waited for: 16 -> 13; matrix products, arithmetic and copies ran while one was open for 2% -> 2% of each run, Pallas kernels for 16% -> 16%
where the time goes in v4:
time: 82.6 us; the launch traced here: 82.4 us
  waiting for transfers between devices  33.1 us (40%)
  starting transfers between devices  32.7 us (40%)
  Pallas kernels  14.1 us (17%)
  other arithmetic  2.05 us (2%)
    ppermute x34, waiting for transfers between devices, send(): return lax.ppermute(array, PAIR, pairs)  33.1 us
    ppermute x34, starting transfers between devices, send(): return lax.ppermute(array, PAIR, pairs)  32.7 us
    pallas_call x2, Pallas kernels, run_experts(): pl.pallas_call(functools.partial(experts_kernel, first, counts, block, ro...  13.1 us
    convert_element_type x9, other arithmetic, add(): functools.reduce(lambda a, b: a + b, [t.astype(F32) for t in terms])  1.85 us
  transfers between devices with their start and end apart: 34, of which 13 were waited for; matrix products, arithmetic and copies ran while one was open for 2% of the time, Pallas kernels for 16%

profile of v4, /device:TPU:0, one launch (start us, length us, event | category | flops | bytes accessed | tf_op | source)
XLA Modules:
  0.0 82.4 jit_solution(6608135671371950574)
XLA Ops:
  1.0 3.1 %collective-permute-start = (bf16[64,1152]{1,0:T(8,128)(2,1)S(1)}, bf16[64,1152]{1,0:T(8,128)(2,1)S(1)}, u32[]{:S(2)}, u32[]{:S(2)}) collective-permute-start(bf16[64,1152]{1,0:T(8,128)(2,1)S(1)} %shard_map.64), channel_id=1, source_target_pairs={{0,4},{1,5},{2,6},{3,7},{4,0},{5,1},{6,2},{7,3},{8,12},{9,13},{10,... | collective-permute-start | bytes 442376 | tf_op jit(solution)/shard_map/ppermute | solution.py:239
  4.1 2.6 %collective-permute-start.8 = (bf16[64,1152]{1,0:T(8,128)(2,1)S(1)}, bf16[64,1152]{1,0:T(8,128)(2,1)S(1)}, u32[]{:S(2)}, u32[]{:S(2)}) collective-permute-start(bf16[64,1152]{1,0:T(8,128)(2,1)S(1)} %shard_map.64), channel_id=1, source_target_pairs={{0,8},{1,9},{2,10},{3,11},{4,12},{5,13},{6,14},{7,15},{8,0},{9,1},... | collective-permute-start | bytes 442376 | tf_op jit(solution)/shard_map/ppermute | solution.py:239
  6.7 3.3 %collective-permute-done = bf16[64,1152]{1,0:T(8,128)(2,1)S(1)} collective-permute-done((bf16[64,1152]{1,0:T(8,128)(2,1)S(1)}, bf16[64,1152]{1,0:T(8,128)(2,1)S(1)}, u32[]{:S(2)}, u32[]{:S(2)}) %collective-permute-start) | collective-permute-done | bytes 147488 | tf_op jit(solution)/shard_map/ppermute | solution.py:239
  9.9 1.8 %collective-permute-start.2 = (bf16[128,1024]{1,0:T(8,128)(2,1)S(1)}, bf16[128,1024]{1,0:T(8,128)(2,1)S(1)}, u32[]{:S(2)}, u32[]{:S(2)}) collective-permute-start(bf16[128,1024]{1,0:T(8,128)(2,1)S(1)} %fusion.4), channel_id=1, source_target_pairs={{0,16},{1,17},{2,18},{3,19},{4,20},{5,21},{6,22},{7,23},{8,24},{9,... | collective-permute-start | bytes 786440 | tf_op jit(solution)/shard_map/ppermute | solution.py:239
  11.7 1.4 %collective-permute-start.6 = (bf16[128,1024]{1,0:T(8,128)(2,1)S(1)}, bf16[128,1024]{1,0:T(8,128)(2,1)S(1)}, u32[]{:S(2)}, u32[]{:S(2)}) collective-permute-start(bf16[128,1024]{1,0:T(8,128)(2,1)S(1)} %fusion.4), channel_id=1, source_target_pairs={{0,18},{1,19},{2,16},{3,17},{4,22},{5,23},{6,20},{7,21},{8,26},{9,... | collective-permute-start | bytes 786440 | tf_op jit(solution)/shard_map/ppermute | solution.py:239
  13.6 4.5 %collective-permute-done.8 = bf16[64,1152]{1,0:T(8,128)(2,1)S(1)} collective-permute-done((bf16[64,1152]{1,0:T(8,128)(2,1)S(1)}, bf16[64,1152]{1,0:T(8,128)(2,1)S(1)}, u32[]{:S(2)}, u32[]{:S(2)}) %collective-permute-start.8) | collective-permute-done | bytes 147488 | tf_op jit(solution)/shard_map/ppermute | solution.py:239
  18.1 1.6 %collective-permute-start.11 = (bf16[128,1024]{1,0:T(8,128)(2,1)S(1)}, bf16[128,1024]{1,0:T(8,128)(2,1)S(1)}, u32[]{:S(2)}, u32[]{:S(2)}) collective-permute-start(bf16[128,1024]{1,0:T(8,128)(2,1)S(1)} %slice.114), channel_id=1, source_target_pairs={{0,16},{1,17},{2,18},{3,19},{4,20},{5,21},{6,22},{7,23},{8,24},{9,... | collective-permute-start | bytes 786440 | tf_op jit(solution)/shard_map/ppermute | solution.py:239
  19.7 1.5 %collective-permute-start.13 = (bf16[128,1152]{1,0:T(8,128)(2,1)S(1)}, bf16[128,1152]{1,0:T(8,128)(2,1)S(1)}, u32[]{:S(2)}, u32[]{:S(2)}) collective-permute-start(bf16[128,1152]{1,0:T(8,128)(2,1)S(1)} %constant_dynamic-update-slice_fusion.refs_0_), channel_id=1, source_target_pairs={{0,2},{1,3},{2,0},{3,1},{4,6},{5,7},{6,4},{7,5},{8,10},{9,11},{10,... | collective-permute-start | bytes 884744 | tf_op jit(solution)/shard_map/ppermute | solution.py:239
  22.1 4.1 %collective-permute-done.4.refs_4_ = bf16[128,1152]{1,0:T(8,128)(2,1)S(1)} collective-permute-done((bf16[128,1152]{1,0:T(8,128)(2,1)S(1)}, bf16[128,1152]{1,0:T(8,128)(2,1)S(1)}, u32[]{:S(2)}, u32[]{:S(2)}) %collective-permute-start.4) | collective-permute-done | bytes 294944 | tf_op jit(solution)/shard_map/ppermute | solution.py:239
  26.8 2.6 %collective-permute-done.13.by_x.refs_4_ = bf16[128,1152]{1,0:T(8,128)(2,1)S(1)} collective-permute-done((bf16[128,1152]{1,0:T(8,128)(2,1)S(1)}, bf16[128,1152]{1,0:T(8,128)(2,1)S(1)}, u32[]{:S(2)}, u32[]{:S(2)}) %collective-permute-start.13) | collective-permute-done | bytes 294944 | tf_op jit(solution)/shard_map/ppermute | solution.py:239
  30.0 1.4 %collective-permute-start.15 = (bf16[64,1024]{1,0:T(8,128)(2,1)S(1)}, bf16[64,1024]{1,0:T(8,128)(2,1)S(1)}, u32[]{:S(2)}, u32[]{:S(2)}) collective-permute-start(bf16[64,1024]{1,0:T(8,128)(2,1)S(1)} %get-tuple-element.25), channel_id=1, source_target_pairs={{0,16},{1,17},{2,18},{3,19},{4,20},{5,21},{6,22},{7,23},{8,24},{9,... | collective-permute-start | bytes 393224 | tf_op jit(solution)/shard_map/ppermute | solution.py:239
  31.3 1.5 %collective-permute-start.16 = (bf16[64,1024]{1,0:T(8,128)(2,1)S(1)}, bf16[64,1024]{1,0:T(8,128)(2,1)S(1)}, u32[]{:S(2)}, u32[]{:S(2)}) collective-permute-start(bf16[64,1024]{1,0:T(8,128)(2,1)S(1)} %get-tuple-element.26), channel_id=1, source_target_pairs={{0,2},{1,3},{2,0},{3,1},{4,6},{5,7},{6,4},{7,5},{8,10},{9,11},{10,... | collective-permute-start | bytes 393224 | tf_op jit(solution)/shard_map/ppermute | solution.py:239
  32.9 7.9 %shard_map.65 = (bf16[128,1024]{1,0:T(8,128)(2,1)S(1)}, bf16[128,1024]{1,0:T(8,128)(2,1)S(1)}, bf16[3,128,1024]{2,1,0:T(8,128)(2,1)S(1)}, bf16[3,128,1024]{2,1,0...) custom-call(s32[2]{0:T(128)S(1)} %pad_add_fusion.places, ...), custom_call_target="tpu_custom_call" | custom-call | flops 512 | bytes 512 | tf_op jit(solution)/shard_map/pallas_call | solution.py:182
  43.0 5.2 %shard_map.67 = (bf16[128,1024]{1,0:T(8,128)(2,1)S(1)}, bf16[128,1024]{1,0:T(8,128)(2,1)S(1)}, bf16[3,128,1024]{2,1,0:T(8,128)(2,1)S(1)}, bf16[3,128,1024]{2,1,0:T(8,128)(2,1)S(1)}) custom-call(s32[2]{0:T(128)S(1)} %pad_add_fusion.places, bf16[2,2048,512]{2,1,0:T(8,128)(2,1)S(1)} %get-tuple-element.22.gate_in, ...), custom_call_target="tpu_custom_call" | custom-call | flops 512 | bytes 512 | tf_op jit(solution)/shard_map/pallas_call | solution.py:182
  50.2 1.4 %collective-permute-start.22 = (bf16[64,1024]{1,0:T(8,128)(2,1)S(1)}, bf16[64,1024]{1,0:T(8,128)(2,1)S(1)}, u32[]{:S(2)}, u32[]{:S(2)}) collective-permute-start(bf16[64,1024]{1,0:T(8,128)(2,1)S(1)} %get-tuple-element.49), channel_id=1, source_target_pairs={{0,2},{1,3},{2,0},{3,1},{4,6},{5,7},{6,4},{7,5},{8,10},{9,11},{10,... | collective-permute-start | bytes 393224 | tf_op jit(solution)/shard_map/ppermute | solution.py:239
  51.6 1.5 %collective-permute-start.21 = (bf16[64,1024]{1,0:T(8,128)(2,1)S(1)}, bf16[64,1024]{1,0:T(8,128)(2,1)S(1)}, u32[]{:S(2)}, u32[]{:S(2)}) collective-permute-start(bf16[64,1024]{1,0:T(8,128)(2,1)S(1)} %get-tuple-element.50), channel_id=1, source_target_pairs={{0,16},{1,17},{2,18},{3,19},{4,20},{5,21},{6,22},{7,23},{8,24},{9,... | collective-permute-start | bytes 393224 | tf_op jit(solution)/shard_map/ppermute | solution.py:239
  53.5 4.0 %collective-permute-done.22 = bf16[64,1024]{1,0:T(8,128)(2,1)S(1)} collective-permute-done((bf16[64,1024]{1,0:T(8,128)(2,1)S(1)}, bf16[64,1024]{1,0:T(8,128)(2,1)S(1)}, u32[]{:S(2)}, u32[]{:S(2)}) %collective-permute-start.22) | collective-permute-done | bytes 131104 | tf_op jit(solution)/shard_map/ppermute | solution.py:239
  57.9 1.5 %collective-permute-start.23 = (bf16[128,1024]{1,0:T(8,128)(2,1)S(1)}, bf16[128,1024]{1,0:T(8,128)(2,1)S(1)}, u32[]{:S(2)}, u32[]{:S(2)}) collective-permute-start(bf16[128,1024]{1,0:T(8,128)(2,1)S(1)} %get-tuple-element.31), channel_id=1, source_target_pairs={{0,2},{1,3},{2,0},{3,1},{4,6},{5,7},{6,4},{7,5},{8,10},{9,11},{10,... | collective-permute-start | bytes 786440 | tf_op jit(solution)/shard_map/ppermute | solution.py:239
  60.4 5.0 %collective-permute-done.23 = bf16[128,1024]{1,0:T(8,128)(2,1)S(1)} collective-permute-done((bf16[128,1024]{1,0:T(8,128)(2,1)S(1)}, bf16[128,1024]{1,0:T(8,128)(2,1)S(1)}, u32[]{:S(2)}, u32[]{:S(2)}) %collective-permute-start.23) | collective-permute-done | bytes 262176 | tf_op jit(solution)/shard_map/ppermute | solution.py:239
  65.4 1.1 %collective-permute-done.24 = bf16[128,1024]{1,0:T(8,128)(2,1)S(1)} collective-permute-done((bf16[128,1024]{1,0:T(8,128)(2,1)S(1)}, bf16[128,1024]{1,0:T(8,128)(2,1)S(1)}, u32[]{:S(2)}, u32[]{:S(2)}) %collective-permute-start.24) | collective-permute-done | bytes 262176 | tf_op jit(solution)/shard_map/ppermute | solution.py:239
  67.9 5.6 %collective-permute-start.26 = (bf16[64,1024]{1,0:T(8,128)(2,1)S(1)}, bf16[64,1024]{1,0:T(8,128)(2,1)S(1)}, u32[]{:S(2)}, u32[]{:S(2)}) collective-permute-start(bf16[64,1024]{1,0:T(8,128)(2,1)S(1)} %get-tuple-element.48), channel_id=1, source_target_pairs={{0,12},{1,13},{2,14},{3,15},{4,8},{5,9},{6,10},{7,11},{8,4},{9,5},... | collective-permute-start | bytes 393224 | tf_op jit(solution)/shard_map/ppermute | solution.py:239
  73.6 1.6 %collective-permute-start.33 = (bf16[64,1024]{1,0:T(8,128)(2,1)S(1)}, bf16[64,1024]{1,0:T(8,128)(2,1)S(1)}, u32[]{:S(2)}, u32[]{:S(2)}) collective-permute-start(bf16[64,1024]{1,0:T(8,128)(2,1)S(1)} %slice.132), channel_id=1, source_target_pairs={{0,4},{1,5},{2,6},{3,7},{4,0},{5,1},{6,2},{7,3},{8,12},{9,13},{10,... | collective-permute-start | bytes 393224 | tf_op jit(solution)/shard_map/ppermute | solution.py:239
  75.3 1.5 %collective-permute-done.26 = bf16[64,1024]{1,0:T(8,128)(2,1)S(1)} collective-permute-done((bf16[64,1024]{1,0:T(8,128)(2,1)S(1)}, bf16[64,1024]{1,0:T(8,128)(2,1)S(1)}, u32[]{:S(2)}, u32[]{:S(2)}) %collective-permute-start.26) | collective-permute-done | bytes 131104 | tf_op jit(solution)/shard_map/ppermute | solution.py:239
  76.8 4.9 %collective-permute-done.25 = bf16[64,1024]{1,0:T(8,128)(2,1)S(1)} collective-permute-done((bf16[64,1024]{1,0:T(8,128)(2,1)S(1)}, bf16[64,1024]{1,0:T(8,128)(2,1)S(1)}, u32[]{:S(2)}, u32[]{:S(2)}) %collective-permute-start.25) | collective-permute-done | bytes 131104 | tf_op jit(solution)/shard_map/ppermute | solution.py:239
  (71 shorter events, 11.6 us)
Async XLA Ops:
  1.0 8.9 %collective-permute-start = (bf16[64,1152]{1,0:T(8,128)(2,1)S(1)}, bf16[64,1152]{1,0:T(8,128)(2,1)S(1)}, u32[]{:S(2)}, u32[]{:S(2)}) collective-permute-start(bf16[64,1152]{1,0:T(8,128)(2,1)S(1)} %shard_map.64), channel_id=1, source_target_pairs={{0,4},{1,5},{2,6},{3,7},{4,0},{5,1},{6,2},{7,3},{8,12},{9,13},{10,... | collective-permute-start | bytes 442376 | tf_op jit(solution)/shard_map/ppermute | solution.py:239
  4.1 14.0 %collective-permute-start.8 = (bf16[64,1152]{1,0:T(8,128)(2,1)S(1)}, bf16[64,1152]{1,0:T(8,128)(2,1)S(1)}, u32[]{:S(2)}, u32[]{:S(2)}) collective-permute-start(bf16[64,1152]{1,0:T(8,128)(2,1)S(1)} %shard_map.64), channel_id=1, source_target_pairs={{0,8},{1,9},{2,10},{3,11},{4,12},{5,13},{6,14},{7,15},{8,0},{9,1},... | collective-permute-start | bytes 442376 | tf_op jit(solution)/shard_map/ppermute | solution.py:239
  6.6 11.4 %collective-permute-start.9 = (bf16[64,1152]{1,0:T(8,128)(2,1)S(1)}, bf16[64,1152]{1,0:T(8,128)(2,1)S(1)}, u32[]{:S(2)}, u32[]{:S(2)}) collective-permute-start(bf16[64,1152]{1,0:T(8,128)(2,1)S(1)} %shard_map.64), channel_id=1, source_target_pairs={{0,12},{1,13},{2,14},{3,15},{4,8},{5,9},{6,10},{7,11},{8,4},{9,5},... | collective-permute-start | bytes 442376 | tf_op jit(solution)/shard_map/ppermute | solution.py:239
  9.9 12.2 %collective-permute-start.2 = (bf16[128,1024]{1,0:T(8,128)(2,1)S(1)}, bf16[128,1024]{1,0:T(8,128)(2,1)S(1)}, u32[]{:S(2)}, u32[]{:S(2)}) collective-permute-start(bf16[128,1024]{1,0:T(8,128)(2,1)S(1)} %fusion.4), channel_id=1, source_target_pairs={{0,16},{1,17},{2,18},{3,19},{4,20},{5,21},{6,22},{7,23},{8,24},{9,... | collective-permute-start | bytes 786440 | tf_op jit(solution)/shard_map/ppermute | solution.py:239
  11.7 14.5 %collective-permute-start.6 = (bf16[128,1024]{1,0:T(8,128)(2,1)S(1)}, bf16[128,1024]{1,0:T(8,128)(2,1)S(1)}, u32[]{:S(2)}, u32[]{:S(2)}) collective-permute-start(bf16[128,1024]{1,0:T(8,128)(2,1)S(1)} %fusion.4), channel_id=1, source_target_pairs={{0,18},{1,19},{2,16},{3,17},{4,22},{5,23},{6,20},{7,21},{8,26},{9,... | collective-permute-start | bytes 786440 | tf_op jit(solution)/shard_map/ppermute | solution.py:239
  13.2 13.0 %collective-permute-start.4 = (bf16[128,1152]{1,0:T(8,128)(2,1)S(1)}, bf16[128,1152]{1,0:T(8,128)(2,1)S(1)}, u32[]{:S(2)}, u32[]{:S(2)}) collective-permute-start(bf16[128,1152]{1,0:T(8,128)(2,1)S(1)} %pad_maximum_fusion.refs_0_), channel_id=1, source_target_pairs={{0,2},{1,3},{2,0},{3,1},{4,6},{5,7},{6,4},{7,5},{8,10},{9,11},{10,... | collective-permute-start | bytes 884744 | tf_op jit(solution)/shard_map/ppermute | solution.py:239
  18.1 8.6 %collective-permute-start.11 = (bf16[128,1024]{1,0:T(8,128)(2,1)S(1)}, bf16[128,1024]{1,0:T(8,128)(2,1)S(1)}, u32[]{:S(2)}, u32[]{:S(2)}) collective-permute-start(bf16[128,1024]{1,0:T(8,128)(2,1)S(1)} %slice.114), channel_id=1, source_target_pairs={{0,16},{1,17},{2,18},{3,19},{4,20},{5,21},{6,22},{7,23},{8,24},{9,... | collective-permute-start | bytes 786440 | tf_op jit(solution)/shard_map/ppermute | solution.py:239
  19.7 9.6 %collective-permute-start.13 = (bf16[128,1152]{1,0:T(8,128)(2,1)S(1)}, bf16[128,1152]{1,0:T(8,128)(2,1)S(1)}, u32[]{:S(2)}, u32[]{:S(2)}) collective-permute-start(bf16[128,1152]{1,0:T(8,128)(2,1)S(1)} %constant_dynamic-update-slice_fusion.refs_0_), channel_id=1, source_target_pairs={{0,2},{1,3},{2,0},{3,1},{4,6},{5,7},{6,4},{7,5},{8,10},{9,11},{10,... | collective-permute-start | bytes 884744 | tf_op jit(solution)/shard_map/ppermute | solution.py:239
  22.1 7.2 %collective-permute-start.1 = (bf16[128,1152]{1,0:T(8,128)(2,1)S(1)}, bf16[128,1152]{1,0:T(8,128)(2,1)S(1)}, u32[]{:S(2)}, u32[]{:S(2)}) collective-permute-start(bf16[128,1152]{1,0:T(8,128)(2,1)S(1)} %pad_maximum_fusion.refs_0_), channel_id=1, source_target_pairs={{0,1},{1,0},{2,3},{3,2},{4,5},{5,4},{6,7},{7,6},{8,9},{9,8},{10,11... | collective-permute-start | bytes 884744 | tf_op jit(solution)/shard_map/ppermute | solution.py:239
  29.4 11.5 %collective-permute-start.10 = (bf16[128,1152]{1,0:T(8,128)(2,1)S(1)}, bf16[128,1152]{1,0:T(8,128)(2,1)S(1)}, u32[]{:S(2)}, u32[]{:S(2)}) collective-permute-start(bf16[128,1152]{1,0:T(8,128)(2,1)S(1)} %constant_dynamic-update-slice_fusion.refs_0_), channel_id=1, source_target_pairs={{0,1},{1,0},{2,3},{3,2},{4,5},{5,4},{6,7},{7,6},{8,9},{9,8},{10,11... | collective-permute-start | bytes 884744 | tf_op jit(solution)/shard_map/ppermute | solution.py:239
  29.4 12.6 %collective-permute-start.12 = (bf16[128,1024]{1,0:T(8,128)(2,1)S(1)}, bf16[128,1024]{1,0:T(8,128)(2,1)S(1)}, u32[]{:S(2)}, u32[]{:S(2)}) collective-permute-start(bf16[128,1024]{1,0:T(8,128)(2,1)S(1)} %collective-permute-done.11.by_y.refs_2_), channel_id=1, source_target_pairs={{0,1},{1,0},{2,3},{3,2},{4,5},{5,4},{6,7},{7,6},{8,9},{9,8},{10,11... | collective-permute-start | bytes 786440 | tf_op jit(solution)/shard_map/ppermute | solution.py:239
  30.0 11.5 %collective-permute-start.15 = (bf16[64,1024]{1,0:T(8,128)(2,1)S(1)}, bf16[64,1024]{1,0:T(8,128)(2,1)S(1)}, u32[]{:S(2)}, u32[]{:S(2)}) collective-permute-start(bf16[64,1024]{1,0:T(8,128)(2,1)S(1)} %get-tuple-element.25), channel_id=1, source_target_pairs={{0,16},{1,17},{2,18},{3,19},{4,20},{5,21},{6,22},{7,23},{8,24},{9,... | collective-permute-start | bytes 393224 | tf_op jit(solution)/shard_map/ppermute | solution.py:239
  31.3 10.2 %collective-permute-start.16 = (bf16[64,1024]{1,0:T(8,128)(2,1)S(1)}, bf16[64,1024]{1,0:T(8,128)(2,1)S(1)}, u32[]{:S(2)}, u32[]{:S(2)}) collective-permute-start(bf16[64,1024]{1,0:T(8,128)(2,1)S(1)} %get-tuple-element.26), channel_id=1, source_target_pairs={{0,2},{1,3},{2,0},{3,1},{4,6},{5,7},{6,4},{7,5},{8,10},{9,11},{10,... | collective-permute-start | bytes 393224 | tf_op jit(solution)/shard_map/ppermute | solution.py:239
  32.8 10.1 %collective-permute-start.14 = (bf16[128,1152]{1,0:T(8,128)(2,1)S(1)}, bf16[128,1152]{1,0:T(8,128)(2,1)S(1)}, u32[]{:S(2)}, u32[]{:S(2)}) collective-permute-start(bf16[128,1152]{1,0:T(8,128)(2,1)S(1)} %collective-permute-done.13.by_x.refs_4_), channel_id=1, source_target_pairs={{0,1},{1,0},{2,3},{3,2},{4,5},{5,4},{6,7},{7,6},{8,9},{9,8},{10,11... | collective-permute-start | bytes 884744 | tf_op jit(solution)/shard_map/ppermute | solution.py:239
  40.9 7.9 %collective-permute-start.28 = (bf16[128,1024]{1,0:T(8,128)(2,1)S(1)}, bf16[128,1024]{1,0:T(8,128)(2,1)S(1)}, u32[]{:S(2)}, u32[]{:S(2)}) collective-permute-start(bf16[128,1024]{1,0:T(8,128)(2,1)S(1)} %get-tuple-element.36), channel_id=1, source_target_pairs={{0,1},{1,0},{2,3},{3,2},{4,5},{5,4},{6,7},{7,6},{8,9},{9,8},{10,11... | collective-permute-start | bytes 786440 | tf_op jit(solution)/shard_map/ppermute | solution.py:239
  41.9 18.0 %collective-permute-start.27 = (bf16[3,128,1024]{2,1,0:T(8,128)(2,1)S(1)}, bf16[3,128,1024]{2,1,0:T(8,128)(2,1)S(1)}, u32[]{:S(2)}, u32[]{:S(2)}) collective-permute-start(bf16[3,128,1024]{2,1,0:T(8,128)(2,1)S(1)} %get-tuple-element.34), channel_id=1, source_target_pairs={{0,1},{1,0},{2,3},{3,2},{4,5},{5,4},{6,7},{7,6},{8,9},{9,8},{10,11... | collective-permute-start | bytes 2359304 | tf_op jit(solution)/shard_map/ppermute | solution.py:239
  48.9 11.4 %collective-permute-start.30 = (bf16[64,1024]{1,0:T(8,128)(2,1)S(1)}, bf16[64,1024]{1,0:T(8,128)(2,1)S(1)}, u32[]{:S(2)}, u32[]{:S(2)}) collective-permute-start(bf16[64,1024]{1,0:T(8,128)(2,1)S(1)} %get-tuple-element.51), channel_id=1, source_target_pairs={{0,2},{1,3},{2,0},{3,1},{4,6},{5,7},{6,4},{7,5},{8,10},{9,11},{10,... | collective-permute-start | bytes 393224 | tf_op jit(solution)/shard_map/ppermute | solution.py:239
  49.5 10.8 %collective-permute-start.29 = (bf16[64,1024]{1,0:T(8,128)(2,1)S(1)}, bf16[64,1024]{1,0:T(8,128)(2,1)S(1)}, u32[]{:S(2)}, u32[]{:S(2)}) collective-permute-start(bf16[64,1024]{1,0:T(8,128)(2,1)S(1)} %get-tuple-element.52), channel_id=1, source_target_pairs={{0,16},{1,17},{2,18},{3,19},{4,20},{5,21},{6,22},{7,23},{8,24},{9,... | collective-permute-start | bytes 393224 | tf_op jit(solution)/shard_map/ppermute | solution.py:239
  50.2 7.3 %collective-permute-start.22 = (bf16[64,1024]{1,0:T(8,128)(2,1)S(1)}, bf16[64,1024]{1,0:T(8,128)(2,1)S(1)}, u32[]{:S(2)}, u32[]{:S(2)}) collective-permute-start(bf16[64,1024]{1,0:T(8,128)(2,1)S(1)} %get-tuple-element.49), channel_id=1, source_target_pairs={{0,2},{1,3},{2,0},{3,1},{4,6},{5,7},{6,4},{7,5},{8,10},{9,11},{10,... | collective-permute-start | bytes 393224 | tf_op jit(solution)/shard_map/ppermute | solution.py:239
  57.9 7.6 %collective-permute-start.23 = (bf16[128,1024]{1,0:T(8,128)(2,1)S(1)}, bf16[128,1024]{1,0:T(8,128)(2,1)S(1)}, u32[]{:S(2)}, u32[]{:S(2)}) collective-permute-start(bf16[128,1024]{1,0:T(8,128)(2,1)S(1)} %get-tuple-element.31), channel_id=1, source_target_pairs={{0,2},{1,3},{2,0},{3,1},{4,6},{5,7},{6,4},{7,5},{8,10},{9,11},{10,... | collective-permute-start | bytes 786440 | tf_op jit(solution)/shard_map/ppermute | solution.py:239
  59.4 7.2 %collective-permute-start.24 = (bf16[128,1024]{1,0:T(8,128)(2,1)S(1)}, bf16[128,1024]{1,0:T(8,128)(2,1)S(1)}, u32[]{:S(2)}, u32[]{:S(2)}) collective-permute-start(bf16[128,1024]{1,0:T(8,128)(2,1)S(1)} %get-tuple-element.32), channel_id=1, source_target_pairs={{0,16},{1,17},{2,18},{3,19},{4,20},{5,21},{6,22},{7,23},{8,24},{9,... | collective-permute-start | bytes 786440 | tf_op jit(solution)/shard_map/ppermute | solution.py:239
  67.9 8.9 %collective-permute-start.26 = (bf16[64,1024]{1,0:T(8,128)(2,1)S(1)}, bf16[64,1024]{1,0:T(8,128)(2,1)S(1)}, u32[]{:S(2)}, u32[]{:S(2)}) collective-permute-start(bf16[64,1024]{1,0:T(8,128)(2,1)S(1)} %get-tuple-element.48), channel_id=1, source_target_pairs={{0,12},{1,13},{2,14},{3,15},{4,8},{5,9},{6,10},{7,11},{8,4},{9,5},... | collective-permute-start | bytes 393224 | tf_op jit(solution)/shard_map/ppermute | solution.py:239
  73.5 8.2 %collective-permute-start.25 = (bf16[64,1024]{1,0:T(8,128)(2,1)S(1)}, bf16[64,1024]{1,0:T(8,128)(2,1)S(1)}, u32[]{:S(2)}, u32[]{:S(2)}) collective-permute-start(bf16[64,1024]{1,0:T(8,128)(2,1)S(1)} %get-tuple-element.47), channel_id=1, source_target_pairs={{0,8},{1,9},{2,10},{3,11},{4,12},{5,13},{6,14},{7,15},{8,0},{9,1},... | collective-permute-start | bytes 393224 | tf_op jit(solution)/shard_map/ppermute | solution.py:239
  73.6 8.1 %collective-permute-start.33 = (bf16[64,1024]{1,0:T(8,128)(2,1)S(1)}, bf16[64,1024]{1,0:T(8,128)(2,1)S(1)}, u32[]{:S(2)}, u32[]{:S(2)}) collective-permute-start(bf16[64,1024]{1,0:T(8,128)(2,1)S(1)} %slice.132), channel_id=1, source_target_pairs={{0,4},{1,5},{2,6},{3,7},{4,0},{5,1},{6,2},{7,3},{8,12},{9,13},{10,... | collective-permute-start | bytes 393224 | tf_op jit(solution)/shard_map/ppermute | solution.py:239
  (10 other events, 42.2 us)

commit v5 on v4

--- a/solution.py
+++ b/solution.py
@@ -293,7 +293,7 @@
         for_x, for_y = after((for_x, for_y), arrived)
         arrived = send(for_x, x=1), send(for_y, y=1)
         mine = add(own, *arrived, *direct)
-        for k in range(count):
+        for k in reversed(range(count)):
             piece = mine[k * block : (k + 1) * block]
             back.append(send(piece, steps=i * count + k) if i or k else piece)
     return add(*back)

time: 82.6 us -> 81.4 us (0.985)
  waiting for transfers between devices: 33.1 us -> 31.9 us
    ppermute x34, waiting for transfers between devices: 33.1 us -> 31.9 us  [send(): return lax.ppermute(array, PAIR, pairs)]
where the time goes in v5:
time: 81.4 us; the launch traced here: 81.2 us
  starting transfers between devices  32.7 us (40%)
  waiting for transfers between devices  31.9 us (39%)
  Pallas kernels  14.1 us (17%)
  other arithmetic  2.05 us (3%)
    ppermute x34, starting transfers between devices, send(): return lax.ppermute(array, PAIR, pairs)  32.7 us
    ppermute x34, waiting for transfers between devices, send(): return lax.ppermute(array, PAIR, pairs)  31.9 us
    pallas_call x2, Pallas kernels, run_experts(): pl.pallas_call(functools.partial(experts_kernel, first, counts, block, ro...  13.1 us
    convert_element_type x9, other arithmetic, add(): functools.reduce(lambda a, b: a + b, [t.astype(F32) for t in terms])  1.85 us
  transfers between devices with their start and end apart: 34, of which 13 were waited for; matrix products, arithmetic and copies ran while one was open for 2% of the time, Pallas kernels for 16%

profile of v5, /device:TPU:0, one launch (start us, length us, event | category | flops | bytes accessed | tf_op | source)
XLA Modules:
  0.0 81.2 jit_solution(16103086745408942210)
XLA Ops:
  1.0 3.1 %collective-permute-start = (bf16[64,1152]{1,0:T(8,128)(2,1)S(1)}, bf16[64,1152]{1,0:T(8,128)(2,1)S(1)}, u32[]{:S(2)}, u32[]{:S(2)}) collective-permute-start(bf16[64,1152]{1,0:T(8,128)(2,1)S(1)} %shard_map.64), channel_id=1, source_target_pairs={{0,4},{1,5},{2,6},{3,7},{4,0},{5,1},{6,2},{7,3},{8,12},{9,13},{10,... | collective-permute-start | bytes 442376 | tf_op jit(solution)/shard_map/ppermute | solution.py:239
  4.1 2.6 %collective-permute-start.8 = (bf16[64,1152]{1,0:T(8,128)(2,1)S(1)}, bf16[64,1152]{1,0:T(8,128)(2,1)S(1)}, u32[]{:S(2)}, u32[]{:S(2)}) collective-permute-start(bf16[64,1152]{1,0:T(8,128)(2,1)S(1)} %shard_map.64), channel_id=1, source_target_pairs={{0,8},{1,9},{2,10},{3,11},{4,12},{5,13},{6,14},{7,15},{8,0},{9,1},... | collective-permute-start | bytes 442376 | tf_op jit(solution)/shard_map/ppermute | solution.py:239
  6.7 3.3 %collective-permute-done = bf16[64,1152]{1,0:T(8,128)(2,1)S(1)} collective-permute-done((bf16[64,1152]{1,0:T(8,128)(2,1)S(1)}, bf16[64,1152]{1,0:T(8,128)(2,1)S(1)}, u32[]{:S(2)}, u32[]{:S(2)}) %collective-permute-start) | collective-permute-done | bytes 147488 | tf_op jit(solution)/shard_map/ppermute | solution.py:239
  9.9 1.8 %collective-permute-start.2 = (bf16[128,1024]{1,0:T(8,128)(2,1)S(1)}, bf16[128,1024]{1,0:T(8,128)(2,1)S(1)}, u32[]{:S(2)}, u32[]{:S(2)}) collective-permute-start(bf16[128,1024]{1,0:T(8,128)(2,1)S(1)} %fusion.4), channel_id=1, source_target_pairs={{0,16},{1,17},{2,18},{3,19},{4,20},{5,21},{6,22},{7,23},{8,24},{9,... | collective-permute-start | bytes 786440 | tf_op jit(solution)/shard_map/ppermute | solution.py:239
  11.7 1.4 %collective-permute-start.6 = (bf16[128,1024]{1,0:T(8,128)(2,1)S(1)}, bf16[128,1024]{1,0:T(8,128)(2,1)S(1)}, u32[]{:S(2)}, u32[]{:S(2)}) collective-permute-start(bf16[128,1024]{1,0:T(8,128)(2,1)S(1)} %fusion.4), channel_id=1, source_target_pairs={{0,18},{1,19},{2,16},{3,17},{4,22},{5,23},{6,20},{7,21},{8,26},{9,... | collective-permute-start | bytes 786440 | tf_op jit(solution)/shard_map/ppermute | solution.py:239
  13.6 4.5 %collective-permute-done.8 = bf16[64,1152]{1,0:T(8,128)(2,1)S(1)} collective-permute-done((bf16[64,1152]{1,0:T(8,128)(2,1)S(1)}, bf16[64,1152]{1,0:T(8,128)(2,1)S(1)}, u32[]{:S(2)}, u32[]{:S(2)}) %collective-permute-start.8) | collective-permute-done | bytes 147488 | tf_op jit(solution)/shard_map/ppermute | solution.py:239
  18.1 1.6 %collective-permute-start.11 = (bf16[128,1024]{1,0:T(8,128)(2,1)S(1)}, bf16[128,1024]{1,0:T(8,128)(2,1)S(1)}, u32[]{:S(2)}, u32[]{:S(2)}) collective-permute-start(bf16[128,1024]{1,0:T(8,128)(2,1)S(1)} %slice.114), channel_id=1, source_target_pairs={{0,16},{1,17},{2,18},{3,19},{4,20},{5,21},{6,22},{7,23},{8,24},{9,... | collective-permute-start | bytes 786440 | tf_op jit(solution)/shard_map/ppermute | solution.py:239
  19.7 1.5 %collective-permute-start.13 = (bf16[128,1152]{1,0:T(8,128)(2,1)S(1)}, bf16[128,1152]{1,0:T(8,128)(2,1)S(1)}, u32[]{:S(2)}, u32[]{:S(2)}) collective-permute-start(bf16[128,1152]{1,0:T(8,128)(2,1)S(1)} %constant_dynamic-update-slice_fusion.refs_0_), channel_id=1, source_target_pairs={{0,2},{1,3},{2,0},{3,1},{4,6},{5,7},{6,4},{7,5},{8,10},{9,11},{10,... | collective-permute-start | bytes 884744 | tf_op jit(solution)/shard_map/ppermute | solution.py:239
  22.1 4.1 %collective-permute-done.4.refs_4_ = bf16[128,1152]{1,0:T(8,128)(2,1)S(1)} collective-permute-done((bf16[128,1152]{1,0:T(8,128)(2,1)S(1)}, bf16[128,1152]{1,0:T(8,128)(2,1)S(1)}, u32[]{:S(2)}, u32[]{:S(2)}) %collective-permute-start.4) | collective-permute-done | bytes 294944 | tf_op jit(solution)/shard_map/ppermute | solution.py:239
  26.8 2.6 %collective-permute-done.13.by_x.refs_4_ = bf16[128,1152]{1,0:T(8,128)(2,1)S(1)} collective-permute-done((bf16[128,1152]{1,0:T(8,128)(2,1)S(1)}, bf16[128,1152]{1,0:T(8,128)(2,1)S(1)}, u32[]{:S(2)}, u32[]{:S(2)}) %collective-permute-start.13) | collective-permute-done | bytes 294944 | tf_op jit(solution)/shard_map/ppermute | solution.py:239
  30.0 1.4 %collective-permute-start.15 = (bf16[64,1024]{1,0:T(8,128)(2,1)S(1)}, bf16[64,1024]{1,0:T(8,128)(2,1)S(1)}, u32[]{:S(2)}, u32[]{:S(2)}) collective-permute-start(bf16[64,1024]{1,0:T(8,128)(2,1)S(1)} %get-tuple-element.25), channel_id=1, source_target_pairs={{0,16},{1,17},{2,18},{3,19},{4,20},{5,21},{6,22},{7,23},{8,24},{9,... | collective-permute-start | bytes 393224 | tf_op jit(solution)/shard_map/ppermute | solution.py:239
  31.3 1.5 %collective-permute-start.16 = (bf16[64,1024]{1,0:T(8,128)(2,1)S(1)}, bf16[64,1024]{1,0:T(8,128)(2,1)S(1)}, u32[]{:S(2)}, u32[]{:S(2)}) collective-permute-start(bf16[64,1024]{1,0:T(8,128)(2,1)S(1)} %get-tuple-element.26), channel_id=1, source_target_pairs={{0,2},{1,3},{2,0},{3,1},{4,6},{5,7},{6,4},{7,5},{8,10},{9,11},{10,... | collective-permute-start | bytes 393224 | tf_op jit(solution)/shard_map/ppermute | solution.py:239
  32.9 7.9 %shard_map.65 = (bf16[128,1024]{1,0:T(8,128)(2,1)S(1)}, bf16[128,1024]{1,0:T(8,128)(2,1)S(1)}, bf16[3,128,1024]{2,1,0:T(8,128)(2,1)S(1)}, bf16[3,128,1024]{2,1,0...) custom-call(s32[2]{0:T(128)S(1)} %pad_add_fusion.places, ...), custom_call_target="tpu_custom_call" | custom-call | flops 512 | bytes 512 | tf_op jit(solution)/shard_map/pallas_call | solution.py:182
  43.0 5.2 %shard_map.67 = (bf16[128,1024]{1,0:T(8,128)(2,1)S(1)}, bf16[128,1024]{1,0:T(8,128)(2,1)S(1)}, bf16[3,128,1024]{2,1,0:T(8,128)(2,1)S(1)}, bf16[3,128,1024]{2,1,0:T(8,128)(2,1)S(1)}) custom-call(s32[2]{0:T(128)S(1)} %pad_add_fusion.places, bf16[2,2048,512]{2,1,0:T(8,128)(2,1)S(1)} %get-tuple-element.22.gate_in, ...), custom_call_target="tpu_custom_call" | custom-call | flops 512 | bytes 512 | tf_op jit(solution)/shard_map/pallas_call | solution.py:182
  50.2 1.4 %collective-permute-start.22 = (bf16[64,1024]{1,0:T(8,128)(2,1)S(1)}, bf16[64,1024]{1,0:T(8,128)(2,1)S(1)}, u32[]{:S(2)}, u32[]{:S(2)}) collective-permute-start(bf16[64,1024]{1,0:T(8,128)(2,1)S(1)} %get-tuple-element.49), channel_id=1, source_target_pairs={{0,2},{1,3},{2,0},{3,1},{4,6},{5,7},{6,4},{7,5},{8,10},{9,11},{10,... | collective-permute-start | bytes 393224 | tf_op jit(solution)/shard_map/ppermute | solution.py:239
  51.6 1.5 %collective-permute-start.21 = (bf16[64,1024]{1,0:T(8,128)(2,1)S(1)}, bf16[64,1024]{1,0:T(8,128)(2,1)S(1)}, u32[]{:S(2)}, u32[]{:S(2)}) collective-permute-start(bf16[64,1024]{1,0:T(8,128)(2,1)S(1)} %get-tuple-element.50), channel_id=1, source_target_pairs={{0,16},{1,17},{2,18},{3,19},{4,20},{5,21},{6,22},{7,23},{8,24},{9,... | collective-permute-start | bytes 393224 | tf_op jit(solution)/shard_map/ppermute | solution.py:239
  53.5 4.0 %collective-permute-done.22 = bf16[64,1024]{1,0:T(8,128)(2,1)S(1)} collective-permute-done((bf16[64,1024]{1,0:T(8,128)(2,1)S(1)}, bf16[64,1024]{1,0:T(8,128)(2,1)S(1)}, u32[]{:S(2)}, u32[]{:S(2)}) %collective-permute-start.22) | collective-permute-done | bytes 131104 | tf_op jit(solution)/shard_map/ppermute | solution.py:239
  57.9 1.5 %collective-permute-start.23 = (bf16[128,1024]{1,0:T(8,128)(2,1)S(1)}, bf16[128,1024]{1,0:T(8,128)(2,1)S(1)}, u32[]{:S(2)}, u32[]{:S(2)}) collective-permute-start(bf16[128,1024]{1,0:T(8,128)(2,1)S(1)} %get-tuple-element.31), channel_id=1, source_target_pairs={{0,2},{1,3},{2,0},{3,1},{4,6},{5,7},{6,4},{7,5},{8,10},{9,11},{10,... | collective-permute-start | bytes 786440 | tf_op jit(solution)/shard_map/ppermute | solution.py:239
  60.4 5.0 %collective-permute-done.23 = bf16[128,1024]{1,0:T(8,128)(2,1)S(1)} collective-permute-done((bf16[128,1024]{1,0:T(8,128)(2,1)S(1)}, bf16[128,1024]{1,0:T(8,128)(2,1)S(1)}, u32[]{:S(2)}, u32[]{:S(2)}) %collective-permute-start.23) | collective-permute-done | bytes 262176 | tf_op jit(solution)/shard_map/ppermute | solution.py:239
  65.4 1.1 %collective-permute-done.24 = bf16[128,1024]{1,0:T(8,128)(2,1)S(1)} collective-permute-done((bf16[128,1024]{1,0:T(8,128)(2,1)S(1)}, bf16[128,1024]{1,0:T(8,128)(2,1)S(1)}, u32[]{:S(2)}, u32[]{:S(2)}) %collective-permute-start.24) | collective-permute-done | bytes 262176 | tf_op jit(solution)/shard_map/ppermute | solution.py:239
  67.9 3.2 %collective-permute-start.26 = (bf16[64,1024]{1,0:T(8,128)(2,1)S(1)}, bf16[64,1024]{1,0:T(8,128)(2,1)S(1)}, u32[]{:S(2)}, u32[]{:S(2)}) collective-permute-start(bf16[64,1024]{1,0:T(8,128)(2,1)S(1)} %get-tuple-element.48), channel_id=1, source_target_pairs={{0,8},{1,9},{2,10},{3,11},{4,12},{5,13},{6,14},{7,15},{8,0},{9,1},... | collective-permute-start | bytes 393224 | tf_op jit(solution)/shard_map/ppermute | solution.py:239
  71.0 2.5 %collective-permute-start.25 = (bf16[64,1024]{1,0:T(8,128)(2,1)S(1)}, bf16[64,1024]{1,0:T(8,128)(2,1)S(1)}, u32[]{:S(2)}, u32[]{:S(2)}) collective-permute-start(bf16[64,1024]{1,0:T(8,128)(2,1)S(1)} %get-tuple-element.47), channel_id=1, source_target_pairs={{0,12},{1,13},{2,14},{3,15},{4,8},{5,9},{6,10},{7,11},{8,4},{9,5},... | collective-permute-start | bytes 393224 | tf_op jit(solution)/shard_map/ppermute | solution.py:239
  73.7 1.6 %collective-permute-start.33 = (bf16[64,1024]{1,0:T(8,128)(2,1)S(1)}, bf16[64,1024]{1,0:T(8,128)(2,1)S(1)}, u32[]{:S(2)}, u32[]{:S(2)}) collective-permute-start(bf16[64,1024]{1,0:T(8,128)(2,1)S(1)} %slice.131), channel_id=1, source_target_pairs={{0,4},{1,5},{2,6},{3,7},{4,0},{5,1},{6,2},{7,3},{8,12},{9,13},{10,... | collective-permute-start | bytes 393224 | tf_op jit(solution)/shard_map/ppermute | solution.py:239
  75.3 4.9 %collective-permute-done.26 = bf16[64,1024]{1,0:T(8,128)(2,1)S(1)} collective-permute-done((bf16[64,1024]{1,0:T(8,128)(2,1)S(1)}, bf16[64,1024]{1,0:T(8,128)(2,1)S(1)}, u32[]{:S(2)}, u32[]{:S(2)}) %collective-permute-start.26) | collective-permute-done | bytes 131104 | tf_op jit(solution)/shard_map/ppermute | solution.py:239
  (71 shorter events, 11.8 us)
Async XLA Ops:
  1.0 8.9 %collective-permute-start = (bf16[64,1152]{1,0:T(8,128)(2,1)S(1)}, bf16[64,1152]{1,0:T(8,128)(2,1)S(1)}, u32[]{:S(2)}, u32[]{:S(2)}) collective-permute-start(bf16[64,1152]{1,0:T(8,128)(2,1)S(1)} %shard_map.64), channel_id=1, source_target_pairs={{0,4},{1,5},{2,6},{3,7},{4,0},{5,1},{6,2},{7,3},{8,12},{9,13},{10,... | collective-permute-start | bytes 442376 | tf_op jit(solution)/shard_map/ppermute | solution.py:239
  4.1 14.0 %collective-permute-start.8 = (bf16[64,1152]{1,0:T(8,128)(2,1)S(1)}, bf16[64,1152]{1,0:T(8,128)(2,1)S(1)}, u32[]{:S(2)}, u32[]{:S(2)}) collective-permute-start(bf16[64,1152]{1,0:T(8,128)(2,1)S(1)} %shard_map.64), channel_id=1, source_target_pairs={{0,8},{1,9},{2,10},{3,11},{4,12},{5,13},{6,14},{7,15},{8,0},{9,1},... | collective-permute-start | bytes 442376 | tf_op jit(solution)/shard_map/ppermute | solution.py:239
  6.6 11.4 %collective-permute-start.9 = (bf16[64,1152]{1,0:T(8,128)(2,1)S(1)}, bf16[64,1152]{1,0:T(8,128)(2,1)S(1)}, u32[]{:S(2)}, u32[]{:S(2)}) collective-permute-start(bf16[64,1152]{1,0:T(8,128)(2,1)S(1)} %shard_map.64), channel_id=1, source_target_pairs={{0,12},{1,13},{2,14},{3,15},{4,8},{5,9},{6,10},{7,11},{8,4},{9,5},... | collective-permute-start | bytes 442376 | tf_op jit(solution)/shard_map/ppermute | solution.py:239
  9.9 12.2 %collective-permute-start.2 = (bf16[128,1024]{1,0:T(8,128)(2,1)S(1)}, bf16[128,1024]{1,0:T(8,128)(2,1)S(1)}, u32[]{:S(2)}, u32[]{:S(2)}) collective-permute-start(bf16[128,1024]{1,0:T(8,128)(2,1)S(1)} %fusion.4), channel_id=1, source_target_pairs={{0,16},{1,17},{2,18},{3,19},{4,20},{5,21},{6,22},{7,23},{8,24},{9,... | collective-permute-start | bytes 786440 | tf_op jit(solution)/shard_map/ppermute | solution.py:239
  11.7 14.5 %collective-permute-start.6 = (bf16[128,1024]{1,0:T(8,128)(2,1)S(1)}, bf16[128,1024]{1,0:T(8,128)(2,1)S(1)}, u32[]{:S(2)}, u32[]{:S(2)}) collective-permute-start(bf16[128,1024]{1,0:T(8,128)(2,1)S(1)} %fusion.4), channel_id=1, source_target_pairs={{0,18},{1,19},{2,16},{3,17},{4,22},{5,23},{6,20},{7,21},{8,26},{9,... | collective-permute-start | bytes 786440 | tf_op jit(solution)/shard_map/ppermute | solution.py:239
  13.2 13.0 %collective-permute-start.4 = (bf16[128,1152]{1,0:T(8,128)(2,1)S(1)}, bf16[128,1152]{1,0:T(8,128)(2,1)S(1)}, u32[]{:S(2)}, u32[]{:S(2)}) collective-permute-start(bf16[128,1152]{1,0:T(8,128)(2,1)S(1)} %pad_maximum_fusion.refs_0_), channel_id=1, source_target_pairs={{0,2},{1,3},{2,0},{3,1},{4,6},{5,7},{6,4},{7,5},{8,10},{9,11},{10,... | collective-permute-start | bytes 884744 | tf_op jit(solution)/shard_map/ppermute | solution.py:239
  18.1 8.6 %collective-permute-start.11 = (bf16[128,1024]{1,0:T(8,128)(2,1)S(1)}, bf16[128,1024]{1,0:T(8,128)(2,1)S(1)}, u32[]{:S(2)}, u32[]{:S(2)}) collective-permute-start(bf16[128,1024]{1,0:T(8,128)(2,1)S(1)} %slice.114), channel_id=1, source_target_pairs={{0,16},{1,17},{2,18},{3,19},{4,20},{5,21},{6,22},{7,23},{8,24},{9,... | collective-permute-start | bytes 786440 | tf_op jit(solution)/shard_map/ppermute | solution.py:239
  19.7 9.6 %collective-permute-start.13 = (bf16[128,1152]{1,0:T(8,128)(2,1)S(1)}, bf16[128,1152]{1,0:T(8,128)(2,1)S(1)}, u32[]{:S(2)}, u32[]{:S(2)}) collective-permute-start(bf16[128,1152]{1,0:T(8,128)(2,1)S(1)} %constant_dynamic-update-slice_fusion.refs_0_), channel_id=1, source_target_pairs={{0,2},{1,3},{2,0},{3,1},{4,6},{5,7},{6,4},{7,5},{8,10},{9,11},{10,... | collective-permute-start | bytes 884744 | tf_op jit(solution)/shard_map/ppermute | solution.py:239
  22.1 7.2 %collective-permute-start.1 = (bf16[128,1152]{1,0:T(8,128)(2,1)S(1)}, bf16[128,1152]{1,0:T(8,128)(2,1)S(1)}, u32[]{:S(2)}, u32[]{:S(2)}) collective-permute-start(bf16[128,1152]{1,0:T(8,128)(2,1)S(1)} %pad_maximum_fusion.refs_0_), channel_id=1, source_target_pairs={{0,1},{1,0},{2,3},{3,2},{4,5},{5,4},{6,7},{7,6},{8,9},{9,8},{10,11... | collective-permute-start | bytes 884744 | tf_op jit(solution)/shard_map/ppermute | solution.py:239
  29.4 11.5 %collective-permute-start.10 = (bf16[128,1152]{1,0:T(8,128)(2,1)S(1)}, bf16[128,1152]{1,0:T(8,128)(2,1)S(1)}, u32[]{:S(2)}, u32[]{:S(2)}) collective-permute-start(bf16[128,1152]{1,0:T(8,128)(2,1)S(1)} %constant_dynamic-update-slice_fusion.refs_0_), channel_id=1, source_target_pairs={{0,1},{1,0},{2,3},{3,2},{4,5},{5,4},{6,7},{7,6},{8,9},{9,8},{10,11... | collective-permute-start | bytes 884744 | tf_op jit(solution)/shard_map/ppermute | solution.py:239
  29.4 12.6 %collective-permute-start.12 = (bf16[128,1024]{1,0:T(8,128)(2,1)S(1)}, bf16[128,1024]{1,0:T(8,128)(2,1)S(1)}, u32[]{:S(2)}, u32[]{:S(2)}) collective-permute-start(bf16[128,1024]{1,0:T(8,128)(2,1)S(1)} %collective-permute-done.11.by_y.refs_2_), channel_id=1, source_target_pairs={{0,1},{1,0},{2,3},{3,2},{4,5},{5,4},{6,7},{7,6},{8,9},{9,8},{10,11... | collective-permute-start | bytes 786440 | tf_op jit(solution)/shard_map/ppermute | solution.py:239
  30.0 11.5 %collective-permute-start.15 = (bf16[64,1024]{1,0:T(8,128)(2,1)S(1)}, bf16[64,1024]{1,0:T(8,128)(2,1)S(1)}, u32[]{:S(2)}, u32[]{:S(2)}) collective-permute-start(bf16[64,1024]{1,0:T(8,128)(2,1)S(1)} %get-tuple-element.25), channel_id=1, source_target_pairs={{0,16},{1,17},{2,18},{3,19},{4,20},{5,21},{6,22},{7,23},{8,24},{9,... | collective-permute-start | bytes 393224 | tf_op jit(solution)/shard_map/ppermute | solution.py:239
  31.3 10.2 %collective-permute-start.16 = (bf16[64,1024]{1,0:T(8,128)(2,1)S(1)}, bf16[64,1024]{1,0:T(8,128)(2,1)S(1)}, u32[]{:S(2)}, u32[]{:S(2)}) collective-permute-start(bf16[64,1024]{1,0:T(8,128)(2,1)S(1)} %get-tuple-element.26), channel_id=1, source_target_pairs={{0,2},{1,3},{2,0},{3,1},{4,6},{5,7},{6,4},{7,5},{8,10},{9,11},{10,... | collective-permute-start | bytes 393224 | tf_op jit(solution)/shard_map/ppermute | solution.py:239
  32.8 10.1 %collective-permute-start.14 = (bf16[128,1152]{1,0:T(8,128)(2,1)S(1)}, bf16[128,1152]{1,0:T(8,128)(2,1)S(1)}, u32[]{:S(2)}, u32[]{:S(2)}) collective-permute-start(bf16[128,1152]{1,0:T(8,128)(2,1)S(1)} %collective-permute-done.13.by_x.refs_4_), channel_id=1, source_target_pairs={{0,1},{1,0},{2,3},{3,2},{4,5},{5,4},{6,7},{7,6},{8,9},{9,8},{10,11... | collective-permute-start | bytes 884744 | tf_op jit(solution)/shard_map/ppermute | solution.py:239
  40.9 7.9 %collective-permute-start.28 = (bf16[128,1024]{1,0:T(8,128)(2,1)S(1)}, bf16[128,1024]{1,0:T(8,128)(2,1)S(1)}, u32[]{:S(2)}, u32[]{:S(2)}) collective-permute-start(bf16[128,1024]{1,0:T(8,128)(2,1)S(1)} %get-tuple-element.36), channel_id=1, source_target_pairs={{0,1},{1,0},{2,3},{3,2},{4,5},{5,4},{6,7},{7,6},{8,9},{9,8},{10,11... | collective-permute-start | bytes 786440 | tf_op jit(solution)/shard_map/ppermute | solution.py:239
  41.9 18.0 %collective-permute-start.27 = (bf16[3,128,1024]{2,1,0:T(8,128)(2,1)S(1)}, bf16[3,128,1024]{2,1,0:T(8,128)(2,1)S(1)}, u32[]{:S(2)}, u32[]{:S(2)}) collective-permute-start(bf16[3,128,1024]{2,1,0:T(8,128)(2,1)S(1)} %get-tuple-element.34), channel_id=1, source_target_pairs={{0,1},{1,0},{2,3},{3,2},{4,5},{5,4},{6,7},{7,6},{8,9},{9,8},{10,11... | collective-permute-start | bytes 2359304 | tf_op jit(solution)/shard_map/ppermute | solution.py:239
  48.9 11.4 %collective-permute-start.30 = (bf16[64,1024]{1,0:T(8,128)(2,1)S(1)}, bf16[64,1024]{1,0:T(8,128)(2,1)S(1)}, u32[]{:S(2)}, u32[]{:S(2)}) collective-permute-start(bf16[64,1024]{1,0:T(8,128)(2,1)S(1)} %get-tuple-element.51), channel_id=1, source_target_pairs={{0,2},{1,3},{2,0},{3,1},{4,6},{5,7},{6,4},{7,5},{8,10},{9,11},{10,... | collective-permute-start | bytes 393224 | tf_op jit(solution)/shard_map/ppermute | solution.py:239
  49.5 10.8 %collective-permute-start.29 = (bf16[64,1024]{1,0:T(8,128)(2,1)S(1)}, bf16[64,1024]{1,0:T(8,128)(2,1)S(1)}, u32[]{:S(2)}, u32[]{:S(2)}) collective-permute-start(bf16[64,1024]{1,0:T(8,128)(2,1)S(1)} %get-tuple-element.52), channel_id=1, source_target_pairs={{0,16},{1,17},{2,18},{3,19},{4,20},{5,21},{6,22},{7,23},{8,24},{9,... | collective-permute-start | bytes 393224 | tf_op jit(solution)/shard_map/ppermute | solution.py:239
  50.2 7.3 %collective-permute-start.22 = (bf16[64,1024]{1,0:T(8,128)(2,1)S(1)}, bf16[64,1024]{1,0:T(8,128)(2,1)S(1)}, u32[]{:S(2)}, u32[]{:S(2)}) collective-permute-start(bf16[64,1024]{1,0:T(8,128)(2,1)S(1)} %get-tuple-element.49), channel_id=1, source_target_pairs={{0,2},{1,3},{2,0},{3,1},{4,6},{5,7},{6,4},{7,5},{8,10},{9,11},{10,... | collective-permute-start | bytes 393224 | tf_op jit(solution)/shard_map/ppermute | solution.py:239
  57.9 7.6 %collective-permute-start.23 = (bf16[128,1024]{1,0:T(8,128)(2,1)S(1)}, bf16[128,1024]{1,0:T(8,128)(2,1)S(1)}, u32[]{:S(2)}, u32[]{:S(2)}) collective-permute-start(bf16[128,1024]{1,0:T(8,128)(2,1)S(1)} %get-tuple-element.31), channel_id=1, source_target_pairs={{0,2},{1,3},{2,0},{3,1},{4,6},{5,7},{6,4},{7,5},{8,10},{9,11},{10,... | collective-permute-start | bytes 786440 | tf_op jit(solution)/shard_map/ppermute | solution.py:239
  59.4 7.2 %collective-permute-start.24 = (bf16[128,1024]{1,0:T(8,128)(2,1)S(1)}, bf16[128,1024]{1,0:T(8,128)(2,1)S(1)}, u32[]{:S(2)}, u32[]{:S(2)}) collective-permute-start(bf16[128,1024]{1,0:T(8,128)(2,1)S(1)} %get-tuple-element.32), channel_id=1, source_target_pairs={{0,16},{1,17},{2,18},{3,19},{4,20},{5,21},{6,22},{7,23},{8,24},{9,... | collective-permute-start | bytes 786440 | tf_op jit(solution)/shard_map/ppermute | solution.py:239
  66.6 7.0 %collective-permute-start.32 = (bf16[128,1024]{1,0:T(8,128)(2,1)S(1)}, bf16[128,1024]{1,0:T(8,128)(2,1)S(1)}, u32[]{:S(2)}, u32[]{:S(2)}) collective-permute-start(bf16[128,1024]{1,0:T(8,128)(2,1)S(1)} %get-tuple-element.38), channel_id=1, source_target_pairs={{0,16},{1,17},{2,18},{3,19},{4,20},{5,21},{6,22},{7,23},{8,24},{9,... | collective-permute-start | bytes 786440 | tf_op jit(solution)/shard_map/ppermute | solution.py:239
  67.9 12.3 %collective-permute-start.26 = (bf16[64,1024]{1,0:T(8,128)(2,1)S(1)}, bf16[64,1024]{1,0:T(8,128)(2,1)S(1)}, u32[]{:S(2)}, u32[]{:S(2)}) collective-permute-start(bf16[64,1024]{1,0:T(8,128)(2,1)S(1)} %get-tuple-element.48), channel_id=1, source_target_pairs={{0,8},{1,9},{2,10},{3,11},{4,12},{5,13},{6,14},{7,15},{8,0},{9,1},... | collective-permute-start | bytes 393224 | tf_op jit(solution)/shard_map/ppermute | solution.py:239
  71.0 9.2 %collective-permute-start.25 = (bf16[64,1024]{1,0:T(8,128)(2,1)S(1)}, bf16[64,1024]{1,0:T(8,128)(2,1)S(1)}, u32[]{:S(2)}, u32[]{:S(2)}) collective-permute-start(bf16[64,1024]{1,0:T(8,128)(2,1)S(1)} %get-tuple-element.47), channel_id=1, source_target_pairs={{0,12},{1,13},{2,14},{3,15},{4,8},{5,9},{6,10},{7,11},{8,4},{9,5},... | collective-permute-start | bytes 393224 | tf_op jit(solution)/shard_map/ppermute | solution.py:239
  (10 other events, 42.2 us)

commit v6 on v5

--- a/solution.py
+++ b/solution.py
@@ -200,25 +200,6 @@
     )(places, *operands)
 
 
-def cut_kernel(by_x, by_y, *refs):
-    out_x, out_y = refs[-2:]
-    half = out_x.shape[0]
-    out_x[...] = by_x[:half, : out_x.shape[1]]
-    out_y[...] = by_y[half:]
-
-
-def cut(by_x, by_y, behind):
-    half = jax.ShapeDtypeStruct((by_y.shape[0] // 2, by_y.shape[1]), BF16)
-    return pl.pallas_call(
-        cut_kernel,
-        in_specs=[VMEM_SPEC] * 2 + [pl.BlockSpec(memory_space=pl.ANY)] * len(behind),
-        out_specs=[VMEM_SPEC] * 2,
-        out_shape=[half, half],
-        compiler_params=pltpu.CompilerParams(vmem_limit_bytes=2 * MIB),
-        cost_estimate=pl.CostEstimate(flops=1, bytes_accessed=1, transcendentals=0),
-    )(near(by_x), near(by_y), *behind)
-
-
 def add(*terms):
     return functools.reduce(lambda a, b: a + b, [t.astype(F32) for t in terms]).astype(BF16)
 
@@ -255,7 +236,8 @@
         if direct:
             corner = [send(features, x=1, y=1)]
         else:
-            half_x, half_y = cut(by_x, by_y, [])
+            half = by_y.shape[0] // 2
+            half_x, half_y = by_x[:half, : tokens.shape[1]], by_y[half:]
             corner = [send(half_x, y=1), send(half_y, x=1)]
         return [[own] + cores([own]), [by_y] + cores([by_y])], [[by_x] + cores([by_x]), corner + cores(corner)]
 
@@ -290,7 +272,9 @@
     back, arrived = [], ()
     for i in reversed(range(parts)):
         own, for_x, for_y, direct = sums[i]
-        for_x, for_y = after((for_x, for_y), arrived)
+        if arrived:
+            for_y = after(for_y, arrived[0])
+            for_x = after(for_x, arrived[1])
         arrived = send(for_x, x=1), send(for_y, y=1)
         mine = add(own, *arrived, *direct)
         for k in reversed(range(count)):

time: 81.4 us -> 80.9 us (level)
  waiting for transfers between devices: 31.9 us -> 30.7 us
    ppermute x34, waiting for transfers between devices: 31.9 us -> 30.7 us  [send(): return lax.ppermute(array, PAIR, pairs)]
  transfers between devices with their start and end apart: 34 -> 34, of which waited for: 13 -> 11; matrix products, arithmetic and copies ran while one was open for 2% -> 2% of each run, Pallas kernels for 16% -> 16%
where the time goes in v6:
time: 80.9 us; the launch traced here: 80.7 us
  starting transfers between devices  33.5 us (41%)
  waiting for transfers between devices  30.7 us (38%)
  Pallas kernels  14.1 us (17%)
  other arithmetic  2.05 us (3%)
    ppermute x34, starting transfers between devices, send(): return lax.ppermute(array, PAIR, pairs)  33.5 us
    ppermute x34, waiting for transfers between devices, send(): return lax.ppermute(array, PAIR, pairs)  30.7 us
    pallas_call x2, Pallas kernels, run_experts(): pl.pallas_call(functools.partial(experts_kernel, first, counts, block, ro...  13.1 us
    convert_element_type x9, other arithmetic, add(): functools.reduce(lambda a, b: a + b, [t.astype(F32) for t in terms])  1.85 us
  transfers between devices with their start and end apart: 34, of which 11 were waited for; matrix products, arithmetic and copies ran while one was open for 2% of the time, Pallas kernels for 16%

profile of v6, /device:TPU:0, one launch (start us, length us, event | category | flops | bytes accessed | tf_op | source)
XLA Modules:
  0.0 80.7 jit_solution(13137161128237792486)
XLA Ops:
  1.0 3.1 %collective-permute-start = (bf16[64,1152]{1,0:T(8,128)(2,1)S(1)}, bf16[64,1152]{1,0:T(8,128)(2,1)S(1)}, u32[]{:S(2)}, u32[]{:S(2)}) collective-permute-start(bf16[64,1152]{1,0:T(8,128)(2,1)S(1)} %shard_map.64), channel_id=1, source_target_pairs={{0,4},{1,5},{2,6},{3,7},{4,0},{5,1},{6,2},{7,3},{8,12},{9,13},{10,... | collective-permute-start | bytes 442376 | tf_op jit(solution)/shard_map/ppermute | solution.py:220
  4.1 2.6 %collective-permute-start.8 = (bf16[64,1152]{1,0:T(8,128)(2,1)S(1)}, bf16[64,1152]{1,0:T(8,128)(2,1)S(1)}, u32[]{:S(2)}, u32[]{:S(2)}) collective-permute-start(bf16[64,1152]{1,0:T(8,128)(2,1)S(1)} %shard_map.64), channel_id=1, source_target_pairs={{0,8},{1,9},{2,10},{3,11},{4,12},{5,13},{6,14},{7,15},{8,0},{9,1},... | collective-permute-start | bytes 442376 | tf_op jit(solution)/shard_map/ppermute | solution.py:220
  6.7 3.3 %collective-permute-done = bf16[64,1152]{1,0:T(8,128)(2,1)S(1)} collective-permute-done((bf16[64,1152]{1,0:T(8,128)(2,1)S(1)}, bf16[64,1152]{1,0:T(8,128)(2,1)S(1)}, u32[]{:S(2)}, u32[]{:S(2)}) %collective-permute-start) | collective-permute-done | bytes 147488 | tf_op jit(solution)/shard_map/ppermute | solution.py:220
  9.9 1.8 %collective-permute-start.2 = (bf16[128,1024]{1,0:T(8,128)(2,1)S(1)}, bf16[128,1024]{1,0:T(8,128)(2,1)S(1)}, u32[]{:S(2)}, u32[]{:S(2)}) collective-permute-start(bf16[128,1024]{1,0:T(8,128)(2,1)S(1)} %fusion.4), channel_id=1, source_target_pairs={{0,16},{1,17},{2,18},{3,19},{4,20},{5,21},{6,22},{7,23},{8,24},{9,... | collective-permute-start | bytes 786440 | tf_op jit(solution)/shard_map/ppermute | solution.py:220
  11.7 1.4 %collective-permute-start.6 = (bf16[128,1024]{1,0:T(8,128)(2,1)S(1)}, bf16[128,1024]{1,0:T(8,128)(2,1)S(1)}, u32[]{:S(2)}, u32[]{:S(2)}) collective-permute-start(bf16[128,1024]{1,0:T(8,128)(2,1)S(1)} %fusion.4), channel_id=1, source_target_pairs={{0,18},{1,19},{2,16},{3,17},{4,22},{5,23},{6,20},{7,21},{8,26},{9,... | collective-permute-start | bytes 786440 | tf_op jit(solution)/shard_map/ppermute | solution.py:220
  13.6 4.5 %collective-permute-done.8 = bf16[64,1152]{1,0:T(8,128)(2,1)S(1)} collective-permute-done((bf16[64,1152]{1,0:T(8,128)(2,1)S(1)}, bf16[64,1152]{1,0:T(8,128)(2,1)S(1)}, u32[]{:S(2)}, u32[]{:S(2)}) %collective-permute-start.8) | collective-permute-done | bytes 147488 | tf_op jit(solution)/shard_map/ppermute | solution.py:220
  18.1 1.6 %collective-permute-start.11 = (bf16[128,1024]{1,0:T(8,128)(2,1)S(1)}, bf16[128,1024]{1,0:T(8,128)(2,1)S(1)}, u32[]{:S(2)}, u32[]{:S(2)}) collective-permute-start(bf16[128,1024]{1,0:T(8,128)(2,1)S(1)} %slice.122), channel_id=1, source_target_pairs={{0,16},{1,17},{2,18},{3,19},{4,20},{5,21},{6,22},{7,23},{8,24},{9,... | collective-permute-start | bytes 786440 | tf_op jit(solution)/shard_map/ppermute | solution.py:220
  19.7 1.5 %collective-permute-start.13 = (bf16[128,1152]{1,0:T(8,128)(2,1)S(1)}, bf16[128,1152]{1,0:T(8,128)(2,1)S(1)}, u32[]{:S(2)}, u32[]{:S(2)}) collective-permute-start(bf16[128,1152]{1,0:T(8,128)(2,1)S(1)} %constant_dynamic-update-slice_fusion.refs_0_), channel_id=1, source_target_pairs={{0,2},{1,3},{2,0},{3,1},{4,6},{5,7},{6,4},{7,5},{8,10},{9,11},{10,... | collective-permute-start | bytes 884744 | tf_op jit(solution)/shard_map/ppermute | solution.py:220
  22.1 4.1 %collective-permute-done.4.refs_4_ = bf16[128,1152]{1,0:T(8,128)(2,1)S(1)} collective-permute-done((bf16[128,1152]{1,0:T(8,128)(2,1)S(1)}, bf16[128,1152]{1,0:T(8,128)(2,1)S(1)}, u32[]{:S(2)}, u32[]{:S(2)}) %collective-permute-start.4) | collective-permute-done | bytes 294944 | tf_op jit(solution)/shard_map/ppermute | solution.py:220
  26.8 2.6 %collective-permute-done.13.refs_4_ = bf16[128,1152]{1,0:T(8,128)(2,1)S(1)} collective-permute-done((bf16[128,1152]{1,0:T(8,128)(2,1)S(1)}, bf16[128,1152]{1,0:T(8,128)(2,1)S(1)}, u32[]{:S(2)}, u32[]{:S(2)}) %collective-permute-start.13) | collective-permute-done | bytes 294944 | tf_op jit(solution)/shard_map/ppermute | solution.py:220
  29.4 1.4 %collective-permute-start.16 = (bf16[64,1024]{1,0:T(8,128)(2,1)S(1)}, bf16[64,1024]{1,0:T(8,128)(2,1)S(1)}, u32[]{:S(2)}, u32[]{:S(2)}) collective-permute-start(bf16[64,1024]{1,0:T(8,128)(2,1)S(1)} %slice.124), channel_id=1, source_target_pairs={{0,2},{1,3},{2,0},{3,1},{4,6},{5,7},{6,4},{7,5},{8,10},{9,11},{10,... | collective-permute-start | bytes 393224 | tf_op jit(solution)/shard_map/ppermute | solution.py:220
  31.0 1.5 %collective-permute-start.15 = (bf16[64,1024]{1,0:T(8,128)(2,1)S(1)}, bf16[64,1024]{1,0:T(8,128)(2,1)S(1)}, u32[]{:S(2)}, u32[]{:S(2)}) collective-permute-start(bf16[64,1024]{1,0:T(8,128)(2,1)S(1)} %slice.123), channel_id=1, source_target_pairs={{0,16},{1,17},{2,18},{3,19},{4,20},{5,21},{6,22},{7,23},{8,24},{9,... | collective-permute-start | bytes 393224 | tf_op jit(solution)/shard_map/ppermute | solution.py:220
  32.6 7.9 %shard_map.65 = (bf16[128,1024]{1,0:T(8,128)(2,1)S(1)}, bf16[128,1024]{1,0:T(8,128)(2,1)S(1)}, bf16[3,128,1024]{2,1,0:T(8,128)(2,1)S(1)}, bf16[3,128,1024]{2,1,0...) custom-call(s32[2]{0:T(128)S(1)} %pad_add_fusion.places, ...), custom_call_target="tpu_custom_call" | custom-call | flops 512 | bytes 512 | tf_op jit(solution)/shard_map/pallas_call | solution.py:182
  42.7 5.2 %shard_map.66 = (bf16[128,1024]{1,0:T(8,128)(2,1)S(1)}, bf16[128,1024]{1,0:T(8,128)(2,1)S(1)}, bf16[3,128,1024]{2,1,0:T(8,128)(2,1)S(1)}, bf16[3,128,1024]{2,1,0:T(8,128)(2,1)S(1)}) custom-call(s32[2]{0:T(128)S(1)} %pad_add_fusion.places, bf16[2,2048,512]{2,1,0:T(8,128)(2,1)S(1)} %get-tuple-element.18.gate_in, ...), custom_call_target="tpu_custom_call" | custom-call | flops 512 | bytes 512 | tf_op jit(solution)/shard_map/pallas_call | solution.py:182
  50.0 1.4 %collective-permute-start.23 = (bf16[64,1024]{1,0:T(8,128)(2,1)S(1)}, bf16[64,1024]{1,0:T(8,128)(2,1)S(1)}, u32[]{:S(2)}, u32[]{:S(2)}) collective-permute-start(bf16[64,1024]{1,0:T(8,128)(2,1)S(1)} %get-tuple-element.41), channel_id=1, source_target_pairs={{0,2},{1,3},{2,0},{3,1},{4,6},{5,7},{6,4},{7,5},{8,10},{9,11},{10,... | collective-permute-start | bytes 393224 | tf_op jit(solution)/shard_map/ppermute | solution.py:220
  51.4 1.5 %collective-permute-start.21 = (bf16[64,1024]{1,0:T(8,128)(2,1)S(1)}, bf16[64,1024]{1,0:T(8,128)(2,1)S(1)}, u32[]{:S(2)}, u32[]{:S(2)}) collective-permute-start(bf16[64,1024]{1,0:T(8,128)(2,1)S(1)} %get-tuple-element.42), channel_id=1, source_target_pairs={{0,16},{1,17},{2,18},{3,19},{4,20},{5,21},{6,22},{7,23},{8,24},{9,... | collective-permute-start | bytes 393224 | tf_op jit(solution)/shard_map/ppermute | solution.py:220
  53.2 4.2 %collective-permute-done.23 = bf16[64,1024]{1,0:T(8,128)(2,1)S(1)} collective-permute-done((bf16[64,1024]{1,0:T(8,128)(2,1)S(1)}, bf16[64,1024]{1,0:T(8,128)(2,1)S(1)}, u32[]{:S(2)}, u32[]{:S(2)}) %collective-permute-start.23) | collective-permute-done | bytes 131104 | tf_op jit(solution)/shard_map/ppermute | solution.py:220
  58.3 1.4 %collective-permute-start.24 = (bf16[128,1024]{1,0:T(8,128)(2,1)S(1)}, bf16[128,1024]{1,0:T(8,128)(2,1)S(1)}, u32[]{:S(2)}, u32[]{:S(2)}) collective-permute-start(bf16[128,1024]{1,0:T(8,128)(2,1)S(1)} %pad_maximum_fusion.2), channel_id=1, source_target_pairs={{0,16},{1,17},{2,18},{3,19},{4,20},{5,21},{6,22},{7,23},{8,24},{9,... | collective-permute-start | bytes 786440 | tf_op jit(solution)/shard_map/ppermute | solution.py:220
  60.3 4.9 %collective-permute-done.22 = bf16[128,1024]{1,0:T(8,128)(2,1)S(1)} collective-permute-done((bf16[128,1024]{1,0:T(8,128)(2,1)S(1)}, bf16[128,1024]{1,0:T(8,128)(2,1)S(1)}, u32[]{:S(2)}, u32[]{:S(2)}) %collective-permute-start.22) | collective-permute-done | bytes 262176 | tf_op jit(solution)/shard_map/ppermute | solution.py:220
  65.2 1.4 %collective-permute-start.32 = (bf16[128,1024]{1,0:T(8,128)(2,1)S(1)}, bf16[128,1024]{1,0:T(8,128)(2,1)S(1)}, u32[]{:S(2)}, u32[]{:S(2)}) collective-permute-start(bf16[128,1024]{1,0:T(8,128)(2,1)S(1)} %pad_maximum_fusion.4), channel_id=1, source_target_pairs={{0,16},{1,17},{2,18},{3,19},{4,20},{5,21},{6,22},{7,23},{8,24},{9,... | collective-permute-start | bytes 786440 | tf_op jit(solution)/shard_map/ppermute | solution.py:220
  67.4 3.2 %collective-permute-start.26 = (bf16[64,1024]{1,0:T(8,128)(2,1)S(1)}, bf16[64,1024]{1,0:T(8,128)(2,1)S(1)}, u32[]{:S(2)}, u32[]{:S(2)}) collective-permute-start(bf16[64,1024]{1,0:T(8,128)(2,1)S(1)} %get-tuple-element.40), channel_id=1, source_target_pairs={{0,8},{1,9},{2,10},{3,11},{4,12},{5,13},{6,14},{7,15},{8,0},{9,1},... | collective-permute-start | bytes 393224 | tf_op jit(solution)/shard_map/ppermute | solution.py:220
  70.6 2.5 %collective-permute-start.25 = (bf16[64,1024]{1,0:T(8,128)(2,1)S(1)}, bf16[64,1024]{1,0:T(8,128)(2,1)S(1)}, u32[]{:S(2)}, u32[]{:S(2)}) collective-permute-start(bf16[64,1024]{1,0:T(8,128)(2,1)S(1)} %get-tuple-element.39), channel_id=1, source_target_pairs={{0,12},{1,13},{2,14},{3,15},{4,8},{5,9},{6,10},{7,11},{8,4},{9,5},... | collective-permute-start | bytes 393224 | tf_op jit(solution)/shard_map/ppermute | solution.py:220
  73.2 1.5 %collective-permute-start.33 = (bf16[64,1024]{1,0:T(8,128)(2,1)S(1)}, bf16[64,1024]{1,0:T(8,128)(2,1)S(1)}, u32[]{:S(2)}, u32[]{:S(2)}) collective-permute-start(bf16[64,1024]{1,0:T(8,128)(2,1)S(1)} %slice.141), channel_id=1, source_target_pairs={{0,4},{1,5},{2,6},{3,7},{4,0},{5,1},{6,2},{7,3},{8,12},{9,13},{10,... | collective-permute-start | bytes 393224 | tf_op jit(solution)/shard_map/ppermute | solution.py:220
  74.8 5.1 %collective-permute-done.26 = bf16[64,1024]{1,0:T(8,128)(2,1)S(1)} collective-permute-done((bf16[64,1024]{1,0:T(8,128)(2,1)S(1)}, bf16[64,1024]{1,0:T(8,128)(2,1)S(1)}, u32[]{:S(2)}, u32[]{:S(2)}) %collective-permute-start.26) | collective-permute-done | bytes 131104 | tf_op jit(solution)/shard_map/ppermute | solution.py:220
  (74 shorter events, 10.9 us)
Async XLA Ops:
  1.0 8.9 %collective-permute-start = (bf16[64,1152]{1,0:T(8,128)(2,1)S(1)}, bf16[64,1152]{1,0:T(8,128)(2,1)S(1)}, u32[]{:S(2)}, u32[]{:S(2)}) collective-permute-start(bf16[64,1152]{1,0:T(8,128)(2,1)S(1)} %shard_map.64), channel_id=1, source_target_pairs={{0,4},{1,5},{2,6},{3,7},{4,0},{5,1},{6,2},{7,3},{8,12},{9,13},{10,... | collective-permute-start | bytes 442376 | tf_op jit(solution)/shard_map/ppermute | solution.py:220
  4.1 14.0 %collective-permute-start.8 = (bf16[64,1152]{1,0:T(8,128)(2,1)S(1)}, bf16[64,1152]{1,0:T(8,128)(2,1)S(1)}, u32[]{:S(2)}, u32[]{:S(2)}) collective-permute-start(bf16[64,1152]{1,0:T(8,128)(2,1)S(1)} %shard_map.64), channel_id=1, source_target_pairs={{0,8},{1,9},{2,10},{3,11},{4,12},{5,13},{6,14},{7,15},{8,0},{9,1},... | collective-permute-start | bytes 442376 | tf_op jit(solution)/shard_map/ppermute | solution.py:220
  6.6 11.4 %collective-permute-start.9 = (bf16[64,1152]{1,0:T(8,128)(2,1)S(1)}, bf16[64,1152]{1,0:T(8,128)(2,1)S(1)}, u32[]{:S(2)}, u32[]{:S(2)}) collective-permute-start(bf16[64,1152]{1,0:T(8,128)(2,1)S(1)} %shard_map.64), channel_id=1, source_target_pairs={{0,12},{1,13},{2,14},{3,15},{4,8},{5,9},{6,10},{7,11},{8,4},{9,5},... | collective-permute-start | bytes 442376 | tf_op jit(solution)/shard_map/ppermute | solution.py:220
  9.9 12.2 %collective-permute-start.2 = (bf16[128,1024]{1,0:T(8,128)(2,1)S(1)}, bf16[128,1024]{1,0:T(8,128)(2,1)S(1)}, u32[]{:S(2)}, u32[]{:S(2)}) collective-permute-start(bf16[128,1024]{1,0:T(8,128)(2,1)S(1)} %fusion.4), channel_id=1, source_target_pairs={{0,16},{1,17},{2,18},{3,19},{4,20},{5,21},{6,22},{7,23},{8,24},{9,... | collective-permute-start | bytes 786440 | tf_op jit(solution)/shard_map/ppermute | solution.py:220
  11.7 14.5 %collective-permute-start.6 = (bf16[128,1024]{1,0:T(8,128)(2,1)S(1)}, bf16[128,1024]{1,0:T(8,128)(2,1)S(1)}, u32[]{:S(2)}, u32[]{:S(2)}) collective-permute-start(bf16[128,1024]{1,0:T(8,128)(2,1)S(1)} %fusion.4), channel_id=1, source_target_pairs={{0,18},{1,19},{2,16},{3,17},{4,22},{5,23},{6,20},{7,21},{8,26},{9,... | collective-permute-start | bytes 786440 | tf_op jit(solution)/shard_map/ppermute | solution.py:220
  13.2 13.0 %collective-permute-start.4 = (bf16[128,1152]{1,0:T(8,128)(2,1)S(1)}, bf16[128,1152]{1,0:T(8,128)(2,1)S(1)}, u32[]{:S(2)}, u32[]{:S(2)}) collective-permute-start(bf16[128,1152]{1,0:T(8,128)(2,1)S(1)} %pad_maximum_fusion.refs_0_), channel_id=1, source_target_pairs={{0,2},{1,3},{2,0},{3,1},{4,6},{5,7},{6,4},{7,5},{8,10},{9,11},{10,... | collective-permute-start | bytes 884744 | tf_op jit(solution)/shard_map/ppermute | solution.py:220
  18.1 8.6 %collective-permute-start.11 = (bf16[128,1024]{1,0:T(8,128)(2,1)S(1)}, bf16[128,1024]{1,0:T(8,128)(2,1)S(1)}, u32[]{:S(2)}, u32[]{:S(2)}) collective-permute-start(bf16[128,1024]{1,0:T(8,128)(2,1)S(1)} %slice.122), channel_id=1, source_target_pairs={{0,16},{1,17},{2,18},{3,19},{4,20},{5,21},{6,22},{7,23},{8,24},{9,... | collective-permute-start | bytes 786440 | tf_op jit(solution)/shard_map/ppermute | solution.py:220
  19.7 9.6 %collective-permute-start.13 = (bf16[128,1152]{1,0:T(8,128)(2,1)S(1)}, bf16[128,1152]{1,0:T(8,128)(2,1)S(1)}, u32[]{:S(2)}, u32[]{:S(2)}) collective-permute-start(bf16[128,1152]{1,0:T(8,128)(2,1)S(1)} %constant_dynamic-update-slice_fusion.refs_0_), channel_id=1, source_target_pairs={{0,2},{1,3},{2,0},{3,1},{4,6},{5,7},{6,4},{7,5},{8,10},{9,11},{10,... | collective-permute-start | bytes 884744 | tf_op jit(solution)/shard_map/ppermute | solution.py:220
  22.1 7.3 %collective-permute-start.1 = (bf16[128,1152]{1,0:T(8,128)(2,1)S(1)}, bf16[128,1152]{1,0:T(8,128)(2,1)S(1)}, u32[]{:S(2)}, u32[]{:S(2)}) collective-permute-start(bf16[128,1152]{1,0:T(8,128)(2,1)S(1)} %pad_maximum_fusion.refs_0_), channel_id=1, source_target_pairs={{0,1},{1,0},{2,3},{3,2},{4,5},{5,4},{6,7},{7,6},{8,9},{9,8},{10,11... | collective-permute-start | bytes 884744 | tf_op jit(solution)/shard_map/ppermute | solution.py:220
  29.4 11.2 %collective-permute-start.10 = (bf16[128,1152]{1,0:T(8,128)(2,1)S(1)}, bf16[128,1152]{1,0:T(8,128)(2,1)S(1)}, u32[]{:S(2)}, u32[]{:S(2)}) collective-permute-start(bf16[128,1152]{1,0:T(8,128)(2,1)S(1)} %constant_dynamic-update-slice_fusion.refs_0_), channel_id=1, source_target_pairs={{0,1},{1,0},{2,3},{3,2},{4,5},{5,4},{6,7},{7,6},{8,9},{9,8},{10,11... | collective-permute-start | bytes 884744 | tf_op jit(solution)/shard_map/ppermute | solution.py:220
  29.4 11.8 %collective-permute-start.16 = (bf16[64,1024]{1,0:T(8,128)(2,1)S(1)}, bf16[64,1024]{1,0:T(8,128)(2,1)S(1)}, u32[]{:S(2)}, u32[]{:S(2)}) collective-permute-start(bf16[64,1024]{1,0:T(8,128)(2,1)S(1)} %slice.124), channel_id=1, source_target_pairs={{0,2},{1,3},{2,0},{3,1},{4,6},{5,7},{6,4},{7,5},{8,10},{9,11},{10,... | collective-permute-start | bytes 393224 | tf_op jit(solution)/shard_map/ppermute | solution.py:220
  30.8 10.9 %collective-permute-start.12 = (bf16[128,1024]{1,0:T(8,128)(2,1)S(1)}, bf16[128,1024]{1,0:T(8,128)(2,1)S(1)}, u32[]{:S(2)}, u32[]{:S(2)}) collective-permute-start(bf16[128,1024]{1,0:T(8,128)(2,1)S(1)} %collective-permute-done.11.refs_2_), channel_id=1, source_target_pairs={{0,1},{1,0},{2,3},{3,2},{4,5},{5,4},{6,7},{7,6},{8,9},{9,8},{10,11... | collective-permute-start | bytes 786440 | tf_op jit(solution)/shard_map/ppermute | solution.py:220
  31.0 10.2 %collective-permute-start.15 = (bf16[64,1024]{1,0:T(8,128)(2,1)S(1)}, bf16[64,1024]{1,0:T(8,128)(2,1)S(1)}, u32[]{:S(2)}, u32[]{:S(2)}) collective-permute-start(bf16[64,1024]{1,0:T(8,128)(2,1)S(1)} %slice.123), channel_id=1, source_target_pairs={{0,16},{1,17},{2,18},{3,19},{4,20},{5,21},{6,22},{7,23},{8,24},{9,... | collective-permute-start | bytes 393224 | tf_op jit(solution)/shard_map/ppermute | solution.py:220
  32.6 10.1 %collective-permute-start.14 = (bf16[128,1152]{1,0:T(8,128)(2,1)S(1)}, bf16[128,1152]{1,0:T(8,128)(2,1)S(1)}, u32[]{:S(2)}, u32[]{:S(2)}) collective-permute-start(bf16[128,1152]{1,0:T(8,128)(2,1)S(1)} %collective-permute-done.13.refs_4_), channel_id=1, source_target_pairs={{0,1},{1,0},{2,3},{3,2},{4,5},{5,4},{6,7},{7,6},{8,9},{9,8},{10,11... | collective-permute-start | bytes 884744 | tf_op jit(solution)/shard_map/ppermute | solution.py:220
  40.6 7.9 %collective-permute-start.28 = (bf16[128,1024]{1,0:T(8,128)(2,1)S(1)}, bf16[128,1024]{1,0:T(8,128)(2,1)S(1)}, u32[]{:S(2)}, u32[]{:S(2)}) collective-permute-start(bf16[128,1024]{1,0:T(8,128)(2,1)S(1)} %get-tuple-element.28), channel_id=1, source_target_pairs={{0,1},{1,0},{2,3},{3,2},{4,5},{5,4},{6,7},{7,6},{8,9},{9,8},{10,11... | collective-permute-start | bytes 786440 | tf_op jit(solution)/shard_map/ppermute | solution.py:220
  41.7 18.1 %collective-permute-start.27 = (bf16[3,128,1024]{2,1,0:T(8,128)(2,1)S(1)}, bf16[3,128,1024]{2,1,0:T(8,128)(2,1)S(1)}, u32[]{:S(2)}, u32[]{:S(2)}) collective-permute-start(bf16[3,128,1024]{2,1,0:T(8,128)(2,1)S(1)} %get-tuple-element.26), channel_id=1, source_target_pairs={{0,1},{1,0},{2,3},{3,2},{4,5},{5,4},{6,7},{7,6},{8,9},{9,8},{10,11... | collective-permute-start | bytes 2359304 | tf_op jit(solution)/shard_map/ppermute | solution.py:220
  48.6 11.5 %collective-permute-start.29 = (bf16[64,1024]{1,0:T(8,128)(2,1)S(1)}, bf16[64,1024]{1,0:T(8,128)(2,1)S(1)}, u32[]{:S(2)}, u32[]{:S(2)}) collective-permute-start(bf16[64,1024]{1,0:T(8,128)(2,1)S(1)} %get-tuple-element.43), channel_id=1, source_target_pairs={{0,16},{1,17},{2,18},{3,19},{4,20},{5,21},{6,22},{7,23},{8,24},{9,... | collective-permute-start | bytes 393224 | tf_op jit(solution)/shard_map/ppermute | solution.py:220
  49.2 10.9 %collective-permute-start.31 = (bf16[64,1024]{1,0:T(8,128)(2,1)S(1)}, bf16[64,1024]{1,0:T(8,128)(2,1)S(1)}, u32[]{:S(2)}, u32[]{:S(2)}) collective-permute-start(bf16[64,1024]{1,0:T(8,128)(2,1)S(1)} %get-tuple-element.44), channel_id=1, source_target_pairs={{0,2},{1,3},{2,0},{3,1},{4,6},{5,7},{6,4},{7,5},{8,10},{9,11},{10,... | collective-permute-start | bytes 393224 | tf_op jit(solution)/shard_map/ppermute | solution.py:220
  50.0 7.5 %collective-permute-start.23 = (bf16[64,1024]{1,0:T(8,128)(2,1)S(1)}, bf16[64,1024]{1,0:T(8,128)(2,1)S(1)}, u32[]{:S(2)}, u32[]{:S(2)}) collective-permute-start(bf16[64,1024]{1,0:T(8,128)(2,1)S(1)} %get-tuple-element.41), channel_id=1, source_target_pairs={{0,2},{1,3},{2,0},{3,1},{4,6},{5,7},{6,4},{7,5},{8,10},{9,11},{10,... | collective-permute-start | bytes 393224 | tf_op jit(solution)/shard_map/ppermute | solution.py:220
  57.6 7.6 %collective-permute-start.22 = (bf16[128,1024]{1,0:T(8,128)(2,1)S(1)}, bf16[128,1024]{1,0:T(8,128)(2,1)S(1)}, u32[]{:S(2)}, u32[]{:S(2)}) collective-permute-start(bf16[128,1024]{1,0:T(8,128)(2,1)S(1)} %pad_maximum_fusion.1), channel_id=1, source_target_pairs={{0,2},{1,3},{2,0},{3,1},{4,6},{5,7},{6,4},{7,5},{8,10},{9,11},{10,... | collective-permute-start | bytes 786440 | tf_op jit(solution)/shard_map/ppermute | solution.py:220
  58.3 8.2 %collective-permute-start.24 = (bf16[128,1024]{1,0:T(8,128)(2,1)S(1)}, bf16[128,1024]{1,0:T(8,128)(2,1)S(1)}, u32[]{:S(2)}, u32[]{:S(2)}) collective-permute-start(bf16[128,1024]{1,0:T(8,128)(2,1)S(1)} %pad_maximum_fusion.2), channel_id=1, source_target_pairs={{0,16},{1,17},{2,18},{3,19},{4,20},{5,21},{6,22},{7,23},{8,24},{9,... | collective-permute-start | bytes 786440 | tf_op jit(solution)/shard_map/ppermute | solution.py:220
  65.2 7.9 %collective-permute-start.32 = (bf16[128,1024]{1,0:T(8,128)(2,1)S(1)}, bf16[128,1024]{1,0:T(8,128)(2,1)S(1)}, u32[]{:S(2)}, u32[]{:S(2)}) collective-permute-start(bf16[128,1024]{1,0:T(8,128)(2,1)S(1)} %pad_maximum_fusion.4), channel_id=1, source_target_pairs={{0,16},{1,17},{2,18},{3,19},{4,20},{5,21},{6,22},{7,23},{8,24},{9,... | collective-permute-start | bytes 786440 | tf_op jit(solution)/shard_map/ppermute | solution.py:220
  67.4 12.4 %collective-permute-start.26 = (bf16[64,1024]{1,0:T(8,128)(2,1)S(1)}, bf16[64,1024]{1,0:T(8,128)(2,1)S(1)}, u32[]{:S(2)}, u32[]{:S(2)}) collective-permute-start(bf16[64,1024]{1,0:T(8,128)(2,1)S(1)} %get-tuple-element.40), channel_id=1, source_target_pairs={{0,8},{1,9},{2,10},{3,11},{4,12},{5,13},{6,14},{7,15},{8,0},{9,1},... | collective-permute-start | bytes 393224 | tf_op jit(solution)/shard_map/ppermute | solution.py:220
  70.6 9.3 %collective-permute-start.25 = (bf16[64,1024]{1,0:T(8,128)(2,1)S(1)}, bf16[64,1024]{1,0:T(8,128)(2,1)S(1)}, u32[]{:S(2)}, u32[]{:S(2)}) collective-permute-start(bf16[64,1024]{1,0:T(8,128)(2,1)S(1)} %get-tuple-element.39), channel_id=1, source_target_pairs={{0,12},{1,13},{2,14},{3,15},{4,8},{5,9},{6,10},{7,11},{8,4},{9,5},... | collective-permute-start | bytes 393224 | tf_op jit(solution)/shard_map/ppermute | solution.py:220
  (10 other events, 42.4 us)

commit v7 on v6

--- a/solution.py
+++ b/solution.py
@@ -247,7 +247,7 @@
     def turn(corner, rest):
         for_x, for_y = rest[1], rest[2]
         half = for_x.shape[0] // 2
-        got_a, got_b = send(corner[:half], x=1), send(corner[half:], y=1)
+        got_b, got_a = send(corner[half:], y=1), send(corner[:half], x=1)
         for_x = join([for_x[:half], add(for_x[half:], got_b)])
         for_y = join([add(for_y[:half], got_a), for_y[half:]])
         return for_x, for_y

time: 80.9 us -> 80.9 us (level)
  no operation moved by 1% of the time
where the time goes in v7:
time: 80.9 us; the launch traced here: 80.7 us
  starting transfers between devices  33.5 us (41%)
  waiting for transfers between devices  30.7 us (38%)
  Pallas kernels  14.1 us (17%)
  other arithmetic  2.05 us (3%)
    ppermute x34, starting transfers between devices, send(): return lax.ppermute(array, PAIR, pairs)  33.5 us
    ppermute x34, waiting for transfers between devices, send(): return lax.ppermute(array, PAIR, pairs)  30.7 us
    pallas_call x2, Pallas kernels, run_experts(): pl.pallas_call(functools.partial(experts_kernel, first, counts, block, ro...  13.1 us
    convert_element_type x9, other arithmetic, add(): functools.reduce(lambda a, b: a + b, [t.astype(F32) for t in terms])  1.85 us
  transfers between devices with their start and end apart: 34, of which 11 were waited for; matrix products, arithmetic and copies ran while one was open for 2% of the time, Pallas kernels for 16%

profile of v7, /device:TPU:0, one launch (start us, length us, event | category | flops | bytes accessed | tf_op | source)
XLA Modules:
  0.0 80.7 jit_solution(13137161128237792486)
XLA Ops:
  1.0 3.1 %collective-permute-start = (bf16[64,1152]{1,0:T(8,128)(2,1)S(1)}, bf16[64,1152]{1,0:T(8,128)(2,1)S(1)}, u32[]{:S(2)}, u32[]{:S(2)}) collective-permute-start(bf16[64,1152]{1,0:T(8,128)(2,1)S(1)} %shard_map.64), channel_id=1, source_target_pairs={{0,4},{1,5},{2,6},{3,7},{4,0},{5,1},{6,2},{7,3},{8,12},{9,13},{10,... | collective-permute-start | bytes 442376 | tf_op jit(solution)/shard_map/ppermute | solution.py:220
  4.1 2.6 %collective-permute-start.8 = (bf16[64,1152]{1,0:T(8,128)(2,1)S(1)}, bf16[64,1152]{1,0:T(8,128)(2,1)S(1)}, u32[]{:S(2)}, u32[]{:S(2)}) collective-permute-start(bf16[64,1152]{1,0:T(8,128)(2,1)S(1)} %shard_map.64), channel_id=1, source_target_pairs={{0,8},{1,9},{2,10},{3,11},{4,12},{5,13},{6,14},{7,15},{8,0},{9,1},... | collective-permute-start | bytes 442376 | tf_op jit(solution)/shard_map/ppermute | solution.py:220
  6.7 3.3 %collective-permute-done = bf16[64,1152]{1,0:T(8,128)(2,1)S(1)} collective-permute-done((bf16[64,1152]{1,0:T(8,128)(2,1)S(1)}, bf16[64,1152]{1,0:T(8,128)(2,1)S(1)}, u32[]{:S(2)}, u32[]{:S(2)}) %collective-permute-start) | collective-permute-done | bytes 147488 | tf_op jit(solution)/shard_map/ppermute | solution.py:220
  9.9 1.8 %collective-permute-start.2 = (bf16[128,1024]{1,0:T(8,128)(2,1)S(1)}, bf16[128,1024]{1,0:T(8,128)(2,1)S(1)}, u32[]{:S(2)}, u32[]{:S(2)}) collective-permute-start(bf16[128,1024]{1,0:T(8,128)(2,1)S(1)} %fusion.4), channel_id=1, source_target_pairs={{0,16},{1,17},{2,18},{3,19},{4,20},{5,21},{6,22},{7,23},{8,24},{9,... | collective-permute-start | bytes 786440 | tf_op jit(solution)/shard_map/ppermute | solution.py:220
  11.7 1.4 %collective-permute-start.6 = (bf16[128,1024]{1,0:T(8,128)(2,1)S(1)}, bf16[128,1024]{1,0:T(8,128)(2,1)S(1)}, u32[]{:S(2)}, u32[]{:S(2)}) collective-permute-start(bf16[128,1024]{1,0:T(8,128)(2,1)S(1)} %fusion.4), channel_id=1, source_target_pairs={{0,18},{1,19},{2,16},{3,17},{4,22},{5,23},{6,20},{7,21},{8,26},{9,... | collective-permute-start | bytes 786440 | tf_op jit(solution)/shard_map/ppermute | solution.py:220
  13.6 4.5 %collective-permute-done.8 = bf16[64,1152]{1,0:T(8,128)(2,1)S(1)} collective-permute-done((bf16[64,1152]{1,0:T(8,128)(2,1)S(1)}, bf16[64,1152]{1,0:T(8,128)(2,1)S(1)}, u32[]{:S(2)}, u32[]{:S(2)}) %collective-permute-start.8) | collective-permute-done | bytes 147488 | tf_op jit(solution)/shard_map/ppermute | solution.py:220
  18.1 1.6 %collective-permute-start.11 = (bf16[128,1024]{1,0:T(8,128)(2,1)S(1)}, bf16[128,1024]{1,0:T(8,128)(2,1)S(1)}, u32[]{:S(2)}, u32[]{:S(2)}) collective-permute-start(bf16[128,1024]{1,0:T(8,128)(2,1)S(1)} %slice.122), channel_id=1, source_target_pairs={{0,16},{1,17},{2,18},{3,19},{4,20},{5,21},{6,22},{7,23},{8,24},{9,... | collective-permute-start | bytes 786440 | tf_op jit(solution)/shard_map/ppermute | solution.py:220
  19.7 1.5 %collective-permute-start.13 = (bf16[128,1152]{1,0:T(8,128)(2,1)S(1)}, bf16[128,1152]{1,0:T(8,128)(2,1)S(1)}, u32[]{:S(2)}, u32[]{:S(2)}) collective-permute-start(bf16[128,1152]{1,0:T(8,128)(2,1)S(1)} %constant_dynamic-update-slice_fusion.refs_0_), channel_id=1, source_target_pairs={{0,2},{1,3},{2,0},{3,1},{4,6},{5,7},{6,4},{7,5},{8,10},{9,11},{10,... | collective-permute-start | bytes 884744 | tf_op jit(solution)/shard_map/ppermute | solution.py:220
  22.1 4.1 %collective-permute-done.4.refs_4_ = bf16[128,1152]{1,0:T(8,128)(2,1)S(1)} collective-permute-done((bf16[128,1152]{1,0:T(8,128)(2,1)S(1)}, bf16[128,1152]{1,0:T(8,128)(2,1)S(1)}, u32[]{:S(2)}, u32[]{:S(2)}) %collective-permute-start.4) | collective-permute-done | bytes 294944 | tf_op jit(solution)/shard_map/ppermute | solution.py:220
  26.8 2.6 %collective-permute-done.13.refs_4_ = bf16[128,1152]{1,0:T(8,128)(2,1)S(1)} collective-permute-done((bf16[128,1152]{1,0:T(8,128)(2,1)S(1)}, bf16[128,1152]{1,0:T(8,128)(2,1)S(1)}, u32[]{:S(2)}, u32[]{:S(2)}) %collective-permute-start.13) | collective-permute-done | bytes 294944 | tf_op jit(solution)/shard_map/ppermute | solution.py:220
  29.4 1.4 %collective-permute-start.16 = (bf16[64,1024]{1,0:T(8,128)(2,1)S(1)}, bf16[64,1024]{1,0:T(8,128)(2,1)S(1)}, u32[]{:S(2)}, u32[]{:S(2)}) collective-permute-start(bf16[64,1024]{1,0:T(8,128)(2,1)S(1)} %slice.124), channel_id=1, source_target_pairs={{0,2},{1,3},{2,0},{3,1},{4,6},{5,7},{6,4},{7,5},{8,10},{9,11},{10,... | collective-permute-start | bytes 393224 | tf_op jit(solution)/shard_map/ppermute | solution.py:220
  31.0 1.5 %collective-permute-start.15 = (bf16[64,1024]{1,0:T(8,128)(2,1)S(1)}, bf16[64,1024]{1,0:T(8,128)(2,1)S(1)}, u32[]{:S(2)}, u32[]{:S(2)}) collective-permute-start(bf16[64,1024]{1,0:T(8,128)(2,1)S(1)} %slice.123), channel_id=1, source_target_pairs={{0,16},{1,17},{2,18},{3,19},{4,20},{5,21},{6,22},{7,23},{8,24},{9,... | collective-permute-start | bytes 393224 | tf_op jit(solution)/shard_map/ppermute | solution.py:220
  32.6 7.9 %shard_map.65 = (bf16[128,1024]{1,0:T(8,128)(2,1)S(1)}, bf16[128,1024]{1,0:T(8,128)(2,1)S(1)}, bf16[3,128,1024]{2,1,0:T(8,128)(2,1)S(1)}, bf16[3,128,1024]{2,1,0...) custom-call(s32[2]{0:T(128)S(1)} %pad_add_fusion.places, ...), custom_call_target="tpu_custom_call" | custom-call | flops 512 | bytes 512 | tf_op jit(solution)/shard_map/pallas_call | solution.py:182
  42.7 5.2 %shard_map.66 = (bf16[128,1024]{1,0:T(8,128)(2,1)S(1)}, bf16[128,1024]{1,0:T(8,128)(2,1)S(1)}, bf16[3,128,1024]{2,1,0:T(8,128)(2,1)S(1)}, bf16[3,128,1024]{2,1,0:T(8,128)(2,1)S(1)}) custom-call(s32[2]{0:T(128)S(1)} %pad_add_fusion.places, bf16[2,2048,512]{2,1,0:T(8,128)(2,1)S(1)} %get-tuple-element.18.gate_in, ...), custom_call_target="tpu_custom_call" | custom-call | flops 512 | bytes 512 | tf_op jit(solution)/shard_map/pallas_call | solution.py:182
  50.0 1.4 %collective-permute-start.23 = (bf16[64,1024]{1,0:T(8,128)(2,1)S(1)}, bf16[64,1024]{1,0:T(8,128)(2,1)S(1)}, u32[]{:S(2)}, u32[]{:S(2)}) collective-permute-start(bf16[64,1024]{1,0:T(8,128)(2,1)S(1)} %get-tuple-element.41), channel_id=1, source_target_pairs={{0,2},{1,3},{2,0},{3,1},{4,6},{5,7},{6,4},{7,5},{8,10},{9,11},{10,... | collective-permute-start | bytes 393224 | tf_op jit(solution)/shard_map/ppermute | solution.py:220
  51.4 1.5 %collective-permute-start.21 = (bf16[64,1024]{1,0:T(8,128)(2,1)S(1)}, bf16[64,1024]{1,0:T(8,128)(2,1)S(1)}, u32[]{:S(2)}, u32[]{:S(2)}) collective-permute-start(bf16[64,1024]{1,0:T(8,128)(2,1)S(1)} %get-tuple-element.42), channel_id=1, source_target_pairs={{0,16},{1,17},{2,18},{3,19},{4,20},{5,21},{6,22},{7,23},{8,24},{9,... | collective-permute-start | bytes 393224 | tf_op jit(solution)/shard_map/ppermute | solution.py:220
  53.2 4.2 %collective-permute-done.23 = bf16[64,1024]{1,0:T(8,128)(2,1)S(1)} collective-permute-done((bf16[64,1024]{1,0:T(8,128)(2,1)S(1)}, bf16[64,1024]{1,0:T(8,128)(2,1)S(1)}, u32[]{:S(2)}, u32[]{:S(2)}) %collective-permute-start.23) | collective-permute-done | bytes 131104 | tf_op jit(solution)/shard_map/ppermute | solution.py:220
  58.3 1.4 %collective-permute-start.24 = (bf16[128,1024]{1,0:T(8,128)(2,1)S(1)}, bf16[128,1024]{1,0:T(8,128)(2,1)S(1)}, u32[]{:S(2)}, u32[]{:S(2)}) collective-permute-start(bf16[128,1024]{1,0:T(8,128)(2,1)S(1)} %pad_maximum_fusion.2), channel_id=1, source_target_pairs={{0,16},{1,17},{2,18},{3,19},{4,20},{5,21},{6,22},{7,23},{8,24},{9,... | collective-permute-start | bytes 786440 | tf_op jit(solution)/shard_map/ppermute | solution.py:220
  60.3 4.9 %collective-permute-done.22 = bf16[128,1024]{1,0:T(8,128)(2,1)S(1)} collective-permute-done((bf16[128,1024]{1,0:T(8,128)(2,1)S(1)}, bf16[128,1024]{1,0:T(8,128)(2,1)S(1)}, u32[]{:S(2)}, u32[]{:S(2)}) %collective-permute-start.22) | collective-permute-done | bytes 262176 | tf_op jit(solution)/shard_map/ppermute | solution.py:220
  65.2 1.4 %collective-permute-start.32 = (bf16[128,1024]{1,0:T(8,128)(2,1)S(1)}, bf16[128,1024]{1,0:T(8,128)(2,1)S(1)}, u32[]{:S(2)}, u32[]{:S(2)}) collective-permute-start(bf16[128,1024]{1,0:T(8,128)(2,1)S(1)} %pad_maximum_fusion.4), channel_id=1, source_target_pairs={{0,16},{1,17},{2,18},{3,19},{4,20},{5,21},{6,22},{7,23},{8,24},{9,... | collective-permute-start | bytes 786440 | tf_op jit(solution)/shard_map/ppermute | solution.py:220
  67.4 3.2 %collective-permute-start.26 = (bf16[64,1024]{1,0:T(8,128)(2,1)S(1)}, bf16[64,1024]{1,0:T(8,128)(2,1)S(1)}, u32[]{:S(2)}, u32[]{:S(2)}) collective-permute-start(bf16[64,1024]{1,0:T(8,128)(2,1)S(1)} %get-tuple-element.40), channel_id=1, source_target_pairs={{0,8},{1,9},{2,10},{3,11},{4,12},{5,13},{6,14},{7,15},{8,0},{9,1},... | collective-permute-start | bytes 393224 | tf_op jit(solution)/shard_map/ppermute | solution.py:220
  70.6 2.5 %collective-permute-start.25 = (bf16[64,1024]{1,0:T(8,128)(2,1)S(1)}, bf16[64,1024]{1,0:T(8,128)(2,1)S(1)}, u32[]{:S(2)}, u32[]{:S(2)}) collective-permute-start(bf16[64,1024]{1,0:T(8,128)(2,1)S(1)} %get-tuple-element.39), channel_id=1, source_target_pairs={{0,12},{1,13},{2,14},{3,15},{4,8},{5,9},{6,10},{7,11},{8,4},{9,5},... | collective-permute-start | bytes 393224 | tf_op jit(solution)/shard_map/ppermute | solution.py:220
  73.2 1.5 %collective-permute-start.33 = (bf16[64,1024]{1,0:T(8,128)(2,1)S(1)}, bf16[64,1024]{1,0:T(8,128)(2,1)S(1)}, u32[]{:S(2)}, u32[]{:S(2)}) collective-permute-start(bf16[64,1024]{1,0:T(8,128)(2,1)S(1)} %slice.141), channel_id=1, source_target_pairs={{0,4},{1,5},{2,6},{3,7},{4,0},{5,1},{6,2},{7,3},{8,12},{9,13},{10,... | collective-permute-start | bytes 393224 | tf_op jit(solution)/shard_map/ppermute | solution.py:220
  74.8 5.1 %collective-permute-done.26 = bf16[64,1024]{1,0:T(8,128)(2,1)S(1)} collective-permute-done((bf16[64,1024]{1,0:T(8,128)(2,1)S(1)}, bf16[64,1024]{1,0:T(8,128)(2,1)S(1)}, u32[]{:S(2)}, u32[]{:S(2)}) %collective-permute-start.26) | collective-permute-done | bytes 131104 | tf_op jit(solution)/shard_map/ppermute | solution.py:220
  (74 shorter events, 10.9 us)
Async XLA Ops:
  1.0 8.9 %collective-permute-start = (bf16[64,1152]{1,0:T(8,128)(2,1)S(1)}, bf16[64,1152]{1,0:T(8,128)(2,1)S(1)}, u32[]{:S(2)}, u32[]{:S(2)}) collective-permute-start(bf16[64,1152]{1,0:T(8,128)(2,1)S(1)} %shard_map.64), channel_id=1, source_target_pairs={{0,4},{1,5},{2,6},{3,7},{4,0},{5,1},{6,2},{7,3},{8,12},{9,13},{10,... | collective-permute-start | bytes 442376 | tf_op jit(solution)/shard_map/ppermute | solution.py:220
  4.1 14.0 %collective-permute-start.8 = (bf16[64,1152]{1,0:T(8,128)(2,1)S(1)}, bf16[64,1152]{1,0:T(8,128)(2,1)S(1)}, u32[]{:S(2)}, u32[]{:S(2)}) collective-permute-start(bf16[64,1152]{1,0:T(8,128)(2,1)S(1)} %shard_map.64), channel_id=1, source_target_pairs={{0,8},{1,9},{2,10},{3,11},{4,12},{5,13},{6,14},{7,15},{8,0},{9,1},... | collective-permute-start | bytes 442376 | tf_op jit(solution)/shard_map/ppermute | solution.py:220
  6.6 11.4 %collective-permute-start.9 = (bf16[64,1152]{1,0:T(8,128)(2,1)S(1)}, bf16[64,1152]{1,0:T(8,128)(2,1)S(1)}, u32[]{:S(2)}, u32[]{:S(2)}) collective-permute-start(bf16[64,1152]{1,0:T(8,128)(2,1)S(1)} %shard_map.64), channel_id=1, source_target_pairs={{0,12},{1,13},{2,14},{3,15},{4,8},{5,9},{6,10},{7,11},{8,4},{9,5},... | collective-permute-start | bytes 442376 | tf_op jit(solution)/shard_map/ppermute | solution.py:220
  9.9 12.2 %collective-permute-start.2 = (bf16[128,1024]{1,0:T(8,128)(2,1)S(1)}, bf16[128,1024]{1,0:T(8,128)(2,1)S(1)}, u32[]{:S(2)}, u32[]{:S(2)}) collective-permute-start(bf16[128,1024]{1,0:T(8,128)(2,1)S(1)} %fusion.4), channel_id=1, source_target_pairs={{0,16},{1,17},{2,18},{3,19},{4,20},{5,21},{6,22},{7,23},{8,24},{9,... | collective-permute-start | bytes 786440 | tf_op jit(solution)/shard_map/ppermute | solution.py:220
  11.7 14.5 %collective-permute-start.6 = (bf16[128,1024]{1,0:T(8,128)(2,1)S(1)}, bf16[128,1024]{1,0:T(8,128)(2,1)S(1)}, u32[]{:S(2)}, u32[]{:S(2)}) collective-permute-start(bf16[128,1024]{1,0:T(8,128)(2,1)S(1)} %fusion.4), channel_id=1, source_target_pairs={{0,18},{1,19},{2,16},{3,17},{4,22},{5,23},{6,20},{7,21},{8,26},{9,... | collective-permute-start | bytes 786440 | tf_op jit(solution)/shard_map/ppermute | solution.py:220
  13.2 13.0 %collective-permute-start.4 = (bf16[128,1152]{1,0:T(8,128)(2,1)S(1)}, bf16[128,1152]{1,0:T(8,128)(2,1)S(1)}, u32[]{:S(2)}, u32[]{:S(2)}) collective-permute-start(bf16[128,1152]{1,0:T(8,128)(2,1)S(1)} %pad_maximum_fusion.refs_0_), channel_id=1, source_target_pairs={{0,2},{1,3},{2,0},{3,1},{4,6},{5,7},{6,4},{7,5},{8,10},{9,11},{10,... | collective-permute-start | bytes 884744 | tf_op jit(solution)/shard_map/ppermute | solution.py:220
  18.1 8.6 %collective-permute-start.11 = (bf16[128,1024]{1,0:T(8,128)(2,1)S(1)}, bf16[128,1024]{1,0:T(8,128)(2,1)S(1)}, u32[]{:S(2)}, u32[]{:S(2)}) collective-permute-start(bf16[128,1024]{1,0:T(8,128)(2,1)S(1)} %slice.122), channel_id=1, source_target_pairs={{0,16},{1,17},{2,18},{3,19},{4,20},{5,21},{6,22},{7,23},{8,24},{9,... | collective-permute-start | bytes 786440 | tf_op jit(solution)/shard_map/ppermute | solution.py:220
  19.7 9.6 %collective-permute-start.13 = (bf16[128,1152]{1,0:T(8,128)(2,1)S(1)}, bf16[128,1152]{1,0:T(8,128)(2,1)S(1)}, u32[]{:S(2)}, u32[]{:S(2)}) collective-permute-start(bf16[128,1152]{1,0:T(8,128)(2,1)S(1)} %constant_dynamic-update-slice_fusion.refs_0_), channel_id=1, source_target_pairs={{0,2},{1,3},{2,0},{3,1},{4,6},{5,7},{6,4},{7,5},{8,10},{9,11},{10,... | collective-permute-start | bytes 884744 | tf_op jit(solution)/shard_map/ppermute | solution.py:220
  22.1 7.3 %collective-permute-start.1 = (bf16[128,1152]{1,0:T(8,128)(2,1)S(1)}, bf16[128,1152]{1,0:T(8,128)(2,1)S(1)}, u32[]{:S(2)}, u32[]{:S(2)}) collective-permute-start(bf16[128,1152]{1,0:T(8,128)(2,1)S(1)} %pad_maximum_fusion.refs_0_), channel_id=1, source_target_pairs={{0,1},{1,0},{2,3},{3,2},{4,5},{5,4},{6,7},{7,6},{8,9},{9,8},{10,11... | collective-permute-start | bytes 884744 | tf_op jit(solution)/shard_map/ppermute | solution.py:220
  29.4 11.2 %collective-permute-start.10 = (bf16[128,1152]{1,0:T(8,128)(2,1)S(1)}, bf16[128,1152]{1,0:T(8,128)(2,1)S(1)}, u32[]{:S(2)}, u32[]{:S(2)}) collective-permute-start(bf16[128,1152]{1,0:T(8,128)(2,1)S(1)} %constant_dynamic-update-slice_fusion.refs_0_), channel_id=1, source_target_pairs={{0,1},{1,0},{2,3},{3,2},{4,5},{5,4},{6,7},{7,6},{8,9},{9,8},{10,11... | collective-permute-start | bytes 884744 | tf_op jit(solution)/shard_map/ppermute | solution.py:220
  29.4 11.8 %collective-permute-start.16 = (bf16[64,1024]{1,0:T(8,128)(2,1)S(1)}, bf16[64,1024]{1,0:T(8,128)(2,1)S(1)}, u32[]{:S(2)}, u32[]{:S(2)}) collective-permute-start(bf16[64,1024]{1,0:T(8,128)(2,1)S(1)} %slice.124), channel_id=1, source_target_pairs={{0,2},{1,3},{2,0},{3,1},{4,6},{5,7},{6,4},{7,5},{8,10},{9,11},{10,... | collective-permute-start | bytes 393224 | tf_op jit(solution)/shard_map/ppermute | solution.py:220
  30.8 10.9 %collective-permute-start.12 = (bf16[128,1024]{1,0:T(8,128)(2,1)S(1)}, bf16[128,1024]{1,0:T(8,128)(2,1)S(1)}, u32[]{:S(2)}, u32[]{:S(2)}) collective-permute-start(bf16[128,1024]{1,0:T(8,128)(2,1)S(1)} %collective-permute-done.11.refs_2_), channel_id=1, source_target_pairs={{0,1},{1,0},{2,3},{3,2},{4,5},{5,4},{6,7},{7,6},{8,9},{9,8},{10,11... | collective-permute-start | bytes 786440 | tf_op jit(solution)/shard_map/ppermute | solution.py:220
  31.0 10.2 %collective-permute-start.15 = (bf16[64,1024]{1,0:T(8,128)(2,1)S(1)}, bf16[64,1024]{1,0:T(8,128)(2,1)S(1)}, u32[]{:S(2)}, u32[]{:S(2)}) collective-permute-start(bf16[64,1024]{1,0:T(8,128)(2,1)S(1)} %slice.123), channel_id=1, source_target_pairs={{0,16},{1,17},{2,18},{3,19},{4,20},{5,21},{6,22},{7,23},{8,24},{9,... | collective-permute-start | bytes 393224 | tf_op jit(solution)/shard_map/ppermute | solution.py:220
  32.6 10.1 %collective-permute-start.14 = (bf16[128,1152]{1,0:T(8,128)(2,1)S(1)}, bf16[128,1152]{1,0:T(8,128)(2,1)S(1)}, u32[]{:S(2)}, u32[]{:S(2)}) collective-permute-start(bf16[128,1152]{1,0:T(8,128)(2,1)S(1)} %collective-permute-done.13.refs_4_), channel_id=1, source_target_pairs={{0,1},{1,0},{2,3},{3,2},{4,5},{5,4},{6,7},{7,6},{8,9},{9,8},{10,11... | collective-permute-start | bytes 884744 | tf_op jit(solution)/shard_map/ppermute | solution.py:220
  40.6 7.9 %collective-permute-start.28 = (bf16[128,1024]{1,0:T(8,128)(2,1)S(1)}, bf16[128,1024]{1,0:T(8,128)(2,1)S(1)}, u32[]{:S(2)}, u32[]{:S(2)}) collective-permute-start(bf16[128,1024]{1,0:T(8,128)(2,1)S(1)} %get-tuple-element.28), channel_id=1, source_target_pairs={{0,1},{1,0},{2,3},{3,2},{4,5},{5,4},{6,7},{7,6},{8,9},{9,8},{10,11... | collective-permute-start | bytes 786440 | tf_op jit(solution)/shard_map/ppermute | solution.py:220
  41.7 18.1 %collective-permute-start.27 = (bf16[3,128,1024]{2,1,0:T(8,128)(2,1)S(1)}, bf16[3,128,1024]{2,1,0:T(8,128)(2,1)S(1)}, u32[]{:S(2)}, u32[]{:S(2)}) collective-permute-start(bf16[3,128,1024]{2,1,0:T(8,128)(2,1)S(1)} %get-tuple-element.26), channel_id=1, source_target_pairs={{0,1},{1,0},{2,3},{3,2},{4,5},{5,4},{6,7},{7,6},{8,9},{9,8},{10,11... | collective-permute-start | bytes 2359304 | tf_op jit(solution)/shard_map/ppermute | solution.py:220
  48.6 11.5 %collective-permute-start.29 = (bf16[64,1024]{1,0:T(8,128)(2,1)S(1)}, bf16[64,1024]{1,0:T(8,128)(2,1)S(1)}, u32[]{:S(2)}, u32[]{:S(2)}) collective-permute-start(bf16[64,1024]{1,0:T(8,128)(2,1)S(1)} %get-tuple-element.43), channel_id=1, source_target_pairs={{0,16},{1,17},{2,18},{3,19},{4,20},{5,21},{6,22},{7,23},{8,24},{9,... | collective-permute-start | bytes 393224 | tf_op jit(solution)/shard_map/ppermute | solution.py:220
  49.2 10.9 %collective-permute-start.31 = (bf16[64,1024]{1,0:T(8,128)(2,1)S(1)}, bf16[64,1024]{1,0:T(8,128)(2,1)S(1)}, u32[]{:S(2)}, u32[]{:S(2)}) collective-permute-start(bf16[64,1024]{1,0:T(8,128)(2,1)S(1)} %get-tuple-element.44), channel_id=1, source_target_pairs={{0,2},{1,3},{2,0},{3,1},{4,6},{5,7},{6,4},{7,5},{8,10},{9,11},{10,... | collective-permute-start | bytes 393224 | tf_op jit(solution)/shard_map/ppermute | solution.py:220
  50.0 7.5 %collective-permute-start.23 = (bf16[64,1024]{1,0:T(8,128)(2,1)S(1)}, bf16[64,1024]{1,0:T(8,128)(2,1)S(1)}, u32[]{:S(2)}, u32[]{:S(2)}) collective-permute-start(bf16[64,1024]{1,0:T(8,128)(2,1)S(1)} %get-tuple-element.41), channel_id=1, source_target_pairs={{0,2},{1,3},{2,0},{3,1},{4,6},{5,7},{6,4},{7,5},{8,10},{9,11},{10,... | collective-permute-start | bytes 393224 | tf_op jit(solution)/shard_map/ppermute | solution.py:220
  57.6 7.6 %collective-permute-start.22 = (bf16[128,1024]{1,0:T(8,128)(2,1)S(1)}, bf16[128,1024]{1,0:T(8,128)(2,1)S(1)}, u32[]{:S(2)}, u32[]{:S(2)}) collective-permute-start(bf16[128,1024]{1,0:T(8,128)(2,1)S(1)} %pad_maximum_fusion.1), channel_id=1, source_target_pairs={{0,2},{1,3},{2,0},{3,1},{4,6},{5,7},{6,4},{7,5},{8,10},{9,11},{10,... | collective-permute-start | bytes 786440 | tf_op jit(solution)/shard_map/ppermute | solution.py:220
  58.3 8.2 %collective-permute-start.24 = (bf16[128,1024]{1,0:T(8,128)(2,1)S(1)}, bf16[128,1024]{1,0:T(8,128)(2,1)S(1)}, u32[]{:S(2)}, u32[]{:S(2)}) collective-permute-start(bf16[128,1024]{1,0:T(8,128)(2,1)S(1)} %pad_maximum_fusion.2), channel_id=1, source_target_pairs={{0,16},{1,17},{2,18},{3,19},{4,20},{5,21},{6,22},{7,23},{8,24},{9,... | collective-permute-start | bytes 786440 | tf_op jit(solution)/shard_map/ppermute | solution.py:220
  65.2 7.9 %collective-permute-start.32 = (bf16[128,1024]{1,0:T(8,128)(2,1)S(1)}, bf16[128,1024]{1,0:T(8,128)(2,1)S(1)}, u32[]{:S(2)}, u32[]{:S(2)}) collective-permute-start(bf16[128,1024]{1,0:T(8,128)(2,1)S(1)} %pad_maximum_fusion.4), channel_id=1, source_target_pairs={{0,16},{1,17},{2,18},{3,19},{4,20},{5,21},{6,22},{7,23},{8,24},{9,... | collective-permute-start | bytes 786440 | tf_op jit(solution)/shard_map/ppermute | solution.py:220
  67.4 12.4 %collective-permute-start.26 = (bf16[64,1024]{1,0:T(8,128)(2,1)S(1)}, bf16[64,1024]{1,0:T(8,128)(2,1)S(1)}, u32[]{:S(2)}, u32[]{:S(2)}) collective-permute-start(bf16[64,1024]{1,0:T(8,128)(2,1)S(1)} %get-tuple-element.40), channel_id=1, source_target_pairs={{0,8},{1,9},{2,10},{3,11},{4,12},{5,13},{6,14},{7,15},{8,0},{9,1},... | collective-permute-start | bytes 393224 | tf_op jit(solution)/shard_map/ppermute | solution.py:220
  70.6 9.3 %collective-permute-start.25 = (bf16[64,1024]{1,0:T(8,128)(2,1)S(1)}, bf16[64,1024]{1,0:T(8,128)(2,1)S(1)}, u32[]{:S(2)}, u32[]{:S(2)}) collective-permute-start(bf16[64,1024]{1,0:T(8,128)(2,1)S(1)} %get-tuple-element.39), channel_id=1, source_target_pairs={{0,12},{1,13},{2,14},{3,15},{4,8},{5,9},{6,10},{7,11},{8,4},{9,5},... | collective-permute-start | bytes 393224 | tf_op jit(solution)/shard_map/ppermute | solution.py:220
  (10 other events, 42.4 us)
